TPU v7x, 32 devices: a whole 2x2x4 slice. The times are simulated.
32 devices in a mesh: dp: 2 (over y), ctx: 4 (over x, core), tensor: 4 (over z).
Axes of the slice: x: 2, y: 2, z: 4, core: 2. Of those that a mesh axis runs over, the one named last changes fastest.
Arguments:
- hidden: bfloat16 [2, 1920, 2048], P('dp', 'ctx'), may hold values from -6 to 6
- cotangent: bfloat16 [2, 1920, 2048], P('dp', 'ctx'), may hold values from -6 to 6
- gain_attn: bfloat16 [2048], P(('dp', 'ctx')), may hold values from 0.5 to 1.5
- query_weight: bfloat16 [2048, 4096], P(('dp', 'ctx'), 'tensor'), may hold values from -0.125 to 0.125
- key_weight: bfloat16 [2048, 512], P(('dp', 'ctx'), 'tensor'), may hold values from -0.125 to 0.125
- value_weight: bfloat16 [2048, 512], P(('dp', 'ctx'), 'tensor'), may hold values from -0.125 to 0.125
- gain_query: bfloat16 [128], P(('dp', 'ctx')), may hold values from 0.25 to 1.75
- gain_key: bfloat16 [128], P(('dp', 'ctx')), may hold values from 0.25 to 1.75
- out_weight: bfloat16 [4096, 2048], P('tensor', ('dp', 'ctx')), may hold values from -0.75 to 0.75
- gain_moe: bfloat16 [2048], P(('dp', 'ctx')), may hold values from 0.5 to 1.5
- router_weight: bfloat16 [2048, 16], P(('dp', 'ctx')), may hold values from -0.0625 to 0.0625
- gate_weight: bfloat16 [16, 2048, 768], P(None, ('dp', 'ctx'), 'tensor'), may hold values from -0.125 to 0.125
- up_weight: bfloat16 [16, 2048, 768], P(None, ('dp', 'ctx'), 'tensor'), may hold values from -0.125 to 0.125
- down_weight: bfloat16 [16, 768, 2048], P(None, 'tensor', ('dp', 'ctx')), may hold values from -0.875 to 0.875
- segment: int32 [2, 1920], P('dp'), may hold values from 0 to 12, as said below
- parent: int32 [2, 13], P('dp'), may hold values from 0 to 12, as said below
- tree_depth: int32 [2, 1920], P('dp', 'ctx'), may hold values from 0 to 1119, as said below
- routes: int32 [2, 1920, 8], P('dp', 'ctx'), may hold values from 0 to 15, all different within a row; in each aligned block of 480 rows (0 to 479, 480 to 959, ..., all dimensions but the last counted through in order) at most 320 rows name the same one
Outputs:
- output: bfloat16 [2, 1920, 2048], P('dp', 'ctx')
- grad_hidden: bfloat16 [2, 1920, 2048], P('dp', 'ctx')
- grad_gain_attn: float32 [2048], P(('dp', 'ctx'))
- grad_query_weight: float32 [2048, 4096], P(('dp', 'ctx'), 'tensor')
- grad_key_weight: float32 [2048, 512], P(('dp', 'ctx'), 'tensor')
- grad_value_weight: float32 [2048, 512], P(('dp', 'ctx'), 'tensor')
- grad_gain_query: float32 [128], P(('dp', 'ctx'))
- grad_gain_key: float32 [128], P(('dp', 'ctx'))
- grad_out_weight: float32 [4096, 2048], P('tensor', ('dp', 'ctx'))
- grad_gain_moe: float32 [2048], P(('dp', 'ctx'))
- grad_router_weight: float32 [2048, 16], P(('dp', 'ctx'))
- grad_gate_weight: float32 [16, 2048, 768], P(None, ('dp', 'ctx'), 'tensor')
- grad_up_weight: float32 [16, 2048, 768], P(None, ('dp', 'ctx'), 'tensor')
- grad_down_weight: float32 [16, 768, 2048], P(None, 'tensor', ('dp', 'ctx'))
Inputs may be any that keep to these rules, and one draw needn't show every extreme that they name: Within a tree, tokens of one segment stand together: the trunk first, then each branch followed by its two leaves; a segment's ancestors stand before it. The trunk is its own parent; the four branches have the trunk as parent, and each branch is the parent of two leaves. `tree_depth`: A token's place on the path from its tree's first token: trunk tokens count from 0, a branch continues after the 896 trunk tokens, a leaf after its branch's 128. `routes`: 8 different experts a token; among the 480 tokens of one device's part of a tree, no expert is named by more than 320 rows; in some of these parts of every draw an expert is named exactly 320 times.
All inputs are finite; a program needn't handle non-finite values.
Results may differ from a plain program's by a relative error of at most 0.03.
Values may be sent and summed in bfloat16 or wider, within the bound.
No kernel may reach another device: no remote copies, remote signals or barrier semaphores. Data moves between devices by JAX's collectives and lax.ppermute only.
A program may use at most 448 MiB of HBM per device.

v0:
```python
from functools import partial
import math

import jax
import jax.numpy as jnp
from jax import lax
from jax.sharding import PartitionSpec as P

HEADS_Q = 32
HEADS_KV = 4
HEAD = 128
TOP = 8
EXPERTS = 16


EPS = 1e-06
THETA = 1000000.0
MASKED = -1e30


def rms_scale(field, gain_vec):
    return field * lax.rsqrt(jnp.mean(field * field, axis=-1, keepdims=True) + EPS) * gain_vec


def angle_tables(positions):
    half_size = HEAD // 2
    frequency = jnp.exp(jnp.arange(half_size, dtype=jnp.float32) * (-2.0 * math.log(THETA) / HEAD))
    angles = positions.astype(jnp.float32)[..., None] * frequency
    angles = jnp.concatenate([angles, angles], -1)
    return (jnp.cos(angles), jnp.sin(angles))


def rotate(field, cosine_table, sine_table):
    half_size = field.shape[-1] // 2
    turned = jnp.concatenate([-field[..., half_size:], field[..., :half_size]], -1)
    return field * cosine_table + turned * sine_table


def shape_heads(cosine_table, sine_table, query_heads, key_heads, gain_q, gain_k):
    return (
        rotate(rms_scale(query_heads, gain_q), cosine_table, sine_table),
        rotate(rms_scale(key_heads, gain_k), cosine_table, sine_table),
    )


def swiglu(gate_pre, up_pre):
    return jax.nn.silu(gate_pre) * up_pre


def lookup_parent(segment_ids, parent):
    seg_table = jnp.arange(parent.shape[-1], dtype=jnp.int32)
    return jnp.sum(jnp.where(segment_ids[..., None] == seg_table, parent[:, None, :], 0), -1)


def shards(
    hidden,
    cotangent,
    gain_attn,
    query_weight,
    key_weight,
    value_weight,
    gain_query,
    gain_key,
    out_weight,
    gain_moe,
    router_weight,
    gate_weight,
    up_weight,
    down_weight,
    segment,
    parent,
    tree_depth,
    routes,
):
    tree_count, local_rows, model_width = hidden.shape
    row_count = tree_count * local_rows
    heads_local = HEADS_Q // lax.axis_size("tensor")
    kv_local = HEADS_KV // lax.axis_size("tensor")
    group_size = HEADS_Q // HEADS_KV
    score_scale = HEAD ** (-0.5)
    ctx_start = lax.axis_index("ctx") * local_rows
    f32 = jnp.float32
    bf16 = jnp.bfloat16
    gathered = (
        lax.all_gather(gain_attn, ("dp", "ctx"), axis=0, tiled=True),
        lax.all_gather(query_weight, ("dp", "ctx"), axis=0, tiled=True),
        lax.all_gather(key_weight, ("dp", "ctx"), axis=0, tiled=True),
        lax.all_gather(value_weight, ("dp", "ctx"), axis=0, tiled=True),
        lax.all_gather(gain_query, ("dp", "ctx"), axis=0, tiled=True),
        lax.all_gather(gain_key, ("dp", "ctx"), axis=0, tiled=True),
        lax.all_gather(out_weight, ("dp", "ctx"), axis=1, tiled=True),
        lax.all_gather(gain_moe, ("dp", "ctx"), axis=0, tiled=True),
        lax.all_gather(router_weight, ("dp", "ctx"), axis=0, tiled=True),
    )
    gain_one, query_all, key_all, value_all, gain_q, gain_k, out_all, gain_two, router_all = (
        gathered
    )
    gate_all, up_all, down_all = (
        lax.all_gather(gate_weight, ("dp", "ctx"), axis=1, tiled=True),
        lax.all_gather(up_weight, ("dp", "ctx"), axis=1, tiled=True),
        lax.all_gather(down_weight, ("dp", "ctx"), axis=2, tiled=True),
    )
    tokens_in = hidden.astype(f32).reshape(row_count, model_width)
    normed, pull_first = jax.vjp(rms_scale, tokens_in, gain_one.astype(f32))
    normed_low = normed.astype(bf16)
    query_proj = jnp.dot(normed_low, query_all, preferred_element_type=f32)
    key_proj = jnp.dot(normed_low, key_all, preferred_element_type=f32)
    value_low = jnp.dot(normed_low, value_all, preferred_element_type=f32).astype(bf16)
    query_four = query_proj.reshape(tree_count, local_rows, heads_local, HEAD).transpose(0, 2, 1, 3)
    key_four = key_proj.reshape(tree_count, local_rows, kv_local, HEAD).transpose(0, 2, 1, 3)
    value_four = value_low.reshape(tree_count, local_rows, kv_local, HEAD).transpose(0, 2, 1, 3)
    cosine_table, sine_table = angle_tables(tree_depth)
    (query_rot, key_rot), pull_heads = jax.vjp(
        partial(shape_heads, cosine_table[:, None], sine_table[:, None]),
        query_four,
        key_four,
        gain_q.astype(f32),
        gain_k.astype(f32),
    )
    query_low = query_rot.astype(bf16).reshape(tree_count, kv_local, group_size, local_rows, HEAD)
    key_low = key_rot.astype(bf16)
    keys_whole, values_whole = (
        lax.all_gather(key_low, "ctx", axis=2, tiled=True),
        lax.all_gather(value_four, "ctx", axis=2, tiled=True),
    )
    own_segment = lax.dynamic_slice_in_dim(segment, ctx_start, local_rows, 1)
    first_up = lookup_parent(own_segment, parent)
    second_up = lookup_parent(first_up, parent)
    query_pos = ctx_start + jnp.arange(local_rows, dtype=jnp.int32)
    key_pos = jnp.arange(segment.shape[1], dtype=jnp.int32)
    related = (
        (segment[:, None, :] == own_segment[..., None])
        | (segment[:, None, :] == first_up[..., None])
        | (segment[:, None, :] == second_up[..., None])
    )
    visible = (key_pos[None, None, :] <= query_pos[None, :, None]) & related

    def forward_tree(pieces):
        query_tree, key_tree, value_tree, seen = pieces
        raw_score = jnp.einsum("hgqd,hkd->hgqk", query_tree, key_tree, preferred_element_type=f32)
        scores = jnp.where(seen[None, None], raw_score * score_scale, MASKED)
        row_max = jnp.max(scores, -1, keepdims=True)
        weight = jnp.exp(scores - row_max)
        row_sum = jnp.sum(weight, -1, keepdims=True)
        prob_low = (weight / row_sum).astype(bf16)
        mixed_tree = jnp.einsum("hgqk,hkd->hgqd", prob_low, value_tree, preferred_element_type=f32)
        return (mixed_tree, row_max, row_sum)

    mixed, row_maxes, row_sums = lax.map(
        forward_tree, (query_low, keys_whole, values_whole, visible)
    )
    attn_low = mixed.transpose(0, 3, 1, 2, 4).reshape(row_count, heads_local * HEAD).astype(bf16)
    attn_add = lax.psum(
        jnp.dot(attn_low, out_all, preferred_element_type=f32).astype(jnp.bfloat16), "tensor"
    ).astype(jnp.float32)
    resid = tokens_in + attn_add
    moe_in, pull_second = jax.vjp(rms_scale, resid, gain_two.astype(f32))
    moe_low = moe_in.astype(bf16)
    logits = jnp.dot(moe_low, router_all, preferred_element_type=f32)
    flat_routes = routes.reshape(row_count, TOP)
    chosen_mask = flat_routes[..., None] == jnp.arange(EXPERTS, dtype=jnp.int32)
    chosen = jnp.sum(jnp.where(chosen_mask, logits[:, None, :], 0.0), -1)
    gates = jax.nn.softmax(chosen, -1)
    capacity = local_rows * TOP // EXPERTS * 4 // 3
    onehot = chosen_mask.reshape(tree_count, local_rows * TOP, EXPERTS).astype(jnp.int32)
    before = jnp.cumsum(onehot, 1) - onehot
    slot_index = (
        jnp.sum(before * onehot, -1) + jnp.arange(tree_count, dtype=jnp.int32)[:, None] * capacity
    ).reshape(-1)
    expert_ids = flat_routes.reshape(-1)
    token_ids = jnp.arange(row_count * TOP, dtype=jnp.int32) // TOP
    dispatched = (
        jnp.zeros((EXPERTS, tree_count * capacity, model_width), bf16)
        .at[expert_ids, slot_index]
        .set(moe_low[token_ids])
    )
    gate_pre = jnp.einsum("ecd,edf->ecf", dispatched, gate_all, preferred_element_type=f32)
    up_pre = jnp.einsum("ecd,edf->ecf", dispatched, up_all, preferred_element_type=f32)
    activated, pull_act = jax.vjp(swiglu, gate_pre, up_pre)
    act_low = activated.astype(bf16)
    expert_out = jnp.einsum("ecf,efd->ecd", act_low, down_all, preferred_element_type=f32)
    picked = expert_out[expert_ids, slot_index].reshape(row_count, TOP, model_width)
    moe_add = lax.psum(jnp.sum(gates[..., None] * picked, 1).astype(jnp.bfloat16), "tensor").astype(
        jnp.float32
    )
    output = (resid + moe_add).astype(bf16).reshape(tree_count, local_rows, model_width)
    grad_out = cotangent.astype(f32).reshape(row_count, model_width)
    back_rows = (
        (gates[..., None] * grad_out[:, None, :]).astype(bf16).reshape(row_count * TOP, model_width)
    )
    back_buffer = jnp.zeros_like(dispatched).at[expert_ids, slot_index].set(back_rows)
    gate_part = jnp.sum(picked * grad_out[:, None, :], -1)
    gate_all, up_all, down_all = (
        lax.all_gather(gate_weight, ("dp", "ctx"), axis=1, tiled=True),
        lax.all_gather(up_weight, ("dp", "ctx"), axis=1, tiled=True),
        lax.all_gather(down_weight, ("dp", "ctx"), axis=2, tiled=True),
    )
    grad_act = jnp.einsum("ecd,efd->ecf", back_buffer, down_all, preferred_element_type=f32)
    grad_down = jnp.einsum("ecf,ecd->efd", act_low, back_buffer, preferred_element_type=f32)
    grad_gate_pre, grad_up_pre = pull_act(grad_act)
    gate_back = grad_gate_pre.astype(bf16)
    up_back = grad_up_pre.astype(bf16)
    grad_gate = jnp.einsum("ecd,ecf->edf", dispatched, gate_back, preferred_element_type=f32)
    grad_up = jnp.einsum("ecd,ecf->edf", dispatched, up_back, preferred_element_type=f32)
    grad_buffer = jnp.einsum(
        "ecf,edf->ecd", gate_back, gate_all, preferred_element_type=f32
    ) + jnp.einsum("ecf,edf->ecd", up_back, up_all, preferred_element_type=f32)
    moe_part = jnp.sum(grad_buffer[expert_ids, slot_index].reshape(row_count, TOP, model_width), 1)
    grad_moe_in, grad_gates = (
        lax.psum(moe_part.astype(jnp.bfloat16), "tensor").astype(jnp.float32),
        lax.psum(gate_part.astype(jnp.bfloat16), "tensor").astype(jnp.float32),
    )
    grad_chosen = gates * (grad_gates - jnp.sum(gates * grad_gates, -1, keepdims=True))
    grad_logits = jnp.sum(jnp.where(chosen_mask, grad_chosen[..., None], 0.0), 1).astype(bf16)
    grad_router = jnp.einsum("td,te->de", moe_low, grad_logits, preferred_element_type=f32)
    grad_moe_in = grad_moe_in + jnp.einsum(
        "te,de->td", grad_logits, router_all, preferred_element_type=f32
    )
    grad_resid, grad_gain_two = pull_second(grad_moe_in)
    grad_resid = grad_resid + grad_out
    resid_low = grad_resid.astype(bf16)
    grad_out_proj = jnp.einsum("te,td->ed", attn_low, resid_low, preferred_element_type=f32)
    grad_mixed = jnp.einsum("td,ed->te", resid_low, out_all, preferred_element_type=f32).astype(
        bf16
    )
    grad_mixed = grad_mixed.reshape(tree_count, local_rows, kv_local, group_size, HEAD).transpose(
        0, 2, 3, 1, 4
    )

    def backward_tree(pieces):
        query_tree, key_tree, value_tree, seen, row_max, row_sum, grad_tree = pieces
        raw_score = jnp.einsum("hgqd,hkd->hgqk", query_tree, key_tree, preferred_element_type=f32)
        scores = jnp.where(seen[None, None], raw_score * score_scale, MASKED)
        probability = jnp.exp(scores - row_max) / row_sum
        prob_low = probability.astype(bf16)
        grad_prob = jnp.einsum("hgqd,hkd->hgqk", grad_tree, value_tree, preferred_element_type=f32)
        inner = jnp.sum(probability * grad_prob, -1, keepdims=True)
        grad_raw = (probability * (grad_prob - inner) * score_scale).astype(bf16)
        grad_query_tree = jnp.einsum(
            "hgqk,hkd->hgqd", grad_raw, key_tree, preferred_element_type=f32
        )
        grad_key_tree = jnp.einsum(
            "hgqk,hgqd->hkd", grad_raw, query_tree, preferred_element_type=f32
        )
        grad_value_tree = jnp.einsum(
            "hgqk,hgqd->hkd", prob_low, grad_tree, preferred_element_type=f32
        )
        return (grad_query_tree, grad_key_tree, grad_value_tree)

    grad_query_rot, grad_keys_whole, grad_values_whole = lax.map(
        backward_tree,
        (query_low, keys_whole, values_whole, visible, row_maxes, row_sums, grad_mixed),
    )
    grad_key_rot, grad_value_four = (
        lax.psum_scatter(
            grad_keys_whole.astype(jnp.bfloat16), "ctx", scatter_dimension=2, tiled=True
        ).astype(jnp.float32),
        lax.psum_scatter(
            grad_values_whole.astype(jnp.bfloat16), "ctx", scatter_dimension=2, tiled=True
        ).astype(jnp.float32),
    )
    grad_query_four, grad_key_four, grad_gain_q, grad_gain_k = pull_heads(
        (grad_query_rot.reshape(tree_count, heads_local, local_rows, HEAD), grad_key_rot)
    )
    query_back = (
        grad_query_four.transpose(0, 2, 1, 3).reshape(row_count, heads_local * HEAD).astype(bf16)
    )
    key_back = grad_key_four.transpose(0, 2, 1, 3).reshape(row_count, kv_local * HEAD).astype(bf16)
    value_back = (
        grad_value_four.transpose(0, 2, 1, 3).reshape(row_count, kv_local * HEAD).astype(bf16)
    )
    grad_query_proj = jnp.einsum("td,te->de", normed_low, query_back, preferred_element_type=f32)
    grad_key_proj = jnp.einsum("td,te->de", normed_low, key_back, preferred_element_type=f32)
    grad_value_proj = jnp.einsum("td,te->de", normed_low, value_back, preferred_element_type=f32)
    attn_part = (
        jnp.einsum("te,de->td", query_back, query_all, preferred_element_type=f32)
        + jnp.einsum("te,de->td", key_back, key_all, preferred_element_type=f32)
        + jnp.einsum("te,de->td", value_back, value_all, preferred_element_type=f32)
    )
    grad_normed, grad_gain_q, grad_gain_k = (
        lax.psum(attn_part.astype(jnp.bfloat16), "tensor").astype(jnp.float32),
        lax.psum(grad_gain_q.astype(jnp.bfloat16), "tensor").astype(jnp.float32),
        lax.psum(grad_gain_k.astype(jnp.bfloat16), "tensor").astype(jnp.float32),
    )
    grad_tokens, grad_gain_one = pull_first(grad_normed)
    grad_tokens = grad_tokens + grad_resid
    attn_grads = (
        lax.psum_scatter(
            grad_gain_one.astype(jnp.bfloat16), ("dp", "ctx"), scatter_dimension=0, tiled=True
        ).astype(jnp.float32),
        lax.psum_scatter(
            grad_query_proj.astype(jnp.bfloat16), ("dp", "ctx"), scatter_dimension=0, tiled=True
        ).astype(jnp.float32),
        lax.psum_scatter(
            grad_key_proj.astype(jnp.bfloat16), ("dp", "ctx"), scatter_dimension=0, tiled=True
        ).astype(jnp.float32),
        lax.psum_scatter(
            grad_value_proj.astype(jnp.bfloat16), ("dp", "ctx"), scatter_dimension=0, tiled=True
        ).astype(jnp.float32),
        lax.psum_scatter(
            grad_gain_q.astype(jnp.bfloat16), ("dp", "ctx"), scatter_dimension=0, tiled=True
        ).astype(jnp.float32),
        lax.psum_scatter(
            grad_gain_k.astype(jnp.bfloat16), ("dp", "ctx"), scatter_dimension=0, tiled=True
        ).astype(jnp.float32),
        lax.psum_scatter(
            grad_out_proj.astype(jnp.bfloat16), ("dp", "ctx"), scatter_dimension=1, tiled=True
        ).astype(jnp.float32),
        lax.psum_scatter(
            grad_gain_two.astype(jnp.bfloat16), ("dp", "ctx"), scatter_dimension=0, tiled=True
        ).astype(jnp.float32),
        lax.psum_scatter(
            grad_router.astype(jnp.bfloat16), ("dp", "ctx"), scatter_dimension=0, tiled=True
        ).astype(jnp.float32),
    )
    expert_grads = (
        lax.psum_scatter(
            grad_gate.astype(jnp.bfloat16), ("dp", "ctx"), scatter_dimension=1, tiled=True
        ).astype(jnp.float32),
        lax.psum_scatter(
            grad_up.astype(jnp.bfloat16), ("dp", "ctx"), scatter_dimension=1, tiled=True
        ).astype(jnp.float32),
        lax.psum_scatter(
            grad_down.astype(jnp.bfloat16), ("dp", "ctx"), scatter_dimension=2, tiled=True
        ).astype(jnp.float32),
    )
    grad_hidden = grad_tokens.astype(bf16).reshape(tree_count, local_rows, model_width)
    return (
        output,
        grad_hidden,
        attn_grads[0],
        attn_grads[1],
        attn_grads[2],
        attn_grads[3],
        attn_grads[4],
        attn_grads[5],
        attn_grads[6],
        attn_grads[7],
        attn_grads[8],
        expert_grads[0],
        expert_grads[1],
        expert_grads[2],
    )


def solution(mesh):
    in_specs = (
        P("dp", "ctx", None),
        P("dp", "ctx", None),
        P(("dp", "ctx")),
        P(("dp", "ctx"), "tensor"),
        P(("dp", "ctx"), "tensor"),
        P(("dp", "ctx"), "tensor"),
        P(("dp", "ctx")),
        P(("dp", "ctx")),
        P("tensor", ("dp", "ctx")),
        P(("dp", "ctx")),
        P(("dp", "ctx"), None),
        P(None, ("dp", "ctx"), "tensor"),
        P(None, ("dp", "ctx"), "tensor"),
        P(None, "tensor", ("dp", "ctx")),
        P("dp", None),
        P("dp", None),
        P("dp", "ctx"),
        P("dp", "ctx", None),
    )
    out_specs = (
        P("dp", "ctx", None),
        P("dp", "ctx", None),
        P(("dp", "ctx")),
        P(("dp", "ctx"), "tensor"),
        P(("dp", "ctx"), "tensor"),
        P(("dp", "ctx"), "tensor"),
        P(("dp", "ctx")),
        P(("dp", "ctx")),
        P("tensor", ("dp", "ctx")),
        P(("dp", "ctx")),
        P(("dp", "ctx"), None),
        P(None, ("dp", "ctx"), "tensor"),
        P(None, ("dp", "ctx"), "tensor"),
        P(None, "tensor", ("dp", "ctx")),
    )
    return jax.shard_map(shards, mesh=mesh, in_specs=in_specs, out_specs=out_specs, check_vma=False)
```

profile of v0, /device:TPU:0, one launch (start us, length us, event | category | flops | bytes accessed | tf_op | source)
XLA Modules:
  0.0 1512.0 jit_solution(15742611145567538519)
XLA Ops:
  12.5 15.3 %all-reduce.11 = (bf16[128]{0:T(256)(128)(2,1)S(1)}, bf16[128]{0:T(256)(128)(2,1)S(1)}) all-reduce(bf16[128]{0:T(256)(128)(2,1)S(1)} %dynamic-update-slice, bf16[128]{0:T(256)(128)(2,1)S(1)} %dynamic-update-slice.1), channel_id=1, replica_groups=mesh['dp'=2,'ctx'=4,'tensor'=4] {'dp','ctx'}, use_global_device_ids=true, to_apply=%add.4 | all-reduce | flops 256 | bytes 1024
  34.2 7.9 all-gather.2
  42.1 10.6 all_gather.48
  52.8 2.6 multiply_reduce_fusion.5
  57.8 9.6 all-gather
  67.4 9.2 all_gather.51
  77.4 4.4 fusion.48
  81.8 10.1 all-gather.1
  91.9 6.9 copy.60
  98.8 4.5 fusion.75
  106.7 18.3 %fusion.165 = (f32[8,480]{1,0:T(8,128)S(1)}, f32[8,480,1920]{2,1,0:T(8,128)}) fusion(pred[480,1920]{1,0:T(8,128)(4,1)} %fusion.48, bf16[8,480,128]{2,1,0:T(8,128)(2,1)} %fusion.90, bf16[1920,128]{1,0:T(8,128)(2,1)S(1)} %all-gather), kind=kOutput, calls=%fused_computation.239 | convolution fusion | flops 1916929920 | bytes 31902720 | tf_op jit(solution)/shard_map/while/body/eval_jaxpr/sub | solution.py:143
  125.6 11.8 fusion.87
  137.9 6.0 convolution_convert_fusion.5
  146.2 8.5 all-gather.3
  154.9 4.6 reduce-window.6
  160.5 8.4 all_gather.55
  170.0 3.9 bitcast_convert_fusion
  173.9 52.2 %all-reduce.18.cloned.1.call-done = bf16[480,2048]{1,0:T(8,128)(2,1)} async-done(((bf16[480,2048]{1,0:T(8,128)(2,1)}), bf16[480,2048]{1,0:T(8,128)(2,1)}) %all-reduce.18.cloned.1.call-update) | async-done | bytes 1966096 | tf_op jit(solution)/shard_map/psum | solution.py:153
  226.1 2.4 multiply_reduce_fusion.3
  232.4 15.7 %gather_fusion = bf16[3840,2048]{1,0:T(8,128)(2,1)} fusion(bf16[480,2048]{1,0:T(8,128)(2,1)S(1)} %multiply_convert_fusion.3, s32[4096]{0:T(1024)S(1)} %pad_clamp_fusion), kind=kCustom, calls=%fused_computation | custom fusion | bytes 31472640 | tf_op jit(solution)/shard_map/gather | solution.py:175
  248.2 10.0 fusion.2
  258.1 38.1 %scatter_custom_fusion.1 = bf16[5120,2048]{1,0:T(8,128)(2,1)} fusion(s32[3840]{0:T(1024)S(1)} %broadcast_select_fusion, bf16[3840,2048]{1,0:T(8,128)(2,1)} %fusion.2, bf16[]{:T(256)} %constant.113.clone.1), kind=kCustom, calls=%fused_computation.29 | custom fusion | bytes 20972032
  296.2 44.6 %scatter_custom_fusion = bf16[5120,2048]{1,0:T(8,128)(2,1)} fusion(s32[3840]{0:T(1024)S(1)} %broadcast_select_fusion, bf16[3840,2048]{1,0:T(8,128)(2,1)} %gather_fusion, bf16[]{:T(256)} %constant.113.clone.1), kind=kCustom, calls=%fused_computation.31 | custom fusion | bytes 20972032
  340.8 17.4 %fusion.172 = f32[16,320,192]{1,2,0:T(8,128)} fusion(bf16[16,320,2048]{2,1,0:T(8,128)(2,1)} %bitcast.268, bf16[16,2048,192]{1,2,0:T(8,128)(2,1)} %all-gather.16.cloned.1.call-done), kind=kOutput, calls=%fused_computation.242 | convolution fusion | flops 4026531840 | bytes 37486592 | tf_op jit(solution)/shard_map/ecd,edf->ecf/dot_general | solution.py:178
  358.2 19.5 %all-gather.14.cloned.1.call-done = bf16[16,2048,192]{1,2,0:T(8,128)(2,1)} async-done(((bf16[16,256,192]{1,2,0:T(8,128)(2,1)}), bf16[16,2048,192]{1,2,0:T(8,128)(2,1)}) %all-gather.14.cloned.1.call-update) | async-done | bytes 12582928 | tf_op jit(solution)/shard_map/all_gather | solution.py:99
  377.7 18.0 %fusion.171 = f32[16,320,192]{1,2,0:T(8,128)} fusion(bf16[16,320,2048]{2,1,0:T(8,128)(2,1)} %bitcast.269, bf16[16,2048,192]{1,2,0:T(8,128)(2,1)} %all-gather.14.cloned.1.call-done), kind=kOutput, calls=%fused_computation.241 | convolution fusion | flops 4026531840 | bytes 37486592 | tf_op jit(solution)/shard_map/ecd,edf->ecf/dot_general | solution.py:177
  395.7 58.3 %all-gather.18.cloned.1.call-done = bf16[16,192,2048]{2,1,0:T(8,128)(2,1)} async-done(((bf16[16,192,256]{2,1,0:T(8,128)(2,1)}), bf16[16,192,2048]{2,1,0:T(8,128)(2,1)}) %all-gather.18.cloned.1.call-update) | async-done | bytes 12582928 | tf_op jit(solution)/shard_map/all_gather | solution.py:101
  454.0 23.6 %multiply_convert_fusion.1 = (bf16[16,320,192]{1,2,0:T(8,128)(2,1)}, bf16[16,320,192]{1,2,0:T(8,128)(2,1)S(1)}, bf16[16,320,192]{1,2,0:T(8,128)(2,1)}) fusion(f32[16,320,192]{1,2,0:T(8,128)} %fusion.171, f32[16,320,192]{1,2,0:T(8,128)} %fusion.172, bf16[16,320,2048]{2,1,0:T(8,128)(2,1)} %bitcast.272, bf16[16,192,2048]{2,1,0:T(8,128)(2,1)} %all-gather.18.cloned.1.call-done), kind=kOutput, calls=%fused_computation.55 | convolution fusion | flops 4042260480 | bytes 47316992 | tf_op jit(solution)/shard_map/ecd,efd->ecf/dot_general | solution.py:198
  477.6 19.8 %fusion.174 = f32[16,320,2048]{2,1,0:T(8,128)} fusion(bf16[16,320,192]{1,2,0:T(8,128)(2,1)S(1)} %get-tuple-element.96, bf16[16,2048,192]{1,2,0:T(8,128)(2,1)} %all-gather.14.cloned.1.call-done), kind=kOutput, calls=%fused_computation.244 | convolution fusion | flops 4026531840 | bytes 56492032 | tf_op jit(solution)/shard_map/ecf,edf->ecd/dot_general | solution.py:205
  497.4 33.7 %convolution_add_fusion = f32[16,320,2048]{2,1,0:T(8,128)} fusion(f32[16,320,2048]{2,1,0:T(8,128)} %fusion.174, bf16[16,320,192]{1,2,0:T(8,128)(2,1)} %get-tuple-element.95, bf16[16,2048,192]{1,2,0:T(8,128)(2,1)} %all-gather.16.cloned.1.call-done), kind=kOutput, calls=%fused_computation.22 | convolution fusion | flops 4037017600 | bytes 98435072 | tf_op jit(solution)/shard_map/ecf,edf->ecd/dot_general | solution.py:207
  531.1 71.8 %gather_fusion.2 = f32[3840,2048]{1,0:T(8,128)} fusion(f32[16,320,2048]{2,1,0:T(8,128)} %convolution_add_fusion, s32[3840]{0:T(1024)S(1)} %copy-done.2), kind=kCustom, calls=%fused_computation.2 | custom fusion | bytes 62945280 | tf_op jit(solution)/shard_map/gather | solution.py:208
  602.9 16.0 %bitcast_reduce_fusion = bf16[480,2048]{1,0:T(8,128)(2,1)} fusion(f32[3840,2048]{1,0:T(8,128)} %gather_fusion.2), kind=kLoop, calls=%fused_computation.7 | loop fusion | flops 6881280 | bytes 33423360 | tf_op jit(solution)/shard_map/reduce_sum | solution.py:208
  619.0 19.6 %fusion.173 = f32[16,320,2048]{2,1,0:T(8,128)} fusion(bf16[16,320,192]{1,2,0:T(8,128)(2,1)S(1)} %copy-done.13, bf16[16,192,2048]{2,1,0:T(8,128)(2,1)} %all-gather.18.cloned.1.call-done), kind=kOutput, calls=%fused_computation.243 | convolution fusion | flops 4026531840 | bytes 56492032 | tf_op jit(solution)/shard_map/ecf,efd->ecd/dot_general | solution.py:181
  638.5 72.1 %gather_fusion.1 = f32[3840,2048]{1,0:T(8,128)} fusion(f32[16,320,2048]{2,1,0:T(8,128)} %fusion.173, s32[3840]{0:T(1024)S(1)} %copy-done.2), kind=kCustom, calls=%fused_computation.1 | custom fusion | bytes 62945280 | tf_op jit(solution)/shard_map/gather | solution.py:182
  710.7 15.8 %fusion.4 = (bf16[480,8]{1,0:T(8,128)(2,1)S(1)}, bf16[480,2048]{1,0:T(8,128)(2,1)}) fusion(f32[3840,2048]{1,0:T(8,128)} %gather_fusion.1, f32[480,2048]{1,0:T(8,128)} %bitcast_convert_fusion, f32[480,8]{1,0:T(8,128)S(1)} %copy-done.20), kind=kLoop, calls=%fused_computation.13 | loop fusion | flops 30470400 | bytes 37378560 | tf_op jit(solution)/shard_map/reduce_sum | solution.py:192
  726.6 11.9 psum.52
  738.8 4.5 multiply_reduce_fusion.1
  745.5 2.2 fusion.86
  748.1 11.7 fusion.98
  759.7 42.2 %fusion.63 = bf16[1,1,1920,128]{3,2,1,0:T(8,128)(2,1)} fusion(bf16[8,480,128]{2,1,0:T(8,128)(2,1)S(1)} %copy-done.36, f32[8,480,1920]{2,1,0:T(8,128)} %fusion.98, f32[8,480,1920]{2,1,0:T(8,128)} %get-tuple-element.121, f32[8,480]{1,0:T(8,128)S(1)} %copy-done.84), kind=kOutput, calls=%fused_computation.90 | convolution fusion | flops 1939297920 | bytes 60472320 | tf_op jit(solution)/shard_map/while/body/eval_jaxpr/hgqk,hgqd->hkd/dot_general | solution.py:242
  802.3 13.0 fusion.66
  816.5 39.0 %fusion.13 = f32[8,480,128]{2,1,0:T(8,128)S(1)} fusion(f32[8,480,1920]{2,1,0:T(8,128)} %fusion.98, bf16[1920,128]{1,0:T(8,128)(2,1)S(1)} %copy-done.40, f32[8,480,1920]{2,1,0:T(8,128)} %get-tuple-element.121, f32[8,480]{1,0:T(8,128)S(1)} %copy-done.84), kind=kOutput, calls=%fused_computation.21 | convolution fusion | flops 1939052160 | bytes 61455360 | tf_op jit(solution)/shard_map/while/body/eval_jaxpr/hgqk,hkd->hgqd/dot_general | solution.py:239
  861.8 4.1 fusion.93
  868.7 2.6 convolution_convert_fusion.6
  871.3 2.9 fusion.129
  881.6 6.4 convolution_convert_fusion.3
  889.2 4.4 convolution_convert_fusion.4
  893.8 14.3 convolution_convert_fusion.2
  908.3 14.4 convolution_convert_fusion
  922.8 15.1 convolution_convert_fusion.1
  942.0 125.2 %all-reduce.22.cloned.1.call-done = (bf16[480,2048]{1,0:T(8,128)(2,1)}, bf16[480,2048]{1,0:T(8,128)(2,1)}) async-done(((bf16[480,2048]{1,0:T(8,128)(2,1)}, bf16[480,2048]{1,0:T(8,128)(2,1)}), (bf16[480,2048]{1,0:T(8,128)(2,1)}, bf16[480,2048]{1,0:T(8,128)(2,1)})) %all-reduce.22.cloned.1.call-update) | async-done | bytes 3932176 | tf_op jit(solution)/shard_map/psum | solution.py:183
  1067.3 3.2 fusion.44
  1070.4 14.2 all-reduce.10
  1084.8 18.8 %reduce-scatter.17.cloned.1.call-done = bf16[256,128]{1,0:T(8,128)(2,1)} async-done(((bf16[2048,128]{1,0:T(8,128)(2,1)}), bf16[256,128]{1,0:T(8,128)(2,1)}) %reduce-scatter.17.cloned.1.call-update) | async-done | bytes 65552 | tf_op jit(solution)/shard_map/reduce_scatter | solution.py:294
  1105.1 11.7 all-reduce.12
  1118.4 6.8 fusion.71
  1125.2 33.3 %reduce-scatter.21.cloned.1.call-done = bf16[1024,256]{1,0:T(8,128)(2,1)} async-done(((bf16[1024,2048]{1,0:T(8,128)(2,1)}), bf16[1024,256]{1,0:T(8,128)(2,1)}) %reduce-scatter.21.cloned.1.call-update) | async-done | bytes 524304 | tf_op jit(solution)/shard_map/reduce_scatter | solution.py:306
  1160.6 52.4 %reduce-scatter.15.cloned.1.call-done = bf16[256,1024]{1,0:T(8,128)(2,1)} async-done(((bf16[2048,1024]{1,0:T(8,128)(2,1)}), bf16[256,1024]{1,0:T(8,128)(2,1)}) %reduce-scatter.15.cloned.1.call-update) | async-done | bytes 524304 | tf_op jit(solution)/shard_map/reduce_scatter | solution.py:291
  1215.1 94.1 %reduce-scatter.29.cloned.1.call-done = bf16[16,192,256]{2,1,0:T(8,128)(2,1)} async-done(((bf16[16,192,2048]{2,1,0:T(8,128)(2,1)}), bf16[16,192,256]{2,1,0:T(8,128)(2,1)}) %reduce-scatter.29.cloned.1.call-update) | async-done | bytes 1572880 | tf_op jit(solution)/shard_map/reduce_scatter | solution.py:323
  1309.2 3.4 convert_element_type.325
  1312.6 92.8 %reduce-scatter.27.cloned.1.call-done = bf16[16,256,192]{1,2,0:T(8,128)(2,1)} async-done(((bf16[16,2048,192]{1,2,0:T(8,128)(2,1)}), bf16[16,256,192]{1,2,0:T(8,128)(2,1)}) %reduce-scatter.27.cloned.1.call-update) | async-done | bytes 1572880 | tf_op jit(solution)/shard_map/reduce_scatter | solution.py:320
  1405.4 3.4 convert_element_type.323
  1408.8 92.8 %reduce-scatter.25.cloned.1.call-done = bf16[16,256,192]{1,2,0:T(8,128)(2,1)} async-done(((bf16[16,2048,192]{1,2,0:T(8,128)(2,1)}), bf16[16,256,192]{1,2,0:T(8,128)(2,1)}) %reduce-scatter.25.cloned.1.call-update) | async-done | bytes 1572880 | tf_op jit(solution)/shard_map/reduce_scatter | solution.py:317
  1501.6 3.4 convert_element_type.321
  (304 shorter events, 58.8 us)
Async XLA Ops:
  7.2 84.7 %all-gather.10.cloned.1.call-start = ((), (), s32[]{:S(2)}) async-start(), calls=%async_computation.10 | async-start | bytes 4718592 | tf_op jit(solution)/shard_map/all_gather | solution.py:86
  7.9 130.0 %all-gather.12.cloned.1.call-start = ((), (), s32[]{:S(2)}) async-start(), calls=%async_computation.11 | async-start | bytes 4718592 | tf_op jit(solution)/shard_map/all_gather | solution.py:91
  8.7 217.4 %all-reduce.18.cloned.1.call-start = ((), (), s32[]{:S(2)}) async-start(), calls=%async_computation.12 | async-start | bytes 3932160 | tf_op jit(solution)/shard_map/psum | solution.py:153
  27.8 76.9 %copy-start.76 = (f32[128]{0:T(128)}, f32[128]{0:T(128)S(1)}, u32[]{:S(2)}) copy-start(f32[128]{0:T(128)S(1)} %convert_element_type.255) | copy-start | bytes 1540
  27.8 28.8 %copy-start.74 = (f32[128]{0:T(128)}, f32[128]{0:T(128)S(1)}, u32[]{:S(2)}) copy-start(f32[128]{0:T(128)S(1)} %convert_element_type.259) | copy-start | bytes 1540
  32.0 66.8 %copy-start.65 = (f32[480]{0:T(512)}, f32[480]{0:T(512)S(1)}, u32[]{:S(2)}) copy-start(f32[480]{0:T(512)S(1)} %fusion.147) | copy-start | bytes 5764
  42.1 56.7 %copy-start.50 = (f32[8,1,256]{2,1,0:T(1,128)}, f32[8,1,256]{2,1,0:T(1,128)S(1)}, u32[]{:S(2)}) copy-start(f32[8,1,256]{2,1,0:T(1,128)S(1)} %convert_element_type.326) | copy-start | bytes 24580
  52.8 14.6 copy-start.54
  52.8 23.9 %copy-start.3 = (bf16[1,480,2048]{2,1,0:T(8,128)(2,1)S(1)}, bf16[1,480,2048]{2,1,0:T(8,128)(2,1)}, u32[]{:S(2)}) copy-start(bf16[1,480,2048]{2,1,0:T(8,128)(2,1)} %param.18) | copy-start | bytes 5898244
  55.4 22.0 %copy-start.17 = (f32[480,128]{1,0:T(8,128)}, f32[480,128]{1,0:T(8,128)S(1)}, u32[]{:S(2)}) copy-start(f32[480,128]{1,0:T(8,128)S(1)} %get-tuple-element.119) | copy-start | bytes 737284
  55.4 22.0 %copy-start.72 = (f32[480]{0:T(512)}, f32[480]{0:T(512)S(1)}, u32[]{:S(2)}) copy-start(f32[480]{0:T(512)S(1)} %get-tuple-element.118) | copy-start | bytes 5764
  55.4 22.0 %copy-start.57 = (f32[480]{0:T(512)}, f32[480]{0:T(512)S(1)}, u32[]{:S(2)}) copy-start(f32[480]{0:T(512)S(1)} %fusion.148) | copy-start | bytes 5764
  57.8 46.9 %copy-start.22 = (f32[480,128]{1,0:T(8,128)}, f32[480,128]{1,0:T(8,128)S(1)}, u32[]{:S(2)}) copy-start(f32[480,128]{1,0:T(8,128)S(1)} %get-tuple-element.107) | copy-start | bytes 737284
  57.8 46.9 %copy-start.24 = (f32[480,128]{1,0:T(8,128)}, f32[480,128]{1,0:T(8,128)S(1)}, u32[]{:S(2)}) copy-start(f32[480,128]{1,0:T(8,128)S(1)} %get-tuple-element.108) | copy-start | bytes 737284
  67.4 39.3 %copy-start.39 = (bf16[1920,128]{1,0:T(8,128)(2,1)}, bf16[1920,128]{1,0:T(8,128)(2,1)S(1)}, u32[]{:S(2)}) copy-start(bf16[1920,128]{1,0:T(8,128)(2,1)S(1)} %all-gather) | copy-start | bytes 1474564
  91.9 33.1 %copy-start.30 = (bf16[1920,128]{1,0:T(8,128)(2,1)}, bf16[1920,128]{1,0:T(8,128)(2,1)S(1)}, u32[]{:S(2)}) copy-start(bf16[1920,128]{1,0:T(8,128)(2,1)S(1)} %all-gather.1) | copy-start | bytes 1474564
  137.8 6.0 copy-start.32
  143.9 16.6 %copy-start.71 = (bf16[256,16]{0,1:T(8,128)(2,1)S(1)}, bf16[256,16]{0,1:T(8,128)(2,1)}, u32[]{:S(2)}) copy-start(bf16[256,16]{0,1:T(8,128)(2,1)} %param.28) | copy-start | bytes 24580
  143.9 196.9 %all-gather.16.cloned.1.call-start = ((), (), s32[]{:S(2)}) async-start(), calls=%async_computation.14 | async-start | bytes 14155776 | tf_op jit(solution)/shard_map/all_gather | solution.py:100
  144.5 25.2 %copy-start.80 = (s32[2]{0:T(128)S(1)}, s32[2]{0:T(128)}, u32[]{:S(2)}) copy-start(s32[2]{0:T(128)} %constant.136) | copy-start | bytes 28
  144.5 25.3 %copy-start.79 = (s32[2]{0:T(128)S(1)}, s32[2]{0:T(128)}, u32[]{:S(2)}) copy-start(s32[2]{0:T(128)} %constant.139) | copy-start | bytes 28
  144.5 233.2 %all-gather.14.cloned.1.call-start = ((), (), s32[]{:S(2)}) async-start(), calls=%async_computation.13 | async-start | bytes 14155776 | tf_op jit(solution)/shard_map/all_gather | solution.py:99
  145.1 308.9 %all-gather.18.cloned.1.call-start = ((), (), s32[]{:S(2)}) async-start(), calls=%async_computation.15 | async-start | bytes 14155776 | tf_op jit(solution)/shard_map/all_gather | solution.py:101
  145.7 593.0 %all-reduce.20.cloned.1.call-start = ((), (), s32[]{:S(2)}) async-start(), calls=%async_computation.16 | async-start | bytes 3932160 | tf_op jit(solution)/shard_map/psum | solution.py:210
  154.8 73.8 %copy-start.52 = (f32[8,1,256]{2,1,0:T(1,128)}, f32[8,1,256]{2,1,0:T(1,128)S(1)}, u32[]{:S(2)}) copy-start(f32[8,1,256]{2,1,0:T(1,128)S(1)} %convert_element_type.327) | copy-start | bytes 24580
  168.9 61.3 %copy-start.45 = (bf16[2048,16]{0,1:T(8,128)(2,1)}, bf16[2048,16]{0,1:T(8,128)(2,1)S(1)}, u32[]{:S(2)}) copy-start(bf16[2048,16]{0,1:T(8,128)(2,1)S(1)} %all_gather.55) | copy-start | bytes 196612
  230.2 18.0 %copy-start = (bf16[480,2048]{1,0:T(8,128)(2,1)}, bf16[480,2048]{1,0:T(8,128)(2,1)S(1)}, u32[]{:S(2)}) copy-start(bf16[480,2048]{1,0:T(8,128)(2,1)S(1)} %multiply_convert_fusion.3) | copy-start | bytes 5898244
  232.3 15.9 %copy-start.19 = (f32[480,8]{1,0:T(8,128)}, f32[480,8]{1,0:T(8,128)S(1)}, u32[]{:S(2)}) copy-start(f32[480,8]{1,0:T(8,128)S(1)} %copy.62) | copy-start | bytes 46084
  477.6 19.8 %copy-start.12 = (bf16[16,320,192]{1,2,0:T(8,128)(2,1)}, bf16[16,320,192]{1,2,0:T(8,128)(2,1)S(1)}, u32[]{:S(2)}) copy-start(bf16[16,320,192]{1,2,0:T(8,128)(2,1)S(1)} %get-tuple-element.96) | copy-start | bytes 5898244
  497.4 33.7 %copy-start.2 = (s32[3840]{0:T(1024)S(1)}, s32[3840]{0:T(1024)}, u32[]{:S(2)}) copy-start(s32[3840]{0:T(1024)} %get-tuple-element.93) | copy-start | bytes 46084
  602.9 16.1 %copy-start.13 = (bf16[16,320,192]{1,2,0:T(8,128)(2,1)S(1)}, bf16[16,320,192]{1,2,0:T(8,128)(2,1)}, u32[]{:S(2)}) copy-start(bf16[16,320,192]{1,2,0:T(8,128)(2,1)} %get-tuple-element.97) | copy-start | bytes 5898244
  618.9 247.0 %reduce-scatter.11.cloned.1.call-start = ((), (), s32[]{:S(2)}) async-start(), calls=%async_computation.17 | async-start | bytes 614400 | tf_op jit(solution)/shard_map/reduce_scatter | solution.py:255
  638.5 72.1 %copy-start.20 = (f32[480,8]{1,0:T(8,128)S(1)}, f32[480,8]{1,0:T(8,128)}, u32[]{:S(2)}) copy-start(f32[480,8]{1,0:T(8,128)} %copy-done.19) | copy-start | bytes 46084
  710.7 27.9 %copy-start.38 = (f32[480,8]{0,1:T(8,128)S(1)}, f32[480,8]{0,1:T(8,128)}, u32[]{:S(2)}) copy-start(f32[480,8]{0,1:T(8,128)} %copy-done.37) | copy-start | bytes 46084
  710.7 27.9 %copy-start.60 = (f32[480]{0:T(512)S(1)}, f32[480]{0:T(512)}, u32[]{:S(2)}) copy-start(f32[480]{0:T(512)} %copy-done.59) | copy-start | bytes 5764
  710.7 27.9 %copy-start.62 = (f32[480]{0:T(512)S(1)}, f32[480]{0:T(512)}, u32[]{:S(2)}) copy-start(f32[480]{0:T(512)} %copy-done.61) | copy-start | bytes 5764
  710.7 27.9 %copy-start.48 = (s32[1,480,8]{1,2,0:T(8,128)S(1)}, s32[1,480,8]{1,2,0:T(8,128)}, u32[]{:S(2)}) copy-start(s32[1,480,8]{1,2,0:T(8,128)} %param.35) | copy-start | bytes 46084
  710.7 28.0 %copy-start.5 = (bf16[1,480,2048]{2,1,0:T(8,128)(2,1)S(1)}, bf16[1,480,2048]{2,1,0:T(8,128)(2,1)}, u32[]{:S(2)}) copy-start(bf16[1,480,2048]{2,1,0:T(8,128)(2,1)} %param.18) | copy-start | bytes 5898244
  710.7 28.0 %copy-start.46 = (bf16[2048,16]{0,1:T(8,128)(2,1)S(1)}, bf16[2048,16]{0,1:T(8,128)(2,1)}, u32[]{:S(2)}) copy-start(bf16[2048,16]{0,1:T(8,128)(2,1)} %copy-done.45) | copy-start | bytes 196612
  710.7 28.0 %copy-start.53 = (f32[8,1,256]{2,1,0:T(1,128)S(1)}, f32[8,1,256]{2,1,0:T(1,128)}, u32[]{:S(2)}) copy-start(f32[8,1,256]{2,1,0:T(1,128)} %copy-done.52) | copy-start | bytes 24580
  710.7 28.0 %copy-start.70 = (f32[480]{0:T(512)S(1)}, f32[480]{0:T(512)}, u32[]{:S(2)}) copy-start(f32[480]{0:T(512)} %copy-done.69) | copy-start | bytes 5764
  748.0 11.7 copy-start.36
  748.1 11.7 copy-start.84
  802.0 13.4 copy-start.1
  802.0 14.5 copy-start.40
  802.0 66.6 %reduce-scatter.13.cloned.1.call-start = ((), (), s32[]{:S(2)}) async-start(), calls=%async_computation.18 | async-start | bytes 614400 | tf_op jit(solution)/shard_map/reduce_scatter | solution.py:258
  815.3 123.9 %reduce-scatter.23.cloned.1.call-start = ((), (), s32[]{:S(2)}) async-start(), calls=%async_computation.23 | async-start | bytes 73728 | tf_op jit(solution)/shard_map/reduce_scatter | solution.py:312
  816.4 39.0 %copy-start.23 = (f32[480,128]{1,0:T(8,128)S(1)}, f32[480,128]{1,0:T(8,128)}, u32[]{:S(2)}) copy-start(f32[480,128]{1,0:T(8,128)} %copy-done.22) | copy-start | bytes 737284
  816.4 124.1 %reduce-scatter.19.cloned.1.call-start = ((), (), s32[]{:S(2)}) async-start(), calls=%async_computation.21 | async-start | bytes 589824 | tf_op jit(solution)/shard_map/reduce_scatter | solution.py:297
  861.7 6.9 copy-start.6
  861.7 6.9 copy-start.51
  861.8 6.9 copy-start.66
  865.9 5.4 copy-start.75
  865.9 8.3 copy-start.73
  867.8 8.2 copy-start.27
  874.2 193.1 %all-reduce.22.cloned.1.call-start = ((), (), s32[]{:S(2)}) async-start(), calls=%async_computation.27 | async-start | bytes 7864320 | tf_op jit(solution)/shard_map/psum | solution.py:183
  878.9 224.6 %reduce-scatter.17.cloned.1.call-start = ((), (), s32[]{:S(2)}) async-start(), calls=%async_computation.20 | async-start | bytes 589824 | tf_op jit(solution)/shard_map/reduce_scatter | solution.py:294
  881.5 277.0 %reduce-scatter.21.cloned.1.call-start = ((), (), s32[]{:S(2)}) async-start(), calls=%async_computation.22 | async-start | bytes 4718592 | tf_op jit(solution)/shard_map/reduce_scatter | solution.py:306
  888.1 325.0 %reduce-scatter.15.cloned.1.call-start = ((), (), s32[]{:S(2)}) async-start(), calls=%async_computation.19 | async-start | bytes 4718592 | tf_op jit(solution)/shard_map/reduce_scatter | solution.py:291
  893.7 415.5 %reduce-scatter.29.cloned.1.call-start = ((), (), s32[]{:S(2)}) async-start(), calls=%async_computation.26 | async-start | bytes 14155776 | tf_op jit(solution)/shard_map/reduce_scatter | solution.py:323
  908.1 497.3 %reduce-scatter.27.cloned.1.call-start = ((), (), s32[]{:S(2)}) async-start(), calls=%async_computation.25 | async-start | bytes 14155776 | tf_op jit(solution)/shard_map/reduce_scatter | solution.py:320
  922.7 578.8 %reduce-scatter.25.cloned.1.call-start = ((), (), s32[]{:S(2)}) async-start(), calls=%async_computation.24 | async-start | bytes 14155776 | tf_op jit(solution)/shard_map/reduce_scatter | solution.py:317
  937.9 132.6 %copy-start.78 = (bf16[2048]{0:T(1024)(128)(2,1)S(1)}, bf16[2048]{0:T(1024)(128)(2,1)}, u32[]{:S(2)}) copy-start(bf16[2048]{0:T(1024)(128)(2,1)} %get-tuple-element.62) | copy-start | bytes 12292
  937.9 180.5 %copy-start.68 = (f32[480]{0:T(512)S(1)}, f32[480]{0:T(512)}, u32[]{:S(2)}) copy-start(f32[480]{0:T(512)} %copy-done.67) | copy-start | bytes 5764
  (39 other events, 94.7 us)
Sparse Core Ops, SparseCore 0:
  9.9 40.1 all-gather.9
  52.0 41.0 all-gather.11
  144.0 82.0 all-reduce.17
  227.8 73.5 all-gather.15
  303.2 74.5 all-gather.13
  379.5 74.5 all-gather.17
  619.0 81.9 all-reduce.19
  802.1 18.8 reduce-scatter.10
  823.6 21.4 reduce-scatter.12
  848.5 31.4 reduce-scatter.22
  883.4 34.1 reduce-scatter.18
  920.4 146.8 all-reduce.21
  1070.3 33.1 reduce-scatter.16
  1107.1 51.3 reduce-scatter.20
  1161.7 51.2 reduce-scatter.14
  1216.8 92.4 reduce-scatter.28
  1313.0 92.3 reduce-scatter.26
  1409.2 92.3 reduce-scatter.24
where the time goes:
time: 1520 us; the launch traced here: 1510 us
  waiting for transfers between devices  643 us (42%)
  matrix products  356 us (23%)
  local copies, waits for them, and re-layouts  264 us (17%)
  blocking collectives  118 us (8%)
  other arithmetic  113 us (7%)
  between operations  17.7 us (1%)
    psum x1, waiting for transfers between devices, shards(): lax.psum(jnp.sum(gates[..., None] * picked, 1).astype(jnp.bfloat16), 'ten...  125 us
    unnamed x183, local copies, waits for them, and re-layouts  94.2 us
    reduce_scatter x1, waiting for transfers between devices, shards(): lax.psum_scatter(grad_down.astype(jnp.bfloat16), ('dp', 'ctx'), scatter_d...  94.1 us
    reduce_scatter x1, waiting for transfers between devices, shards(): lax.psum_scatter(grad_gate.astype(jnp.bfloat16), ('dp', 'ctx'), scatter_d...  92.8 us
    reduce_scatter x1, waiting for transfers between devices, shards(): lax.psum_scatter(grad_up.astype(jnp.bfloat16), ('dp', 'ctx'), scatter_dim...  92.8 us
    gather x1, local copies, waits for them, and re-layouts, shards(): expert_out[expert_ids, slot_index].reshape(row_count, TOP, model_width)  72.1 us
    gather x1, local copies, waits for them, and re-layouts, shards(): grad_buffer[expert_ids, slot_index].reshape(row_count, TOP, model_width)  71.8 us
    all_gather x1, waiting for transfers between devices, shards(): lax.all_gather(down_weight, ('dp', 'ctx'), axis=2, tiled=True)  58.3 us
  transfers between devices with their start and end apart: 18, of which 10 were waited for; matrix products, arithmetic and copies ran while one was open for 32% of the time, Pallas kernels for 0%

commit v1 on v0

v1 whole, which is shorter than its diff:
```python
import functools
import math

import jax
import jax.numpy as jnp
from jax import lax
from jax.experimental import pallas as pl
from jax.experimental.pallas import tpu as pltpu
from jax.sharding import PartitionSpec as P

HEADS_Q = 32
HEADS_KV = 4
HEAD = 128
TOP = 8
EXPERTS = 16

EPS = 1e-06
THETA = 1000000.0
LOG2E = 1.4426950408889634
HIDE = -1e30

F32 = jnp.float32
BF16 = jnp.bfloat16
VMEM_BYTES = 58 * 1024 * 1024


def rounded(v):
    return v.astype(BF16)


def dot(a, b, contract):
    return lax.dot_general(a, b, ((contract[:1], contract[1:]), ((), ())), preferred_element_type=F32)


def after(value, *others):
    return lax.optimization_barrier((value,) + others)[0]


def to_core(v):
    return lax.ppermute(v, "ctx", [(i, i ^ 1) for i in range(4)])


def to_x(v):
    return lax.ppermute(v, "ctx", [(i, i ^ 2) for i in range(4)])


def to_dp(v):
    return lax.ppermute(v, "dp", [(0, 1), (1, 0)])


def sum_z(v):
    size, step = lax.axis_size("tensor"), 1
    while step < size:
        v = v + lax.ppermute(v, "tensor", [(i, i ^ step) for i in range(size)])
        step *= 2
    return v


def place():
    ctx = lax.axis_index("ctx")
    return lax.axis_index("dp"), ctx // 2, ctx % 2


def flips():
    dp, x, _ = place()
    return x + 2 * dp if lax.axis_size("dp") == 2 else x


def flip(v, axis, bit):
    return jnp.where(bit == 0, v, jnp.flip(v, axis))


def relative(v):
    dp, x, _ = place()
    count = lax.axis_size("dp")
    cut = v.reshape(v.shape[:-1] + (count, 2, v.shape[-1] // (2 * count)))
    cut = flip(cut, cut.ndim - 2, x)
    if count == 2:
        cut = flip(cut, cut.ndim - 3, dp)
    return cut.reshape(v.shape)


def halves(v, axis):
    return jnp.split(v, 2, axis)


class Link:
    def __init__(self, move):
        self.move, self.sent, self.last = move, [], []

    def send(self, v, *gate):
        gate = gate + tuple(self.sent[-2:-1]) + tuple(self.last)
        v = after(v, *gate) if gate else v
        self.last = [v]
        self.sent.append(self.move(v))
        return self.sent[-1]


def scatter_far(blocks, axis, x_link, y_link):
    far_first, far_second = halves(blocks[3], axis)
    return x_link.send(far_first), y_link.send(far_second)


def scatter_near(blocks, got, axis, x_link, y_link):
    y_first, y_second = halves(blocks[2], axis)
    x_first, x_second = halves(blocks[1], axis)
    x_got, y_got = x_link.send(x_first), y_link.send(y_second)
    y_first = rounded(y_first.astype(F32) + got[0].astype(F32))
    x_second = rounded(x_second.astype(F32) + got[1].astype(F32))
    return x_got, y_link.send(y_first), x_link.send(x_second), y_got


def scatter_sum(own, near, axis):
    x_first, y_first, x_second, y_second = (v.astype(F32) for v in near)
    return own.astype(F32) + jnp.concatenate([x_first + y_first, x_second + y_second], axis)


def gather_whole(block, axis):
    pair = jnp.concatenate([block, to_x(block)], axis)
    return lax.all_gather(pair, "dp", axis=axis, tiled=True)


def scatter_whole(blocks):
    kept = jnp.stack(blocks[0::2]).astype(F32) + to_x(jnp.stack(blocks[1::2])).astype(F32)
    return lax.psum_scatter(rounded(kept), "dp", scatter_dimension=0, tiled=False).astype(F32)


def whole(array):
    dims = len(array.shape)
    return pl.BlockSpec(array.shape, lambda *_: (0,) * dims)


SCALARS = pl.BlockSpec(memory_space=pltpu.SMEM)


def kernel_call(body, grid, in_specs, out_specs, out_shape, flops, moved, scratch=()):
    return pl.pallas_call(
        body,
        grid=grid,
        in_specs=in_specs,
        out_specs=out_specs,
        out_shape=out_shape,
        scratch_shapes=list(scratch),
        compiler_params=pltpu.CompilerParams(vmem_limit_bytes=VMEM_BYTES),
        cost_estimate=pl.CostEstimate(flops=int(flops), bytes_accessed=int(moved), transcendentals=0),
    )


def sds(shape, dtype):
    return jax.ShapeDtypeStruct(shape, dtype)


def piece_starts(scal, places, shard):
    core = scal[1]
    shift = {0: 0, 1: core * shard, 2: (1 - core) * shard}
    return [
        (start if kind == 0 else pl.multiple_of(start + shift[kind], length), length)
        for start, length, kind in places
    ]


def kernel_inverse_rms(v):
    return lax.rsqrt(jnp.mean(v * v, axis=-1, keepdims=True) + EPS)


def permute_kernel(scal, in_ref, out_ref):
    out_ref[...] = in_ref[...]


def permute_width(v, scal, blocks):
    rows, width = v.shape
    span = width // blocks
    return pl.pallas_call(
        permute_kernel,
        grid_spec=pltpu.PrefetchScalarGridSpec(
            num_scalar_prefetch=1,
            grid=(blocks,),
            in_specs=[pl.BlockSpec((rows, span), lambda j, s: (0, j ^ s[0]))],
            out_specs=pl.BlockSpec((rows, span), lambda j, s: (0, j)),
        ),
        out_shape=sds(v.shape, v.dtype),
        cost_estimate=pl.CostEstimate(flops=0, bytes_accessed=4 * v.size, transcendentals=0),
    )(scal, v)


def pick_columns(v, scal, shard, other):
    rows, width = v.shape
    count = width // (2 * shard)
    if shard % 128:
        which = 1 - scal[1] if other else scal[1]
        cut = v.reshape(rows, count, 2, shard)
        return lax.dynamic_index_in_dim(cut, which, 2, keepdims=False).reshape(rows, count * shard)
    return pl.pallas_call(
        permute_kernel,
        grid_spec=pltpu.PrefetchScalarGridSpec(
            num_scalar_prefetch=1,
            grid=(count,),
            in_specs=[pl.BlockSpec((rows, shard), lambda j, s: (0, 2 * j + (1 - s[1] if other else s[1])))],
            out_specs=pl.BlockSpec((rows, shard), lambda j, s: (0, j)),
        ),
        out_shape=sds((rows, count * shard), v.dtype),
        cost_estimate=pl.CostEstimate(flops=0, bytes_accessed=2 * v.size, transcendentals=0),
    )(scal, v)


def qkv_kernel(places, shard, blocks, scal, hid, gain, gain_q, gain_k, cos, sin, *refs):
    weights, (normed, hid_rel, raw, rot) = refs[: len(places)], refs[len(places) :]
    step, last = pl.program_id(0), pl.num_programs(0) - 1
    width = hid.shape[1]
    span = width // blocks

    @pl.when(step == 0)
    def _():
        for j in range(blocks):
            source = pl.multiple_of((scal[0] ^ j) * span, span)
            hid_rel[:, j * span : (j + 1) * span] = hid[:, pl.ds(source, span)]
        tokens = hid_rel[...].astype(F32)
        normed[...] = rounded(tokens * kernel_inverse_rms(tokens) * gain[...])

    total = jnp.zeros(raw.shape, F32)
    for (start, length), weight in zip(piece_starts(scal, places, shard), weights):
        total += dot(normed[:, pl.ds(start, length)], weight[...], (1, 0))
    raw[...] = total
    vector = jnp.where(step == last, gain_k[...], gain_q[...])
    for head in range(2):
        cut = total[:, head * HEAD : (head + 1) * HEAD]
        scaled = cut * kernel_inverse_rms(cut) * vector
        turned = scaled * cos[...] + pltpu.roll(scaled, HEAD // 2, 1) * sin[...]
        if head == 1:
            turned = jnp.where(step == last, cut, turned)
        rot[:, head * HEAD : (head + 1) * HEAD] = rounded(turned)


def qkv_call(scal, hid, gain, gain_q, gain_k, cos, sin, pieces, places, shard, blocks, columns):
    rows, width = hid.shape
    pair = 2 * HEAD
    small = (gain, gain_q, gain_k, cos, sin)
    block = pl.BlockSpec((rows, pair), lambda i: (0, i))
    return kernel_call(
        functools.partial(qkv_kernel, places, shard, blocks),
        (columns // pair,),
        [SCALARS, whole(hid)]
        + [whole(v) for v in small]
        + [pl.BlockSpec((p.shape[0], pair), lambda i: (0, i)) for p in pieces],
        [whole(hid), whole(hid), block, block],
        [sds(hid.shape, BF16), sds(hid.shape, BF16), sds((rows, columns), F32), sds((rows, columns), BF16)],
        2 * rows * width * columns,
        2 * width * columns + 12 * rows * width,
    )(scal, hid, *small, *pieces)


def write_bias(bias, key_side, query_side):
    seg = key_side[:, 0:1]
    seen = (seg == query_side[0:1]) | (seg == query_side[1:2]) | (seg == query_side[2:3])
    seen = seen & (key_side[:, 1:2] <= query_side[3:4])
    bias[...] = jnp.where(seen, 0.0, HIDE)


def key_tiles(count):
    tile = next(t for t in (384, 320, 256, 128) if count % t == 0)
    return [(s, tile) for s in range(0, count, tile)]


def attend_kernel(query, keys, values, key_side, query_side, mixed, inverse, bias, values_t):
    @pl.when(pl.program_id(0) == 0)
    def _():
        write_bias(bias, key_side[...], query_side[...])
        values_t[...] = values[...].T

    rows = query.shape[0]
    total = jnp.zeros((HEAD, rows), F32)
    row_sum = jnp.zeros((1, rows), F32)
    factor = LOG2E * HEAD**-0.5
    for start, tile in key_tiles(keys.shape[0]):
        raw = dot(keys[start : start + tile], query[...], (1, 1))
        weight = jnp.exp2(raw * factor + bias[start : start + tile])
        row_sum += jnp.sum(weight, 0, keepdims=True)
        total += dot(values_t[:, start : start + tile], rounded(weight), (1, 0))
    scale = 1.0 / row_sum
    mixed[...] = rounded((total * scale).T)
    inverse[0] = scale


def attend_call(rot, kv_all, key_side, query_side, heads):
    rows, count = rot.shape[0], kv_all.shape[0]
    column = pl.BlockSpec((rows, HEAD), lambda h: (0, h))
    return kernel_call(
        attend_kernel,
        (heads,),
        [
            column,
            pl.BlockSpec((count, HEAD), lambda h: (0, 0)),
            pl.BlockSpec((count, HEAD), lambda h: (0, 1)),
            whole(key_side),
            whole(query_side),
        ],
        [column, pl.BlockSpec((1, 1, rows), lambda h: (h, 0, 0))],
        [sds((rows, heads * HEAD), BF16), sds((heads, 1, rows), F32)],
        4 * heads * rows * count * HEAD,
        4 * rows * heads * HEAD + 4 * count * HEAD,
        [pltpu.VMEM((count, rows), F32), pltpu.VMEM((HEAD, count), BF16)],
    )(rot, kv_all, kv_all, key_side, query_side)


def attend_back_kernel(
    query, keys, values, key_side, query_side, grad, mixed, inverse, raw_query, cos, sin, gain,
    query_back, grad_kv, grad_gain, bias, keys_t,
):
    @pl.when(pl.program_id(0) == 0)
    def _():
        write_bias(bias, key_side[...], query_side[...])
        keys_t[...] = keys[...].T
        grad_kv[...] = jnp.zeros(grad_kv.shape, F32)
        grad_gain[...] = jnp.zeros(grad_gain.shape, F32)

    rows = query.shape[0]
    scale = HEAD**-0.5
    factor = LOG2E * scale
    both = grad[...].astype(F32) * mixed[...].astype(F32)
    mean = jnp.sum(both.T, 0, keepdims=True)
    norm = inverse[0]
    total = jnp.zeros((HEAD, rows), F32)
    for start, tile in key_tiles(keys.shape[0]):
        span = slice(start, start + tile)
        raw = dot(keys[span], query[...], (1, 1))
        prob = jnp.exp2(raw * factor + bias[span]) * norm
        grad_prob = dot(values[span], grad[...], (1, 1))
        grad_raw = rounded(prob * (grad_prob - mean) * scale)
        total += dot(keys_t[:, span], grad_raw, (1, 0))
        grad_kv[span, :HEAD] += dot(grad_raw, query[...], (1, 0))
        grad_kv[span, HEAD:] += dot(rounded(prob), grad[...], (1, 0))
    turned = total.T
    turned = turned * cos[...] - pltpu.roll(turned, HEAD // 2, 1) * sin[...]
    value = raw_query[...]
    shrink = kernel_inverse_rms(value)
    normal = value * shrink
    grad_gain[...] += jnp.sum(turned * normal, 0, keepdims=True)
    scaled = turned * gain[...]
    middle = jnp.mean(scaled * normal, axis=-1, keepdims=True)
    query_back[...] = rounded(shrink * (scaled - normal * middle))


def attend_back_call(rot, kv_all, key_side, query_side, grad, mixed, inverse, raw, cos, sin, gain, heads):
    rows, count = rot.shape[0], kv_all.shape[0]
    column = pl.BlockSpec((rows, HEAD), lambda h: (0, h))
    return kernel_call(
        attend_back_kernel,
        (heads,),
        [
            column,
            pl.BlockSpec((count, HEAD), lambda h: (0, 0)),
            pl.BlockSpec((count, HEAD), lambda h: (0, 1)),
            whole(key_side),
            whole(query_side),
            column,
            column,
            pl.BlockSpec((1, 1, rows), lambda h: (h, 0, 0)),
            column,
            whole(cos),
            whole(sin),
            whole(gain),
        ],
        [
            column,
            pl.BlockSpec((count, 2 * HEAD), lambda h: (0, 0)),
            pl.BlockSpec((1, HEAD), lambda h: (0, 0)),
        ],
        [sds((rows, heads * HEAD), BF16), sds((count, 2 * HEAD), F32), sds((1, HEAD), F32)],
        10 * heads * rows * count * HEAD,
        12 * rows * heads * HEAD + 12 * count * HEAD,
        [pltpu.VMEM((count, rows), F32), pltpu.VMEM((HEAD, count), BF16)],
    )(rot, kv_all, kv_all, key_side, query_side, grad, mixed, inverse, raw, cos, sin, gain)


def project_kernel(places, shard, scal, mixed, *refs):
    out = refs[-1]
    for (start, length), weight in zip(piece_starts(scal, places, shard), refs[:-1]):
        out[:, pl.ds(start, length)] = rounded(dot(mixed[...], weight[...], (1, 0)))


def project_call(scal, mixed, pieces, places, shard, width):
    rows, inner = mixed.shape
    return kernel_call(
        functools.partial(project_kernel, places, shard),
        (1,),
        [SCALARS, whole(mixed)] + [whole(p) for p in pieces],
        pl.BlockSpec((rows, width), lambda i: (0, 0)),
        sds((rows, width), BF16),
        2 * rows * inner * width,
        2 * inner * width + 2 * rows * (inner + width),
    )(scal, mixed, *pieces)


def project_back_kernel(places, shard, scal, grad, *refs):
    out = refs[-1]
    total = jnp.zeros(out.shape, F32)
    for (start, length), weight in zip(piece_starts(scal, places, shard), refs[:-1]):
        total += dot(grad[:, pl.ds(start, length)], weight[...], (1, 1))
    out[...] = rounded(total)


def project_back_call(scal, grad, pieces, places, shard, inner):
    rows, width = grad.shape
    tile = inner // 2
    return kernel_call(
        functools.partial(project_back_kernel, places, shard),
        (2,),
        [SCALARS, whole(grad)] + [pl.BlockSpec((tile, p.shape[1]), lambda i: (i, 0)) for p in pieces],
        pl.BlockSpec((rows, tile), lambda i: (0, i)),
        sds((rows, inner), BF16),
        2 * rows * inner * width,
        2 * inner * width + 2 * rows * (inner + width),
    )(scal, grad, *pieces)


def qkv_back_kernel(places, shard, scal, back, hid, *refs):
    weights, (part, grad_gain) = refs[: len(places)], refs[len(places) :]
    tokens = hid[...].astype(F32)
    shrink = kernel_inverse_rms(tokens)
    for (start, length), weight in zip(piece_starts(scal, places, shard), weights):
        lanes = pl.ds(start, length)
        value = dot(back[...], weight[...], (1, 1))
        part[:, lanes] = rounded(value)
        normal = hid[:, lanes].astype(F32) * shrink
        grad_gain[:, lanes] = jnp.sum(value * normal, 0, keepdims=True)


def qkv_back_call(scal, back, hid, pieces, places, shard):
    rows, width = hid.shape
    columns = back.shape[1]
    return kernel_call(
        functools.partial(qkv_back_kernel, places, shard),
        (1,),
        [SCALARS, whole(back), whole(hid)] + [whole(p) for p in pieces],
        [pl.BlockSpec((rows, width), lambda i: (0, 0)), pl.BlockSpec((1, width), lambda i: (0, 0))],
        [sds((rows, width), BF16), sds((1, width), F32)],
        2 * rows * columns * width,
        2 * columns * width + 2 * rows * (columns + 2 * width),
    )(scal, back, hid, *pieces)


def join_rows(own, other, scratch):
    rows = own.shape[0]

    @pl.when(pl.program_id(0) == 0)
    def _():
        scratch[:rows] = own[...]
        scratch[rows:] = other[...]


def product(weights, rows_ref):
    return dot(jnp.concatenate([w[...] for w in weights], 1), rows_ref[...], (1, 1))


def single(shape):
    dims = len(shape)
    return pl.BlockSpec(shape, lambda *_: (0,) * dims, pipeline_mode=pl.Buffered(1))


def products_kernel(own, other, *refs):
    weights, (out, both) = refs[:-2], refs[-2:]
    join_rows(own, other, both)
    out[...] = product(weights, both)


def products_call(own, other, pieces):
    rows, width = own.shape
    hidden = pieces[0].shape[0]
    tile = hidden // 4
    return kernel_call(
        products_kernel,
        (4,),
        [single(own.shape), single(own.shape)]
        + [pl.BlockSpec((tile, w.shape[1]), lambda i: (i, 0)) for w in pieces],
        pl.BlockSpec((tile, 2 * rows), lambda i: (i, 0)),
        sds((hidden, 2 * rows), F32),
        4 * rows * width * hidden,
        2 * hidden * width + 4 * rows * width + 8 * hidden * rows,
        [pltpu.VMEM((2 * rows, width), BF16)],
    )(own, other, *pieces)


def experts_kernel(places, hid, own, other, gate_ref, grad_act, gates, *refs):
    n = len(places)
    gated, gate_back, up_back, gated_t, gate_back_t, up_back_t, gate_part, both = refs[n:]
    join_rows(own, other, both)
    gate_pre, up_pre = gate_ref[...], product(refs[:n], both)
    sig = 1.0 / (1.0 + jnp.exp(-gate_pre))
    silu = gate_pre * sig
    act = silu * up_pre
    slope = sig * (1.0 + gate_pre * (1.0 - sig))
    count = gates.shape[0]
    for e in range(count):
        rows = slice(e * hid, (e + 1) * hid)
        gate = gates[e]
        raw = grad_act[rows, :]
        back = gate * raw
        gated[rows, :] = rounded(gate * act[rows])
        gate_back[rows, :] = rounded(back * up_pre[rows] * slope[rows])
        up_back[rows, :] = rounded(back * silu[rows])
        gate_part[e] = jnp.sum(act[rows] * raw, 0, keepdims=True)
    gated_t[...] = gated[...].T
    gate_back_t[...] = gate_back[...].T
    up_back_t[...] = up_back[...].T


def experts_call(own, other, gate_pre, grad_act, gates, up_p, places, hid):
    rows, width = own.shape
    both = 2 * rows
    experts = gates.shape[0]
    per = 2
    tile = per * hid
    act = pl.BlockSpec((tile, both), lambda i: (i, 0))
    act_t = pl.BlockSpec((both, tile), lambda i: (0, i))
    gate = pl.BlockSpec((per, 1, both), lambda i: (i, 0, 0))
    weights = list(up_p)
    hidden = experts * hid
    return kernel_call(
        functools.partial(experts_kernel, places, hid),
        (experts // per,),
        [single(own.shape), single(own.shape), act, act, gate]
        + [pl.BlockSpec((tile, w.shape[1]), lambda i: (i, 0)) for w in weights],
        [act, act, act, act_t, act_t, act_t, gate],
        [sds((hidden, both), BF16)] * 3
        + [sds((both, hidden), BF16)] * 3
        + [sds((experts, 1, both), F32)],
        2 * both * width * hidden,
        2 * hidden * width + 20 * hidden * both + 2 * both * width,
        [pltpu.VMEM((both, width), BF16)],
    )(own, other, gate_pre, grad_act, gates, *weights)


def backward_tiles(places, tile):
    return [(p, k) for p, (_, length, _) in enumerate(places) for k in range(length // tile)]


def spread_kernel(tiles, terms, *refs):
    acts = refs[:terms]
    n = (len(refs) - terms - 2) // terms
    own_ref, other_ref = refs[-2:]
    step = pl.program_id(0)
    rows = own_ref.shape[0]
    for p in range(n):
        steps = [t for t, (q, _) in enumerate(tiles) if q == p]

        @pl.when((step >= steps[0]) & (step <= steps[-1]))
        def _():
            value = sum(dot(acts[k][...], refs[terms + k * n + p][...], (1, 0)) for k in range(terms))
            own_ref[...] = value[:rows]
            other_ref[...] = rounded(value[rows:])


def spread_call(acts, weights, places):
    both, hidden = acts[0].shape
    rows = both // 2
    width = sum(length for _, length, _ in places)
    tile = 256
    tiles = backward_tiles(places, tile)
    assert [s for s, _, _ in places] == sorted(s for s, _, _ in places)

    def spec(p):
        steps = [t for t, (q, _) in enumerate(tiles) if q == p]
        first, last = steps[0], steps[-1]
        return pl.BlockSpec((hidden, tile), lambda t: (0, jnp.clip(t, first, last) - first))

    out = pl.BlockSpec((rows, tile), lambda t: (0, t))
    return kernel_call(
        functools.partial(spread_kernel, tiles, len(acts)),
        (len(tiles),),
        [single(a.shape) for a in acts] + [spec(p) for _ in acts for p in range(len(places))],
        [out, out],
        [sds((rows, width), F32), sds((rows, width), BF16)],
        2 * both * width * hidden * len(acts),
        2 * hidden * (width + both) * len(acts) + 6 * rows * width,
    )(*acts, *[w for pieces in weights for w in pieces])


def route_kernel(top_count, hid, attn_add, gain, router_t, routes, resid, moe_low, gates):
    value = hid[...].astype(F32) + attn_add[...].astype(F32)
    resid[...] = value
    moe_low[...] = rounded(value * kernel_inverse_rms(value) * gain[...])
    logits = dot(moe_low[...], router_t[...], (1, 1))
    numbers = lax.broadcasted_iota(jnp.int32, logits.shape, 1)
    chosen = routes[:, 0:1] == numbers
    for k in range(1, top_count):
        chosen = chosen | (routes[:, k : k + 1] == numbers)
    top = jnp.max(jnp.where(chosen, logits, HIDE), -1, keepdims=True)
    lift = jnp.where(chosen, jnp.exp(jnp.where(chosen, logits, top) - top), 0.0)
    gates[...] = lift / jnp.sum(lift, -1, keepdims=True)


def row_specs(arrays, rows, tile):
    return [
        pl.BlockSpec((tile, a.shape[1]), lambda i: (i, 0)) if a.shape[0] == rows else whole(a) for a in arrays
    ]


def route_call(hid, attn_add, gain, router_t, routes):
    rows, width = hid.shape
    tile = rows // 3
    arrays = (hid, attn_add, gain, router_t, routes)
    outs = [sds((rows, width), F32), sds((rows, width), BF16), sds((rows, router_t.shape[0]), F32)]
    return kernel_call(
        functools.partial(route_kernel, routes.shape[1]),
        (3,),
        row_specs(arrays, rows, tile),
        row_specs(outs, rows, tile),
        outs,
        40 * rows * width,
        10 * rows * width,
    )(*arrays)


def route_back_kernel(
    grad_moe, gate_grads, gates, resid, cot, router_t, gain, grad_resid, resid_low, grad_logits, grad_gain
):
    chosen = gates[...]
    part = gate_grads[...]
    middle = jnp.sum(chosen * part, -1, keepdims=True)
    grad_logits[...] = rounded(chosen * (part - middle))
    total = grad_moe[...].astype(F32) + dot(grad_logits[...], router_t[...], (1, 0))
    value = resid[...]
    shrink = kernel_inverse_rms(value)
    normal = value * shrink

    @pl.when(pl.program_id(0) == 0)
    def _():
        grad_gain[...] = jnp.zeros(grad_gain.shape, F32)

    grad_gain[...] += jnp.sum(total * normal, 0, keepdims=True)
    scaled = total * gain[...]
    mean = jnp.mean(scaled * normal, axis=-1, keepdims=True)
    out = cot[...].astype(F32) + shrink * (scaled - normal * mean)
    grad_resid[...] = out
    resid_low[...] = rounded(out)


def route_back_call(grad_moe, gate_grads, gates, resid, cot, router_t, gain):
    rows, width = resid.shape
    tile = rows // 3
    arrays = (grad_moe, gate_grads, gates, resid, cot, router_t, gain)
    outs = [
        sds((rows, width), F32),
        sds((rows, width), BF16),
        sds(gates.shape, BF16),
        sds((1, width), F32),
    ]
    return kernel_call(
        route_back_kernel,
        (3,),
        row_specs(arrays, rows, tile),
        row_specs(outs, rows, tile),
        outs,
        50 * rows * width,
        14 * rows * width,
    )(*arrays)


def to_whole_order(scal, blocks, value, out):
    span = value.shape[1] // blocks
    for j in range(blocks):
        target = pl.multiple_of((scal[0] ^ j) * span, span)
        out[:, pl.ds(target, span)] = value[:, j * span : (j + 1) * span]


def add_kernel(blocks, scal, first, second, out):
    value = rounded(first[...] + second[...].astype(F32))
    to_whole_order(scal, blocks, value, out)


def last_kernel(blocks, scal, hid, grad_resid, grad_normed, gain, out):
    tokens = hid[...].astype(F32)
    shrink = kernel_inverse_rms(tokens)
    normal = tokens * shrink
    scaled = grad_normed[...].astype(F32) * gain[...]
    middle = jnp.mean(scaled * normal, axis=-1, keepdims=True)
    value = rounded(grad_resid[...] + shrink * (scaled - normal * middle))
    to_whole_order(scal, blocks, value, out)


def by_rows(body, scal, arrays, blocks, steps):
    rows, width = arrays[0].shape
    tile = rows // steps
    spec = pl.BlockSpec((tile, width), lambda i: (i, 0))
    return kernel_call(
        functools.partial(body, blocks),
        (steps,),
        [SCALARS] + [spec if a.shape[0] == rows else whole(a) for a in arrays],
        spec,
        sds((rows, width), BF16),
        10 * rows * width,
        8 * rows * width,
    )(scal, *arrays)


def inverse_rms(v):
    return lax.rsqrt(jnp.mean(v * v, axis=-1, keepdims=True) + EPS)


def angle_tables(positions):
    half_size = HEAD // 2
    frequency = jnp.exp(jnp.arange(half_size, dtype=F32) * (-2.0 * math.log(THETA) / HEAD))
    angles = positions.astype(F32)[..., None] * frequency
    sine = jnp.sin(angles)
    cosine = jnp.cos(angles)
    return jnp.concatenate([cosine, cosine], -1), jnp.concatenate([-sine, sine], -1)


def rotate_back(field, cosine, signed_sine):
    half_size = field.shape[-1] // 2
    turned = jnp.concatenate([field[..., half_size:], field[..., :half_size]], -1)
    return field * cosine - turned * signed_sine


def norm_back(scaled, scale, normal):
    return scale * (scaled - normal * jnp.mean(scaled * normal, axis=-1, keepdims=True))


def lookup_parent(segment_ids, parent):
    seg_table = jnp.arange(parent.shape[-1], dtype=jnp.int32)
    return jnp.sum(jnp.where(segment_ids[..., None] == seg_table, parent, 0), -1)


def shards(
    hidden,
    cotangent,
    gain_attn,
    query_weight,
    key_weight,
    value_weight,
    gain_query,
    gain_key,
    out_weight,
    gain_moe,
    router_weight,
    gate_weight,
    up_weight,
    down_weight,
    segment,
    parent,
    tree_depth,
    routes,
):
    _, rows, width = hidden.shape
    dp, x, core = place()
    ctx = lax.axis_index("ctx")
    count = lax.axis_size("dp")
    paired = count == 2
    chips = 2 * count
    tensor = lax.axis_size("tensor")
    heads = HEADS_Q // tensor
    shard = query_weight.shape[0]
    span = 2 * shard
    inner = heads * HEAD
    columns = inner + 2 * HEAD
    half = EXPERTS // 2
    hid = down_weight.shape[1]
    scal = jnp.stack([flips(), core]).astype(jnp.int32)

    def by_core(own, other, axis):
        return jnp.where(core == 0, jnp.stack([own, other], axis), jnp.stack([other, own], axis))

    x_link, y_link = Link(to_x), Link(to_dp)

    def near_pieces(block):
        return x_link.send(block), y_link.send(block)

    def far_pieces(block, near, axis):
        x_block, y_block = near
        far_first = y_link.send(halves(x_block, axis)[0])
        far_second = x_link.send(halves(y_block, axis)[1])
        size = block.shape[axis]
        arrays = [block, x_block, y_block, far_first, far_second]
        starts = [0, span, 2 * span, 3 * span, 3 * span + size // 2]
        return arrays, [(s, a.shape[axis], 0) for s, a in zip(starts, arrays)]

    def whole_piece(block, axis):
        own = gather_whole(block, axis)
        cut = own.shape[:axis] + (chips, shard) + own.shape[axis + 1 :]
        full = by_core(own.reshape(cut), to_core(own).reshape(cut), axis + 1)
        return [full.reshape(own.shape[:axis] + (width,) + own.shape[axis + 1 :])], [(0, width, 0)]

    per = gain_query.shape[0]
    gain_row = jnp.concatenate([gain_query, gain_key])
    small = jnp.concatenate(
        [
            gain_attn[None],
            gain_moe[None],
            router_weight.T,
            jnp.pad(gain_row, (0, shard - 2 * per))[None],
            jnp.zeros((13, shard), BF16),
        ]
    )
    qkv_shard = jnp.concatenate([query_weight, key_weight, value_weight], 1)
    if paired:
        qkv_near = near_pieces(qkv_shard)
        small_x, small_y = near_pieces(small)
        qkv_own, places = far_pieces(qkv_shard, qkv_near, 0)
        small_own = jnp.stack([small, small_x, small_y, y_link.send(small_x)], 1)
        qkv_pieces = qkv_own + [to_core(a) for a in qkv_own]
        qkv_places = [(s, n, kind) for kind in (1, 2) for s, n, _ in places]
    else:
        small_own = gather_whole(small, 1).reshape(32, chips, shard)
        qkv_pieces, qkv_places = whole_piece(qkv_shard, 0)
    small_all = by_core(small_own, to_core(small_own), 2).reshape(32, width)
    gain_one = small_all[0:1].astype(F32)
    gain_two = small_all[1:2].astype(F32)
    router_t = small_all[2 : 2 + EXPERTS]
    gain_heads = relative(small_all[2 + EXPERTS])
    gain_heads = gain_heads.reshape(2 * chips, shard)[:, : 2 * per].astype(F32)
    gain_q = gain_heads[:, :per].reshape(1, HEAD)
    gain_k = gain_heads[:, per:].reshape(1, HEAD)

    if paired:
        out_own, places = far_pieces(out_weight, near_pieces(out_weight), 1)
        out_pieces = out_own + [to_core(a) for a in out_own]
        out_places = [(s, n, kind) for kind in (1, 2) for s, n, _ in places]
    else:
        out_pieces, out_places = whole_piece(out_weight, 1)

    def expert_block(weight):
        own = lax.dynamic_slice_in_dim(weight, core * half, half, 0)
        sent = lax.dynamic_slice_in_dim(weight, (1 - core) * half, half, 0)
        return by_core(own, to_core(sent), 2).reshape(half * hid, span)

    expert_blocks = [
        expert_block(after(w, qkv_pieces[1 % len(qkv_pieces)]))
        for w in (down_weight, gate_weight.transpose(0, 2, 1), up_weight.transpose(0, 2, 1))
    ]

    cosine, sine = angle_tables(tree_depth[0])
    normed, tokens_low, raw, rot = qkv_call(
        scal, hidden[0], gain_one, gain_q, gain_k, cosine, sine, qkv_pieces, qkv_places, shard, chips, columns
    )
    key_value = rot[:, inner:]
    kv_x = x_link.send(key_value)
    kv_other = to_core(key_value)
    kv_all = jnp.concatenate([key_value, kv_other, kv_x, to_core(kv_x)])
    if paired:
        down_near = near_pieces(expert_blocks[0])
        gate_near = near_pieces(expert_blocks[1])
        down_pieces, expert_places = far_pieces(expert_blocks[0], down_near, 1)
        up_near = near_pieces(expert_blocks[2])
        gate_pieces, _ = far_pieces(expert_blocks[1], gate_near, 1)
        up_pieces, _ = far_pieces(expert_blocks[2], up_near, 1)
    else:
        down_pieces, gate_pieces, up_pieces = ([gather_whole(b, 1)] for b in expert_blocks)
        expert_places = [(0, width, 0)]

    seg = segment[0].reshape(2, 2, rows)
    seg_rel = flip(flip(seg, 0, x), 1, core).reshape(4 * rows)
    position = jnp.arange(4 * rows, dtype=jnp.int32).reshape(2, 2, rows)
    key_pos = flip(flip(position, 0, x), 1, core).reshape(4 * rows)
    first_up = lookup_parent(seg_rel[:rows], parent[0])
    second_up = lookup_parent(first_up, parent[0])
    key_side = jnp.stack([seg_rel, key_pos], 1)
    query_side = jnp.stack([seg_rel[:rows], first_up, second_up, key_pos[:rows]])

    mixed_low, inverse = attend_call(rot, kv_all, key_side, query_side, heads)
    attn_part = project_call(scal, mixed_low, out_pieces, out_places, shard, width)
    attn_add = lax.psum(attn_part, "tensor")

    cot = permute_width(cotangent[0], scal, chips)
    cot_other = to_core(cot)
    grad_act = products_call(cot, cot_other, down_pieces)
    attn_add = after(attn_add, grad_act, *gate_pieces[1:3])
    resid, moe_low, gates = route_call(tokens_low, attn_add, gain_two, router_t, routes[0])
    moe_other = to_core(moe_low)
    gate_pre = products_call(moe_low, moe_other, gate_pieces)
    gates_t = gates.T
    gates_own = lax.dynamic_slice_in_dim(gates_t, core * half, half, 0)
    gates_sent = lax.dynamic_slice_in_dim(gates_t, (1 - core) * half, half, 0)
    gate_pair = jnp.concatenate([gates_own, to_core(gates_sent)], 1)[:, None, :]

    gated_act, gate_back, up_back, gated_t, gate_back_t, up_back_t, gate_part = experts_call(
        moe_low, moe_other, gate_pre, grad_act, gate_pair, up_pieces, expert_places, hid
    )
    part_own, part_other = spread_call([gate_back_t, up_back_t], [gate_pieces, up_pieces], expert_places)
    moe_sum = rounded(part_own + to_core(part_other).astype(F32))
    grad_moe_in = lax.psum(moe_sum, "tensor")
    gate_part = gate_part[:, 0]
    gate_other = to_core(gate_part[:, rows:])
    gate_grads = sum_z(by_core(gate_part[:, :rows], gate_other, 0).reshape(EXPERTS, rows)).T
    pair_x = jnp.concatenate([moe_low, moe_other])
    pair_dy = jnp.concatenate([cot, cot_other])

    def expert_blocks_of(left, right):
        left = after(left, moe_sum)
        return [rounded(dot(left, right[:, r * span : (r + 1) * span], (1, 0))) for r in range(chips)]

    grad_blocks = [
        expert_blocks_of(gated_act, pair_dy),
        expert_blocks_of(gate_back, pair_x),
        expert_blocks_of(up_back, pair_x),
    ]
    if paired:
        down_far = scatter_far(grad_blocks[0], 1, x_link, y_link)
        gate_far = scatter_far(grad_blocks[1], 1, x_link, y_link)
        down_got = scatter_near(grad_blocks[0], down_far, 1, x_link, y_link)
        up_far = scatter_far(grad_blocks[2], 1, x_link, y_link)
        gate_got = scatter_near(grad_blocks[1], gate_far, 1, x_link, y_link)

    out_own, out_other = spread_call([after(gated_t, moe_sum)], [down_pieces], expert_places)
    out_sum = rounded(out_own + to_core(out_other).astype(F32))
    quarter = rows // tensor
    first_row = lax.axis_index("tensor") * quarter
    out_sum = after(out_sum, grad_moe_in)
    moe_add = lax.psum_scatter(out_sum, "tensor", scatter_dimension=0, tiled=True)
    moe_add = by_rows(add_kernel, scal, [lax.dynamic_slice_in_dim(resid, first_row, quarter, 0), moe_add], chips, 1)
    output = lax.all_gather(moe_add, "tensor", axis=0, tiled=True)[None]

    grad_resid, resid_low, grad_logits, grad_gain_two = route_back_call(
        grad_moe_in, gate_grads, gates, resid, cot, router_t, gain_two
    )

    grad_mixed = project_back_call(scal, after(resid_low, out_sum), out_pieces, out_places, shard, inner)
    query_back, grad_kv, grad_gain_q = attend_back_call(
        rot, kv_all, key_side, query_side, grad_mixed, mixed_low, inverse, raw, cosine, sine, gain_q, heads
    )
    grad_kv = after(grad_kv, moe_add).reshape(4, rows, 2 * HEAD)
    kv_got = to_core(rounded(jnp.stack([grad_kv[1], grad_kv[3]]))).astype(F32)
    kv_far = x_link.send(rounded(grad_kv[2] + kv_got[1])).astype(F32)
    kv_sum = grad_kv[0] + kv_got[0] + kv_far
    value_back = rounded(kv_sum[:, HEAD:])
    grad_key_n = rotate_back(kv_sum[:, :HEAD], cosine, sine)
    raw_key = raw[:, inner : inner + HEAD]
    scale_k = inverse_rms(raw_key)
    normal_k = raw_key * scale_k
    grad_gain_k = jnp.sum(grad_key_n * normal_k, 0)
    key_back = rounded(norm_back(grad_key_n * gain_k, scale_k, normal_k))
    qkv_back = jnp.concatenate([query_back, key_back, value_back], 1)

    back_part, grad_gain_one = qkv_back_call(scal, qkv_back, tokens_low, qkv_pieces, qkv_places, shard)
    grad_normed = lax.psum(back_part, "tensor")
    grad_hidden = by_rows(last_kernel, scal, [tokens_low, grad_resid, grad_normed, gain_one], chips, 3)[None]

    late_resid, late_mixed, late_normed, late_moe = lax.optimization_barrier(
        (resid_low, mixed_low, normed, moe_low, back_part)
    )[:4]
    grad_router_t = dot(grad_logits, late_moe, (0, 0))
    normed_sent, normed_own = (pick_columns(late_normed, scal, shard, other) for other in (True, False))
    qkv_sent = to_core(rounded(dot(normed_sent, qkv_back, (0, 0))))
    qkv_sum = dot(normed_own, qkv_back, (0, 0)) + qkv_sent.astype(F32)
    qkv_sum = rounded(qkv_sum)
    resid_sent, resid_own = (pick_columns(late_resid, scal, shard, other) for other in (True, False))
    out_sent = to_core(rounded(dot(late_mixed, resid_sent, (0, 0))))
    out_sum = dot(late_mixed, resid_own, (0, 0)) + out_sent.astype(F32)
    out_sum = rounded(out_sum)
    qkv_blocks = [qkv_sum[r * shard : (r + 1) * shard] for r in range(chips)]
    out_blocks = [out_sum[:, r * shard : (r + 1) * shard] for r in range(chips)]
    if paired:
        up_got = scatter_near(grad_blocks[2], after(up_far, query_back), 1, x_link, y_link)
        qkv_far = scatter_far(qkv_blocks, 0, x_link, y_link)
        out_far = scatter_far(out_blocks, 0, x_link, y_link)
        qkv_got = scatter_near(qkv_blocks, qkv_far, 0, x_link, y_link)
        out_got = scatter_near(out_blocks, out_far, 0, x_link, y_link)
        expert_sums = [
            scatter_sum(grad_blocks[0][0], after(down_got, query_back), 1),
            scatter_sum(grad_blocks[1][0], after(gate_got, back_part), 1),
            scatter_sum(grad_blocks[2][0], up_got, 1),
        ]
        grad_qkv = scatter_sum(qkv_blocks[0], qkv_got, 0)
        grad_out_weight = scatter_sum(out_blocks[0], out_got, 0)
    else:
        expert_sums = [scatter_whole(b) for b in grad_blocks]
        grad_qkv, grad_out_weight = scatter_whole(qkv_blocks), scatter_whole(out_blocks)

    def expert_grad(total):
        total = total.reshape(half, hid, span)
        own = lax.dynamic_slice_in_dim(total, core * shard, shard, 2)
        sent = lax.dynamic_slice_in_dim(total, (1 - core) * shard, shard, 2)
        other = to_core(rounded(sent)).astype(F32)
        return by_core(own, other, 0).reshape(EXPERTS, hid, shard)

    grad_down, grad_gate, grad_up = (expert_grad(v) for v in expert_sums)
    grad_gate, grad_up = grad_gate.transpose(0, 2, 1), grad_up.transpose(0, 2, 1)

    share = 1.0 / tensor
    head_rows = jnp.concatenate(
        [grad_gain_q.reshape(2 * chips, per), grad_gain_k.reshape(2 * chips, per)], 1
    )
    head_rows = relative(jnp.pad(head_rows, ((0, 0), (0, shard - 2 * per))).reshape(width))
    table = jnp.concatenate(
        [
            grad_gain_one,
            grad_gain_two * share,
            grad_router_t * share,
            head_rows[None],
            jnp.zeros((5, width), F32),
        ]
    ).reshape(24, chips, 2, shard)
    table_own = lax.dynamic_index_in_dim(table, core, 2, keepdims=False)
    table_sent = lax.dynamic_index_in_dim(table, 1 - core, 2, keepdims=False)
    table = table_own + to_core(table_sent)
    table = table.reshape(24, count, 2, shard)
    table = table[:, :, 0] + to_x(table[:, :, 1])
    if paired:
        table = table[:, 0] + to_dp(table[:, 1])
    else:
        table = lax.psum_scatter(table, "dp", scatter_dimension=1, tiled=False)
    mine = sum_z(table)
    gains = mine[2 + EXPERTS, : 2 * per]

    return (
        output,
        grad_hidden,
        mine[0],
        grad_qkv[:, :inner],
        grad_qkv[:, inner : inner + HEAD],
        grad_qkv[:, inner + HEAD :],
        gains[:per],
        gains[per:],
        grad_out_weight,
        mine[1],
        mine[2 : 2 + EXPERTS].T,
        grad_gate,
        grad_up,
        grad_down,
    )


def solution(mesh):
    plane = ("dp", "ctx")
    in_specs = (
        P("dp", "ctx", None),
        P("dp", "ctx", None),
        P(plane),
        P(plane, "tensor"),
        P(plane, "tensor"),
        P(plane, "tensor"),
        P(plane),
        P(plane),
        P("tensor", plane),
        P(plane),
        P(plane, None),
        P(None, plane, "tensor"),
        P(None, plane, "tensor"),
        P(None, "tensor", plane),
        P("dp", None),
        P("dp", None),
        P("dp", "ctx"),
        P("dp", "ctx", None),
    )
    out_specs = (
        P("dp", "ctx", None),
        P("dp", "ctx", None),
        P(plane),
        P(plane, "tensor"),
        P(plane, "tensor"),
        P(plane, "tensor"),
        P(plane),
        P(plane),
        P("tensor", plane),
        P(plane),
        P(plane, None),
        P(None, plane, "tensor"),
        P(None, plane, "tensor"),
        P(None, "tensor", plane),
    )
    return jax.shard_map(shards, mesh=mesh, in_specs=in_specs, out_specs=out_specs, check_vma=False)
```

time: 1520 us -> 766 us (0.50)
  waiting for transfers between devices: 643 us -> 268 us
  matrix products: 356 us -> 52 us
  Pallas kernels: 0 us -> 202 us
  local copies, waits for them, and re-layouts: 264 us -> 83.1 us
  blocking collectives: 118 us -> 0 us
  starting transfers between devices: 1.52 us -> 69.8 us
  other arithmetic: 113 us -> 64.9 us
    reduce_scatter x10 -> x1, waiting for transfers between devices: 384 us -> 0.01 us  [shards(): lax.psum_scatter(out_sum, 'tensor', scatter_dimension=0, tiled=True)]
    dot_general x29 -> x17, matrix products: 338 us -> 52 us  [dot(): lax.dot_general(a, b, ((contract[:1], contract[1:]), ((), ())), preferred...]
    ppermute x0 -> x90, waiting for transfers between devices: none -> 205 us  [the longest x29 141 us: to_x(): return lax.ppermute(v, 'ctx', [(i, i ^ 2) for i in range(4)])]
    pallas_call x0 -> x20, Pallas kernels: none -> 202 us  [the longest x2 33.8 us: spread_call(): kernel_call(functools.partial(spread_kernel, tiles, len(acts)), (len(tile...]
    gather x3 -> x0, local copies, waits for them, and re-layouts: 160 us -> none  [the longest x1 72.1 us: shards(): expert_out[expert_ids, slot_index].reshape(row_count, TOP, model_width)]
    psum x3, waiting for transfers between devices: 177 us -> 62.4 us  [the longest x1 50.4 us: shards(): grad_moe_in = lax.psum(moe_sum, 'tensor')]
    all_gather x5 -> x1, waiting for transfers between devices: 77.9 us -> 0.01 us  [shards(): output = lax.all_gather(moe_add, 'tensor', axis=0, tiled=True)[None]]
    unnamed x183 -> x181, local copies, waits for them, and re-layouts: 94.2 us -> 21.9 us
  transfers between devices with their start and end apart: 18 -> 95, of which waited for: 10 -> 29; matrix products, arithmetic and copies ran while one was open for 32% -> 23% of each run, Pallas kernels for 0% -> 20%
where the time goes in v1:
time: 766 us; the launch traced here: 755 us
  waiting for transfers between devices  268 us (35%)
  Pallas kernels  202 us (26%)
  local copies, waits for them, and re-layouts  83.1 us (11%)
  starting transfers between devices  69.8 us (9%)
  other arithmetic  64.9 us (8%)
  matrix products  52 us (7%)
  between operations  15.9 us (2%)
    ppermute x29, waiting for transfers between devices, to_x(): return lax.ppermute(v, 'ctx', [(i, i ^ 2) for i in range(4)])  141 us
    dot_general x17, matrix products, dot(): lax.dot_general(a, b, ((contract[:1], contract[1:]), ((), ())), preferred...  52 us
    psum x1, waiting for transfers between devices, shards(): grad_moe_in = lax.psum(moe_sum, 'tensor')  50.4 us
    ppermute x28, waiting for transfers between devices, to_dp(): return lax.ppermute(v, 'dp', [(0, 1), (1, 0)])  42 us
    ppermute x29, starting transfers between devices, to_x(): return lax.ppermute(v, 'ctx', [(i, i ^ 2) for i in range(4)])  34.3 us
    pallas_call x2, Pallas kernels, spread_call(): kernel_call(functools.partial(spread_kernel, tiles, len(acts)), (len(tile...  33.8 us
    pallas_call x1, Pallas kernels, attend_back_call(): kernel_call(attend_back_kernel, (heads,), [column, pl.BlockSpec((count, H...  30.1 us
    ppermute x28, starting transfers between devices, to_dp(): return lax.ppermute(v, 'dp', [(0, 1), (1, 0)])  27 us
  transfers between devices with their start and end apart: 95, of which 29 were waited for; matrix products, arithmetic and copies ran while one was open for 23% of the time, Pallas kernels for 20%

profile of v1, /device:TPU:0, one launch (start us, length us, event | category | flops | bytes accessed | tf_op | source)
XLA Modules:
  0.0 755.3 jit_solution(8603733651398625471)
XLA Ops:
  10.2 3.0 collective-permute-start.2
  23.7 4.5 collective-permute-done
  34.1 2.4 dynamic-slice_bitcast_fusion.4
  41.9 5.5 collective-permute-done.7.refs_4_
  47.9 8.1 %collective-permute-done.14.refs_1_ = bf16[1024,256]{1,0:T(8,128)(2,1)} collective-permute-done((bf16[1024,256]{1,0:T(8,128)(2,1)}, bf16[1024,256]{1,0:T(8,128)(2,1)}, u32[]{:S(2)}, u32[]{:S(2)}) %collective-permute-start.14) | collective-permute-done | bytes 524320 | tf_op jit(solution)/shard_map/ppermute | solution.py:44
  63.6 11.6 %shard_map.281 = (bf16[480,2048]{1,0:T(8,128)(2,1)}, bf16[480,2048]{1,0:T(8,128)(2,1)}, f32[480,1280]{1,0:T(8,128)}, bf16[480,1280]{1,0:T(8,128)(2,1)}) custom-call(s32[2]{0:T(128)} %pad_add_fusion.2.scal, bf16[480,2048]{1,0:T(8,128)(2,1)} %bitcast.192, f32[1,2048]{1,0:T(1,128)} %reshape.208.gain, f32[1,128]{1,0:T(1,128)} %reshape.192.gain_q.gain, ...), custom_call_target="tpu_custom_call" | custom-call | flops 2516582400 | bytes 17039360 | tf_op jit(solution)/shard_map/pallas_call | solution.py:239
  80.9 10.4 %collective-permute-done.16 = bf16[480,256]{1,0:T(8,128)(2,1)} collective-permute-done((bf16[480,256]{1,0:T(8,128)(2,1)S(1)}, bf16[480,256]{1,0:T(8,128)(2,1)}, u32[]{:S(2)}, u32[]{:S(2)}) %collective-permute-start.16) | collective-permute-done | bytes 245792 | tf_op jit(solution)/shard_map/ppermute | solution.py:44
  91.9 2.3 maximum_select_fusion.3
  98.8 4.5 shard_map.284.own.cot
  105.7 2.2 pad_maximum_fusion.3.keys.values
  108.0 16.4 %shard_map.282 = (bf16[480,1024]{1,0:T(8,128)(2,1)}, f32[8,1,480]{2,1,0:T(1,128)}) custom-call(bf16[480,1280]{1,0:T(8,128)(2,1)} %get-tuple-element.125.query, bf16[1920,256]{1,0:T(8,128)(2,1)} %pad_maximum_fusion.3.keys.values, bf16[1920,256]{1,0:T(8,128)(2,1)} %pad_maximum_fusion.3.keys.values, s32[1920,2]{1,0:T(8,128)} %copy.179.key_side, ...), custom_call_target="tpu_custom_call" | custom-call | flops 3774873600 | bytes 2949120 | tf_op jit(solution)/shard_map/pallas_call | solution.py:287
  125.3 6.6 shard_map.283
  144.9 44.8 %collective-permute-done.31.refs_4_.refs_5_ = bf16[1536,256]{1,0:T(8,128)(2,1)S(1)} collective-permute-done((bf16[1536,256]{1,0:T(8,128)(2,1)S(1)}, bf16[1536,256]{1,0:T(8,128)(2,1)S(1)}, u32[]{:S(2)}, u32[]{:S(2)}) %collective-permute-start.31) | collective-permute-done | bytes 786464 | tf_op jit(solution)/shard_map/ppermute | solution.py:44
  190.5 12.2 %shard_map.285.grad_act = f32[1536,960]{1,0:T(8,128)} custom-call(bf16[480,2048]{1,0:T(8,128)(2,1)} %shard_map.284.own.cot, bf16[480,2048]{1,0:T(8,128)(2,1)} %collective-permute-done.25.other, bf16[1536,512]{1,0:T(8,128)(2,1)} %bitcast.167, bf16[1536,512]{1,0:T(8,128)(2,1)} %collective-permute-done.27.refs_1_.refs_2_, ...), custom_call_target="tpu_custom_call" | custom-call | flops 6039797760 | bytes 16121856 | tf_op jit(solution)/shard_map/pallas_call | solution.py:470
  202.8 12.0 %all-reduce.6.cloned.1.call-done.attn_add = bf16[480,2048]{1,0:T(8,128)(2,1)} async-done(((bf16[480,2048]{1,0:T(8,128)(2,1)}), bf16[480,2048]{1,0:T(8,128)(2,1)}) %all-reduce.6.cloned.1.call-update) | async-done | bytes 1966096 | tf_op jit(solution)/shard_map/psum | solution.py:861
  214.8 6.3 shard_map.286
  235.4 26.7 %collective-permute-done.40.refs_2_.refs_9_ = bf16[1536,512]{1,0:T(8,128)(2,1)} collective-permute-done((bf16[1536,512]{1,0:T(8,128)(2,1)S(1)}, bf16[1536,512]{1,0:T(8,128)(2,1)}, u32[]{:S(2)}, u32[]{:S(2)}) %collective-permute-start.40) | collective-permute-done | bytes 1572896 | tf_op jit(solution)/shard_map/ppermute | solution.py:48
  268.3 12.2 %collective-permute-done.37.refs_4_.refs_6_ = bf16[1536,256]{1,0:T(8,128)(2,1)} collective-permute-done((bf16[1536,256]{1,0:T(8,128)(2,1)}, bf16[1536,256]{1,0:T(8,128)(2,1)}, u32[]{:S(2)}, u32[]{:S(2)}) %collective-permute-start.37) | collective-permute-done | bytes 786464 | tf_op jit(solution)/shard_map/ppermute | solution.py:44
  281.8 11.7 %shard_map.287.gate_ref = f32[1536,960]{1,0:T(8,128)} custom-call(bf16[480,2048]{1,0:T(8,128)(2,1)} %get-tuple-element.190.own, bf16[480,2048]{1,0:T(8,128)(2,1)} %copy-done.3, bf16[1536,512]{1,0:T(8,128)(2,1)} %bitcast.77.refs_0_.refs_2_, bf16[1536,512]{1,0:T(8,128)(2,1)} %collective-permute-done.32.refs_1_.refs_3_, ...), custom_call_target="tpu_custom_call" | custom-call | flops 6039797760 | bytes 16121856 | tf_op jit(solution)/shard_map/pallas_call | solution.py:470
  293.5 3.0 collective-permute-done.42.refs_4_.refs_11_
  298.3 19.7 %shard_map.288 = (bf16[1536,960]{1,0:T(8,128)(2,1)}, bf16[1536,960]{1,0:T(8,128)(2,1)}, bf16[1536,960]{1,0:T(8,128)(2,1)}, bf16[960,1536]{1,0:T(8,128)(2,1)}, bf...) custom-call(bf16[480,2048]{1,0:T(8,128)(2,1)} %get-tuple-element.190.own, ...), custom_call_target="tpu_custom_call" | custom-call | flops 6039797760 | bytes 39714816 | tf_op jit(solution)/shard_map/pallas_call | solution.py:518
  318.1 21.0 %shard_map.289 = (f32[480,2048]{1,0:T(8,128)}, bf16[480,2048]{1,0:T(8,128)(2,1)}) custom-call(bf16[960,1536]{1,0:T(8,128)(2,1)} %get-tuple-element.152.refs_0_, bf16[960,1536]{1,0:T(8,128)(2,1)} %get-tuple-element.153.refs_1_, bf16[1536,512]{1,0:T(8,128)(2,1)} %bitcast.77.refs_0_.refs_2_, bf16[1536,512]{1,0:T(8,128)(2,1)} %collective-permute-done.32.refs_1_.refs_3_, ...), custom_call_target="tpu_custom_call" | custom-call | flops 12079595520 | bytes 24379392 | tf_op jit(solution)/shard_map/pallas_call | solution.py:567
  343.7 2.4 constant_dynamic-slice_fusion.3.first
  346.1 5.2 collective-permute-done.46
  354.3 10.2 %collective-permute-done.47 = f32[16,480]{0,1:T(8,128)S(1)} collective-permute-done((f32[16,480]{0,1:T(8,128)S(1)}, f32[16,480]{0,1:T(8,128)S(1)}, u32[]{:S(2)}, u32[]{:S(2)}) %collective-permute-start.47) | collective-permute-done | bytes 30752 | tf_op jit(solution)/shard_map/ppermute | solution.py:54
  365.3 3.6 add_convert_fusion.3
  368.9 12.9 %shard_map.290 = (f32[480,2048]{1,0:T(8,128)}, bf16[480,2048]{1,0:T(8,128)(2,1)}) custom-call(bf16[960,1536]{1,0:T(8,128)(2,1)} %get-tuple-element.156.refs_0_, bf16[1536,512]{1,0:T(8,128)(2,1)} %bitcast.168, bf16[1536,512]{1,0:T(8,128)(2,1)} %collective-permute-done.27.refs_1_.refs_2_, bf16[1536,512]{1,0:T(8,128)(2,1)} %collective-permute-done.28.refs_2_.refs_3_, ...), custom_call_target="tpu_custom_call" | custom-call | flops 6039797760 | bytes 15138816 | tf_op jit(solution)/shard_map/pallas_call | solution.py:567
  381.8 3.8 convolution_convert_fusion.10
  388.8 4.1 convolution_convert_fusion.9
  396.2 2.9 convolution_convert_fusion.6
  400.6 3.0 convolution_convert_fusion.11
  414.0 3.6 add_convert_fusion.2
  417.5 50.4 %all-reduce.8.cloned.1.call-done.grad_moe = bf16[480,2048]{1,0:T(8,128)(2,1)} async-done(((bf16[480,2048]{1,0:T(8,128)(2,1)}), bf16[480,2048]{1,0:T(8,128)(2,1)}) %all-reduce.8.cloned.1.call-update) | async-done | bytes 1966096 | tf_op jit(solution)/shard_map/psum | solution.py:880
  468.0 4.1 convolution_convert_fusion.5
  473.2 3.2 convolution_convert_fusion.4
  484.2 2.2 add_convert_fusion.8
  486.5 2.3 add_convert_fusion.4
  488.7 12.5 %collective-permute-done.53 = bf16[1536,256]{1,0:T(8,128)(2,1)S(1)} collective-permute-done((bf16[1536,256]{1,0:T(8,128)(2,1)S(1)}, bf16[1536,256]{1,0:T(8,128)(2,1)S(1)}, u32[]{:S(2)}, u32[]{:S(2)}) %collective-permute-start.53) | collective-permute-done | bytes 786464 | tf_op jit(solution)/shard_map/ppermute | solution.py:44
  502.7 15.4 %collective-permute-done.52 = bf16[1536,256]{1,0:T(8,128)(2,1)S(1)} collective-permute-done((bf16[1536,256]{1,0:T(8,128)(2,1)S(1)}, bf16[1536,256]{1,0:T(8,128)(2,1)S(1)}, u32[]{:S(2)}, u32[]{:S(2)}) %collective-permute-start.52) | collective-permute-done | bytes 786464 | tf_op jit(solution)/shard_map/ppermute | solution.py:44
  522.5 8.8 %shard_map.292 = (f32[480,2048]{1,0:T(8,128)}, bf16[480,2048]{1,0:T(8,128)(2,1)}, bf16[480,16]{1,0:T(8,128)(2,1)}, f32[1,2048]{1,0:T(1,128)}) custom-call(bf16[480,2048]{1,0:T(8,128)(2,1)} %all-reduce.8.cloned.1.call-done.grad_moe, f32[480,16]{1,0:T(8,128)} %add_bitcast_fusion.gate_grads, f32[480,16]{1,0:T(8,128)} %get-tuple-element.148.gates, ...), custom_call_target="tpu_custom_call" | custom-call | flops 49152000 | bytes 13762560 | tf_op jit(solution)/shard_map/pallas_call | solution.py:648
  531.3 6.5 shard_map.293.grad
  537.8 30.1 %shard_map.294 = (bf16[480,1024]{1,0:T(8,128)(2,1)}, f32[1920,256]{1,0:T(8,128)}, f32[1,128]{1,0:T(1,128)}) custom-call(bf16[480,1280]{1,0:T(8,128)(2,1)} %get-tuple-element.125.query, bf16[1920,256]{1,0:T(8,128)(2,1)} %pad_maximum_fusion.3.keys.values, bf16[1920,256]{1,0:T(8,128)(2,1)} %pad_maximum_fusion.3.keys.values, s32[1920,2]{1,0:T(8,128)} %copy.179.key_side, ...), custom_call_target="tpu_custom_call" | custom-call | flops 9437184000 | bytes 8847360 | tf_op jit(solution)/shard_map/pallas_call | solution.py:346
  568.0 2.2 shard_map.291
  579.0 4.0 collective-permute-done.57
  587.5 8.4 %shard_map.295 = (bf16[480,2048]{1,0:T(8,128)(2,1)}, f32[1,2048]{1,0:T(1,128)}) custom-call(s32[2]{0:T(128)} %pad_add_fusion.2.scal, bf16[480,1280]{1,0:T(8,128)(2,1)} %pad_maximum_fusion.back, bf16[480,2048]{1,0:T(8,128)(2,1)} %get-tuple-element.124.hid, bf16[256,1280]{1,0:T(8,128)(2,1)} %copy-done.56, bf16[256,1280]{1,0:T(8,128)(2,1)} %collective-permute-done.2.refs_1_, ...), custom_call_target="tpu_custom_call" | custom-call | flops 2516582400 | bytes 10403840 | tf_op jit(solution)/shard_map/pallas_call | solution.py:431
  596.0 3.2 collective-permute-done.64
  600.3 4.6 maximum_add_fusion.2
  611.7 2.3 add_convert_fusion.5
  615.4 2.2 add_convert_fusion.6
  632.2 4.8 maximum_add_fusion
  637.0 4.1 shard_map.298
  642.7 4.4 convolution_convert_fusion
  647.1 4.1 shard_map.300
  652.8 3.8 convolution_convert_fusion.13
  657.3 4.7 collective-permute-done.61
  662.6 4.0 shard_map.297
  666.6 4.2 shard_map.299
  674.8 14.5 %collective-permute-done.70 = bf16[1536,256]{1,0:T(8,128)(2,1)S(1)} collective-permute-done((bf16[1536,256]{1,0:T(8,128)(2,1)}, bf16[1536,256]{1,0:T(8,128)(2,1)S(1)}, u32[]{:S(2)}, u32[]{:S(2)}) %collective-permute-start.70) | collective-permute-done | bytes 786464 | tf_op jit(solution)/shard_map/ppermute | solution.py:44
  690.7 3.0 maximum_add_fusion.1
  706.5 5.6 collective-permute-done.78
  713.5 4.2 collective-permute-done.77
  722.1 6.2 shard_map.296
  739.3 2.9 collective-permute-done.84
  742.3 2.5 collective-permute-done.85
  (527 shorter events, 204.8 us)
Async XLA Ops:
  7.2 207.6 %all-reduce.6.cloned.1.call-start = ((), (), s32[]{:S(2)}) async-start(), calls=%async_computation.1 | async-start | bytes 3932160 | tf_op jit(solution)/shard_map/psum | solution.py:861
  10.2 19.6 %collective-permute-start.2 = (bf16[256,1280]{1,0:T(8,128)(2,1)S(1)}, bf16[256,1280]{1,0:T(8,128)(2,1)}, u32[]{:S(2)}, u32[]{:S(2)}) collective-permute-start(bf16[256,1280]{1,0:T(8,128)(2,1)S(1)} %constant_dynamic-update-slice_fusion.refs_0_), channel_id=1, source_target_pairs={{0,8},{4,12},{8,0},{12,4},{1,9},{5,13},{9,1},{13,5},{2,10},{6,14},... | collective-permute-start | bytes 1966088 | tf_op jit(solution)/shard_map/ppermute | solution.py:44
  13.2 17.6 %collective-permute-start.3 = (bf16[256,1280]{1,0:T(8,128)(2,1)S(1)}, bf16[256,1280]{1,0:T(8,128)(2,1)S(1)}, u32[]{:S(2)}, u32[]{:S(2)}) collective-permute-start(bf16[256,1280]{1,0:T(8,128)(2,1)S(1)} %constant_dynamic-update-slice_fusion.refs_0_), channel_id=1, source_target_pairs={{0,16},{16,0},{1,17},{17,1},{2,18},{18,2},{3,19},{19,3},{4,20},{20... | collective-permute-start | bytes 1966088 | tf_op jit(solution)/shard_map/ppermute | solution.py:48
  18.4 23.1 %collective-permute-start.8 = (bf16[256,1280]{1,0:T(8,128)(2,1)S(1)}, bf16[256,1280]{1,0:T(8,128)(2,1)}, u32[]{:S(2)}, u32[]{:S(2)}) collective-permute-start(bf16[256,1280]{1,0:T(8,128)(2,1)S(1)} %constant_dynamic-update-slice_fusion.refs_0_), channel_id=1, source_target_pairs={{0,4},{4,0},{8,12},{12,8},{1,5},{5,1},{9,13},{13,9},{2,6},{6,2},{1... | collective-permute-start | bytes 1966088 | tf_op jit(solution)/shard_map/ppermute | solution.py:40
  30.8 16.6 %collective-permute-start.6 = (bf16[128,1280]{1,0:T(8,128)(2,1)S(1)}, bf16[128,1280]{1,0:T(8,128)(2,1)}, u32[]{:S(2)}, u32[]{:S(2)}) collective-permute-start(bf16[128,1280]{1,0:T(8,128)(2,1)S(1)} %split.160), channel_id=1, source_target_pairs={{0,16},{16,0},{1,17},{17,1},{2,18},{18,2},{3,19},{19,3},{4,20},{20... | collective-permute-start | bytes 983048 | tf_op jit(solution)/shard_map/ppermute | solution.py:48
  37.2 18.9 %collective-permute-start.14 = (bf16[1024,256]{1,0:T(8,128)(2,1)}, bf16[1024,256]{1,0:T(8,128)(2,1)}, u32[]{:S(2)}, u32[]{:S(2)}) collective-permute-start(bf16[1024,256]{1,0:T(8,128)(2,1)} %refs_0_.3), channel_id=1, source_target_pairs={{0,8},{4,12},{8,0},{12,4},{1,9},{5,13},{9,1},{13,5},{2,10},{6,14},... | collective-permute-start | bytes 1572872 | tf_op jit(solution)/shard_map/ppermute | solution.py:44
  41.0 21.6 %collective-permute-start.9 = (bf16[256,1280]{1,0:T(8,128)(2,1)}, bf16[256,1280]{1,0:T(8,128)(2,1)}, u32[]{:S(2)}, u32[]{:S(2)}) collective-permute-start(bf16[256,1280]{1,0:T(8,128)(2,1)} %collective-permute-done.2.refs_1_), channel_id=1, source_target_pairs={{0,4},{4,0},{8,12},{12,8},{1,5},{5,1},{9,13},{13,9},{2,6},{6,2},{1... | collective-permute-start | bytes 1966088 | tf_op jit(solution)/shard_map/ppermute | solution.py:40
  41.5 22.2 %collective-permute-start.10 = (bf16[256,1280]{1,0:T(8,128)(2,1)}, bf16[256,1280]{1,0:T(8,128)(2,1)}, u32[]{:S(2)}, u32[]{:S(2)}) collective-permute-start(bf16[256,1280]{1,0:T(8,128)(2,1)} %copy-done.60), channel_id=1, source_target_pairs={{0,4},{4,0},{8,12},{12,8},{1,5},{5,1},{9,13},{13,9},{2,6},{6,2},{1... | collective-permute-start | bytes 1966088 | tf_op jit(solution)/shard_map/ppermute | solution.py:40
  56.1 20.1 %collective-permute-start.15 = (bf16[1024,256]{1,0:T(8,128)(2,1)}, bf16[1024,256]{1,0:T(8,128)(2,1)}, u32[]{:S(2)}, u32[]{:S(2)}) collective-permute-start(bf16[1024,256]{1,0:T(8,128)(2,1)} %refs_0_.3), channel_id=1, source_target_pairs={{0,16},{16,0},{1,17},{17,1},{2,18},{18,2},{3,19},{19,3},{4,20},{20... | collective-permute-start | bytes 1572872 | tf_op jit(solution)/shard_map/ppermute | solution.py:48
  57.8 22.4 %collective-permute-start.26 = (bf16[8,192,256]{2,1,0:T(8,128)(2,1)}, bf16[8,192,256]{2,1,0:T(8,128)(2,1)S(1)}, u32[]{:S(2)}, u32[]{:S(2)}) collective-permute-start(bf16[8,192,256]{2,1,0:T(8,128)(2,1)} %get-tuple-element.252), channel_id=1, source_target_pairs={{0,4},{4,0},{8,12},{12,8},{1,5},{5,1},{9,13},{13,9},{2,6},{6,2},{1... | collective-permute-start | bytes 2359304 | tf_op jit(solution)/shard_map/ppermute | solution.py:40
  58.6 22.3 %collective-permute-start.29 = (bf16[8,192,256]{2,1,0:T(8,128)(2,1)}, bf16[8,192,256]{2,1,0:T(8,128)(2,1)S(1)}, u32[]{:S(2)}, u32[]{:S(2)}) collective-permute-start(bf16[8,192,256]{2,1,0:T(8,128)(2,1)} %get-tuple-element.250), channel_id=1, source_target_pairs={{0,4},{4,0},{8,12},{12,8},{1,5},{5,1},{9,13},{13,9},{2,6},{6,2},{1... | collective-permute-start | bytes 2359304 | tf_op jit(solution)/shard_map/ppermute | solution.py:40
  62.6 17.5 %collective-permute-start.18 = (bf16[1024,128]{1,0:T(8,128)(2,1)}, bf16[1024,128]{1,0:T(8,128)(2,1)}, u32[]{:S(2)}, u32[]{:S(2)}) collective-permute-start(bf16[1024,128]{1,0:T(8,128)(2,1)} %split.163), channel_id=1, source_target_pairs={{0,16},{16,0},{1,17},{17,1},{2,18},{18,2},{3,19},{19,3},{4,20},{20... | collective-permute-start | bytes 786440 | tf_op jit(solution)/shard_map/ppermute | solution.py:48
  80.1 16.0 %collective-permute-start.20 = (bf16[1024,256]{1,0:T(8,128)(2,1)}, bf16[1024,256]{1,0:T(8,128)(2,1)S(1)}, u32[]{:S(2)}, u32[]{:S(2)}) collective-permute-start(bf16[1024,256]{1,0:T(8,128)(2,1)} %refs_0_.3), channel_id=1, source_target_pairs={{0,4},{4,0},{8,12},{12,8},{1,5},{5,1},{9,13},{13,9},{2,6},{6,2},{1... | collective-permute-start | bytes 1572872 | tf_op jit(solution)/shard_map/ppermute | solution.py:40
  80.3 27.6 %collective-permute-start.21 = (bf16[1024,256]{1,0:T(8,128)(2,1)}, bf16[1024,256]{1,0:T(8,128)(2,1)}, u32[]{:S(2)}, u32[]{:S(2)}) collective-permute-start(bf16[1024,256]{1,0:T(8,128)(2,1)} %collective-permute-done.14.refs_1_), channel_id=1, source_target_pairs={{0,4},{4,0},{8,12},{12,8},{1,5},{5,1},{9,13},{13,9},{2,6},{6,2},{1... | collective-permute-start | bytes 1572872 | tf_op jit(solution)/shard_map/ppermute | solution.py:40
  80.8 16.4 %collective-permute-start.13 = (bf16[480,256]{1,0:T(8,128)(2,1)S(1)}, bf16[480,256]{1,0:T(8,128)(2,1)S(1)}, u32[]{:S(2)}, u32[]{:S(2)}) collective-permute-start(bf16[480,256]{1,0:T(8,128)(2,1)S(1)} %slice.191), channel_id=1, source_target_pairs={{0,4},{4,0},{8,12},{12,8},{1,5},{5,1},{9,13},{13,9},{2,6},{6,2},{1... | collective-permute-start | bytes 737288 | tf_op jit(solution)/shard_map/ppermute | solution.py:40
  96.2 41.3 %collective-permute-start.28 = (bf16[1536,512]{1,0:T(8,128)(2,1)S(1)}, bf16[1536,512]{1,0:T(8,128)(2,1)}, u32[]{:S(2)}, u32[]{:S(2)}) collective-permute-start(bf16[1536,512]{1,0:T(8,128)(2,1)S(1)} %bitcast.165), channel_id=1, source_target_pairs={{0,16},{16,0},{1,17},{17,1},{2,18},{18,2},{3,19},{19,3},{4,20},{20... | collective-permute-start | bytes 4718600 | tf_op jit(solution)/shard_map/ppermute | solution.py:48
  98.0 40.9 %collective-permute-start.27 = (bf16[1536,512]{1,0:T(8,128)(2,1)S(1)}, bf16[1536,512]{1,0:T(8,128)(2,1)}, u32[]{:S(2)}, u32[]{:S(2)}) collective-permute-start(bf16[1536,512]{1,0:T(8,128)(2,1)S(1)} %bitcast.166), channel_id=1, source_target_pairs={{0,8},{4,12},{8,0},{12,4},{1,9},{5,13},{9,1},{13,5},{2,10},{6,14},... | collective-permute-start | bytes 4718600 | tf_op jit(solution)/shard_map/ppermute | solution.py:44
  105.2 37.5 %collective-permute-start.25 = (bf16[480,2048]{1,0:T(8,128)(2,1)}, bf16[480,2048]{1,0:T(8,128)(2,1)}, u32[]{:S(2)}, u32[]{:S(2)}) collective-permute-start(bf16[480,2048]{1,0:T(8,128)(2,1)} %shard_map.284.own.cot), channel_id=1, source_target_pairs={{0,4},{4,0},{8,12},{12,8},{1,5},{5,1},{9,13},{13,9},{2,6},{6,2},{1... | collective-permute-start | bytes 5898248 | tf_op jit(solution)/shard_map/ppermute | solution.py:40
  105.2 19.2 %collective-permute-start.22 = (bf16[1024,256]{1,0:T(8,128)(2,1)}, bf16[1024,256]{1,0:T(8,128)(2,1)S(1)}, u32[]{:S(2)}, u32[]{:S(2)}) collective-permute-start(bf16[1024,256]{1,0:T(8,128)(2,1)} %collective-permute-done.15.refs_2_), channel_id=1, source_target_pairs={{0,4},{4,0},{8,12},{12,8},{1,5},{5,1},{9,13},{13,9},{2,6},{6,2},{1... | collective-permute-start | bytes 1572872 | tf_op jit(solution)/shard_map/ppermute | solution.py:40
  107.9 16.5 %collective-permute-start.24 = (bf16[1024,128]{1,0:T(8,128)(2,1)}, bf16[1024,128]{1,0:T(8,128)(2,1)S(1)}, u32[]{:S(2)}, u32[]{:S(2)}) collective-permute-start(bf16[1024,128]{1,0:T(8,128)(2,1)} %collective-permute-done.19.refs_4_), channel_id=1, source_target_pairs={{0,4},{4,0},{8,12},{12,8},{1,5},{5,1},{9,13},{13,9},{2,6},{6,2},{1... | collective-permute-start | bytes 786440 | tf_op jit(solution)/shard_map/ppermute | solution.py:40
  132.0 336.0 %all-reduce.8.cloned.1.call-start = ((), (), s32[]{:S(2)}) async-start(), calls=%async_computation.2 | async-start | bytes 3932160 | tf_op jit(solution)/shard_map/psum | solution.py:880
  135.1 67.7 %collective-permute-start.33 = (bf16[1536,512]{1,0:T(8,128)(2,1)}, bf16[1536,512]{1,0:T(8,128)(2,1)}, u32[]{:S(2)}, u32[]{:S(2)}) collective-permute-start(bf16[1536,512]{1,0:T(8,128)(2,1)} %bitcast.77.refs_0_.refs_2_), channel_id=1, source_target_pairs={{0,16},{16,0},{1,17},{17,1},{2,18},{18,2},{3,19},{19,3},{4,20},{20... | collective-permute-start | bytes 4718600 | tf_op jit(solution)/shard_map/ppermute | solution.py:48
  136.1 66.6 %collective-permute-start.32 = (bf16[1536,512]{1,0:T(8,128)(2,1)}, bf16[1536,512]{1,0:T(8,128)(2,1)}, u32[]{:S(2)}, u32[]{:S(2)}) collective-permute-start(bf16[1536,512]{1,0:T(8,128)(2,1)} %bitcast.77.refs_0_.refs_2_), channel_id=1, source_target_pairs={{0,8},{4,12},{8,0},{12,4},{1,9},{5,13},{9,1},{13,5},{2,10},{6,14},... | collective-permute-start | bytes 4718600 | tf_op jit(solution)/shard_map/ppermute | solution.py:44
  140.1 49.6 %collective-permute-start.31 = (bf16[1536,256]{1,0:T(8,128)(2,1)S(1)}, bf16[1536,256]{1,0:T(8,128)(2,1)S(1)}, u32[]{:S(2)}, u32[]{:S(2)}) collective-permute-start(bf16[1536,256]{1,0:T(8,128)(2,1)S(1)} %split.165), channel_id=1, source_target_pairs={{0,8},{4,12},{8,0},{12,4},{1,9},{5,13},{9,1},{13,5},{2,10},{6,14},... | collective-permute-start | bytes 2359304 | tf_op jit(solution)/shard_map/ppermute | solution.py:44
  140.8 48.9 %collective-permute-start.30 = (bf16[1536,256]{1,0:T(8,128)(2,1)S(1)}, bf16[1536,256]{1,0:T(8,128)(2,1)}, u32[]{:S(2)}, u32[]{:S(2)}) collective-permute-start(bf16[1536,256]{1,0:T(8,128)(2,1)S(1)} %split.164), channel_id=1, source_target_pairs={{0,16},{16,0},{1,17},{17,1},{2,18},{18,2},{3,19},{19,3},{4,20},{20... | collective-permute-start | bytes 2359304 | tf_op jit(solution)/shard_map/ppermute | solution.py:48
  142.7 78.4 %collective-permute-start.35 = (bf16[8,192,256]{2,1,0:T(8,128)(2,1)}, bf16[8,192,256]{2,1,0:T(8,128)(2,1)}, u32[]{:S(2)}, u32[]{:S(2)}) collective-permute-start(bf16[8,192,256]{2,1,0:T(8,128)(2,1)} %get-tuple-element.248), channel_id=1, source_target_pairs={{0,4},{4,0},{8,12},{12,8},{1,5},{5,1},{9,13},{13,9},{2,6},{6,2},{1... | collective-permute-start | bytes 2359304 | tf_op jit(solution)/shard_map/ppermute | solution.py:40
  221.1 59.3 %collective-permute-start.34 = (bf16[480,2048]{1,0:T(8,128)(2,1)}, bf16[480,2048]{1,0:T(8,128)(2,1)S(1)}, u32[]{:S(2)}, u32[]{:S(2)}) collective-permute-start(bf16[480,2048]{1,0:T(8,128)(2,1)} %get-tuple-element.190.own), channel_id=1, source_target_pairs={{0,4},{4,0},{8,12},{12,8},{1,5},{5,1},{9,13},{13,9},{2,6},{6,2},{1... | collective-permute-start | bytes 5898248 | tf_op jit(solution)/shard_map/ppermute | solution.py:40
  224.7 37.4 %collective-permute-start.40 = (bf16[1536,512]{1,0:T(8,128)(2,1)S(1)}, bf16[1536,512]{1,0:T(8,128)(2,1)}, u32[]{:S(2)}, u32[]{:S(2)}) collective-permute-start(bf16[1536,512]{1,0:T(8,128)(2,1)S(1)} %bitcast.144), channel_id=1, source_target_pairs={{0,16},{16,0},{1,17},{17,1},{2,18},{18,2},{3,19},{19,3},{4,20},{20... | collective-permute-start | bytes 4718600 | tf_op jit(solution)/shard_map/ppermute | solution.py:48
  226.3 37.3 %collective-permute-start.39 = (bf16[1536,512]{1,0:T(8,128)(2,1)S(1)}, bf16[1536,512]{1,0:T(8,128)(2,1)}, u32[]{:S(2)}, u32[]{:S(2)}) collective-permute-start(bf16[1536,512]{1,0:T(8,128)(2,1)S(1)} %bitcast.145), channel_id=1, source_target_pairs={{0,8},{4,12},{8,0},{12,4},{1,9},{5,13},{9,1},{13,5},{2,10},{6,14},... | collective-permute-start | bytes 4718600 | tf_op jit(solution)/shard_map/ppermute | solution.py:44
  231.9 48.6 %collective-permute-start.37 = (bf16[1536,256]{1,0:T(8,128)(2,1)}, bf16[1536,256]{1,0:T(8,128)(2,1)}, u32[]{:S(2)}, u32[]{:S(2)}) collective-permute-start(bf16[1536,256]{1,0:T(8,128)(2,1)} %split.167), channel_id=1, source_target_pairs={{0,8},{4,12},{8,0},{12,4},{1,9},{5,13},{9,1},{13,5},{2,10},{6,14},... | collective-permute-start | bytes 2359304 | tf_op jit(solution)/shard_map/ppermute | solution.py:44
  232.4 48.0 %collective-permute-start.36 = (bf16[1536,256]{1,0:T(8,128)(2,1)}, bf16[1536,256]{1,0:T(8,128)(2,1)}, u32[]{:S(2)}, u32[]{:S(2)}) collective-permute-start(bf16[1536,256]{1,0:T(8,128)(2,1)} %split.166), channel_id=1, source_target_pairs={{0,16},{16,0},{1,17},{17,1},{2,18},{18,2},{3,19},{19,3},{4,20},{20... | collective-permute-start | bytes 2359304 | tf_op jit(solution)/shard_map/ppermute | solution.py:48
  263.6 32.9 %collective-permute-start.42 = (bf16[1536,256]{1,0:T(8,128)(2,1)S(1)}, bf16[1536,256]{1,0:T(8,128)(2,1)S(1)}, u32[]{:S(2)}, u32[]{:S(2)}) collective-permute-start(bf16[1536,256]{1,0:T(8,128)(2,1)S(1)} %split.169), channel_id=1, source_target_pairs={{0,8},{4,12},{8,0},{12,4},{1,9},{5,13},{9,1},{13,5},{2,10},{6,14},... | collective-permute-start | bytes 2359304 | tf_op jit(solution)/shard_map/ppermute | solution.py:44
  266.3 30.2 %collective-permute-start.41 = (bf16[1536,256]{1,0:T(8,128)(2,1)S(1)}, bf16[1536,256]{1,0:T(8,128)(2,1)S(1)}, u32[]{:S(2)}, u32[]{:S(2)}) collective-permute-start(bf16[1536,256]{1,0:T(8,128)(2,1)S(1)} %split.168), channel_id=1, source_target_pairs={{0,16},{16,0},{1,17},{17,1},{2,18},{18,2},{3,19},{19,3},{4,20},{20... | collective-permute-start | bytes 2359304 | tf_op jit(solution)/shard_map/ppermute | solution.py:48
  339.0 26.2 %collective-permute-start.43 = (bf16[480,2048]{1,0:T(8,128)(2,1)}, bf16[480,2048]{1,0:T(8,128)(2,1)}, u32[]{:S(2)}, u32[]{:S(2)}) collective-permute-start(bf16[480,2048]{1,0:T(8,128)(2,1)} %get-tuple-element.155), channel_id=1, source_target_pairs={{0,4},{4,0},{8,12},{12,8},{1,5},{5,1},{9,13},{13,9},{2,6},{6,2},{1... | collective-permute-start | bytes 5898248 | tf_op jit(solution)/shard_map/ppermute | solution.py:40
  381.7 32.2 %collective-permute-start.44 = (bf16[480,2048]{1,0:T(8,128)(2,1)}, bf16[480,2048]{1,0:T(8,128)(2,1)}, u32[]{:S(2)}, u32[]{:S(2)}) collective-permute-start(bf16[480,2048]{1,0:T(8,128)(2,1)} %get-tuple-element.158), channel_id=1, source_target_pairs={{0,4},{4,0},{8,12},{12,8},{1,5},{5,1},{9,13},{13,9},{2,6},{6,2},{1... | collective-permute-start | bytes 5898248 | tf_op jit(solution)/shard_map/ppermute | solution.py:40
  386.8 92.0 %collective-permute-start.51 = (bf16[1536,256]{1,0:T(8,128)(2,1)}, bf16[1536,256]{1,0:T(8,128)(2,1)}, u32[]{:S(2)}, u32[]{:S(2)}) collective-permute-start(bf16[1536,256]{1,0:T(8,128)(2,1)} %get-tuple-element.174), channel_id=1, source_target_pairs={{0,8},{4,12},{8,0},{12,4},{1,9},{5,13},{9,1},{13,5},{2,10},{6,14},... | collective-permute-start | bytes 2359304 | tf_op jit(solution)/shard_map/ppermute | solution.py:44
  388.3 179.6 %reduce-scatter.2.cloned.1.call-start = ((), (), s32[]{:S(2)}) async-start(), calls=%async_computation.3 | async-start | bytes 2457600 | tf_op jit(solution)/shard_map/reduce_scatter | solution.py:908
  394.2 83.1 %collective-permute-start.49 = (bf16[1536,256]{1,0:T(8,128)(2,1)}, bf16[1536,256]{1,0:T(8,128)(2,1)}, u32[]{:S(2)}, u32[]{:S(2)}) collective-permute-start(bf16[1536,256]{1,0:T(8,128)(2,1)} %get-tuple-element.173), channel_id=1, source_target_pairs={{0,16},{16,0},{1,17},{17,1},{2,18},{18,2},{3,19},{19,3},{4,20},{20... | collective-permute-start | bytes 2359304 | tf_op jit(solution)/shard_map/ppermute | solution.py:48
  394.7 85.4 %collective-permute-start.55 = (bf16[1536,256]{1,0:T(8,128)(2,1)}, bf16[1536,256]{1,0:T(8,128)(2,1)}, u32[]{:S(2)}, u32[]{:S(2)}) collective-permute-start(bf16[1536,256]{1,0:T(8,128)(2,1)} %get-tuple-element.182), channel_id=1, source_target_pairs={{0,16},{16,0},{1,17},{17,1},{2,18},{18,2},{3,19},{19,3},{4,20},{20... | collective-permute-start | bytes 2359304 | tf_op jit(solution)/shard_map/ppermute | solution.py:48
  404.6 79.0 %collective-permute-start.50 = (bf16[1536,256]{1,0:T(8,128)(2,1)}, bf16[1536,256]{1,0:T(8,128)(2,1)}, u32[]{:S(2)}, u32[]{:S(2)}) collective-permute-start(bf16[1536,256]{1,0:T(8,128)(2,1)} %get-tuple-element.175), channel_id=1, source_target_pairs={{0,8},{4,12},{8,0},{12,4},{1,9},{5,13},{9,1},{13,5},{2,10},{6,14},... | collective-permute-start | bytes 2359304 | tf_op jit(solution)/shard_map/ppermute | solution.py:44
  468.0 254.2 %all-reduce.10.cloned.1.call-start = ((), (), s32[]{:S(2)}) async-start(), calls=%async_computation.5 | async-start | bytes 3932160 | tf_op jit(solution)/shard_map/psum | solution.py:934
  477.3 42.3 %collective-permute-start.66 = (bf16[1536,256]{1,0:T(8,128)(2,1)S(1)}, bf16[1536,256]{1,0:T(8,128)(2,1)S(1)}, u32[]{:S(2)}, u32[]{:S(2)}) collective-permute-start(bf16[1536,256]{1,0:T(8,128)(2,1)S(1)} %copy-done.38), channel_id=1, source_target_pairs={{0,16},{16,0},{1,17},{17,1},{2,18},{18,2},{3,19},{19,3},{4,20},{20... | collective-permute-start | bytes 2359304 | tf_op jit(solution)/shard_map/ppermute | solution.py:48
  480.2 41.8 %collective-permute-start.72 = (bf16[1536,256]{1,0:T(8,128)(2,1)S(1)}, bf16[1536,256]{1,0:T(8,128)(2,1)}, u32[]{:S(2)}, u32[]{:S(2)}) collective-permute-start(bf16[1536,256]{1,0:T(8,128)(2,1)S(1)} %add_convert_fusion.7), channel_id=1, source_target_pairs={{0,16},{16,0},{1,17},{17,1},{2,18},{18,2},{3,19},{19,3},{4,20},{20... | collective-permute-start | bytes 2359304 | tf_op jit(solution)/shard_map/ppermute | solution.py:48
  480.8 20.5 %collective-permute-start.53 = (bf16[1536,256]{1,0:T(8,128)(2,1)S(1)}, bf16[1536,256]{1,0:T(8,128)(2,1)S(1)}, u32[]{:S(2)}, u32[]{:S(2)}) collective-permute-start(bf16[1536,256]{1,0:T(8,128)(2,1)S(1)} %copy-done.39), channel_id=1, source_target_pairs={{0,8},{4,12},{8,0},{12,4},{1,9},{5,13},{9,1},{13,5},{2,10},{6,14},... | collective-permute-start | bytes 2359304 | tf_op jit(solution)/shard_map/ppermute | solution.py:44
  483.6 34.5 %collective-permute-start.52 = (bf16[1536,256]{1,0:T(8,128)(2,1)S(1)}, bf16[1536,256]{1,0:T(8,128)(2,1)S(1)}, u32[]{:S(2)}, u32[]{:S(2)}) collective-permute-start(bf16[1536,256]{1,0:T(8,128)(2,1)S(1)} %add_convert_fusion.9), channel_id=1, source_target_pairs={{0,8},{4,12},{8,0},{12,4},{1,9},{5,13},{9,1},{13,5},{2,10},{6,14},... | collective-permute-start | bytes 2359304 | tf_op jit(solution)/shard_map/ppermute | solution.py:44
  501.3 72.3 %collective-permute-start.56 = (bf16[1536,256]{1,0:T(8,128)(2,1)}, bf16[1536,256]{1,0:T(8,128)(2,1)}, u32[]{:S(2)}, u32[]{:S(2)}) collective-permute-start(bf16[1536,256]{1,0:T(8,128)(2,1)} %get-tuple-element.180), channel_id=1, source_target_pairs={{0,8},{4,12},{8,0},{12,4},{1,9},{5,13},{9,1},{13,5},{2,10},{6,14},... | collective-permute-start | bytes 2359304 | tf_op jit(solution)/shard_map/ppermute | solution.py:44
  518.1 56.0 %collective-permute-start.54 = (bf16[1536,256]{1,0:T(8,128)(2,1)}, bf16[1536,256]{1,0:T(8,128)(2,1)}, u32[]{:S(2)}, u32[]{:S(2)}) collective-permute-start(bf16[1536,256]{1,0:T(8,128)(2,1)} %split.170), channel_id=1, source_target_pairs={{0,8},{4,12},{8,0},{12,4},{1,9},{5,13},{9,1},{13,5},{2,10},{6,14},... | collective-permute-start | bytes 2359304 | tf_op jit(solution)/shard_map/ppermute | solution.py:44
  520.5 57.1 %collective-permute-start.67 = (bf16[1536,256]{1,0:T(8,128)(2,1)}, bf16[1536,256]{1,0:T(8,128)(2,1)}, u32[]{:S(2)}, u32[]{:S(2)}) collective-permute-start(bf16[1536,256]{1,0:T(8,128)(2,1)} %get-tuple-element.196), channel_id=1, source_target_pairs={{0,16},{16,0},{1,17},{17,1},{2,18},{18,2},{3,19},{19,3},{4,20},{20... | collective-permute-start | bytes 2359304 | tf_op jit(solution)/shard_map/ppermute | solution.py:48
  522.0 74.0 %collective-permute-start.74 = (bf16[1536,256]{1,0:T(8,128)(2,1)}, bf16[1536,256]{1,0:T(8,128)(2,1)}, u32[]{:S(2)}, u32[]{:S(2)}) collective-permute-start(bf16[1536,256]{1,0:T(8,128)(2,1)} %split.191), channel_id=1, source_target_pairs={{0,16},{16,0},{1,17},{17,1},{2,18},{18,2},{3,19},{19,3},{4,20},{20... | collective-permute-start | bytes 2359304 | tf_op jit(solution)/shard_map/ppermute | solution.py:48
  576.3 22.8 %collective-permute-start.64 = (bf16[1536,256]{1,0:T(8,128)(2,1)S(1)}, bf16[1536,256]{1,0:T(8,128)(2,1)}, u32[]{:S(2)}, u32[]{:S(2)}) collective-permute-start(bf16[1536,256]{1,0:T(8,128)(2,1)S(1)} %copy-done.43), channel_id=1, source_target_pairs={{0,8},{4,12},{8,0},{12,4},{1,9},{5,13},{9,1},{13,5},{2,10},{6,14},... | collective-permute-start | bytes 2359304 | tf_op jit(solution)/shard_map/ppermute | solution.py:44
  577.6 21.6 %collective-permute-start.73 = (bf16[1536,256]{1,0:T(8,128)(2,1)S(1)}, bf16[1536,256]{1,0:T(8,128)(2,1)S(1)}, u32[]{:S(2)}, u32[]{:S(2)}) collective-permute-start(bf16[1536,256]{1,0:T(8,128)(2,1)S(1)} %copy-done.40), channel_id=1, source_target_pairs={{0,16},{16,0},{1,17},{17,1},{2,18},{18,2},{3,19},{19,3},{4,20},{20... | collective-permute-start | bytes 2359304 | tf_op jit(solution)/shard_map/ppermute | solution.py:48
  600.1 128.2 %all-gather.2.cloned.1.call-start = ((), (), s32[]{:S(2)}) async-start(), calls=%async_computation.4 | async-start | bytes 2457600 | tf_op jit(solution)/shard_map/all_gather | solution.py:910
  614.0 60.8 %collective-permute-start.76 = (bf16[1536,256]{1,0:T(8,128)(2,1)}, bf16[1536,256]{1,0:T(8,128)(2,1)}, u32[]{:S(2)}, u32[]{:S(2)}) collective-permute-start(bf16[1536,256]{1,0:T(8,128)(2,1)} %split.192), channel_id=1, source_target_pairs={{0,16},{16,0},{1,17},{17,1},{2,18},{18,2},{3,19},{19,3},{4,20},{20... | collective-permute-start | bytes 2359304 | tf_op jit(solution)/shard_map/ppermute | solution.py:48
  620.9 51.7 %collective-permute-start.75 = (bf16[1536,256]{1,0:T(8,128)(2,1)}, bf16[1536,256]{1,0:T(8,128)(2,1)}, u32[]{:S(2)}, u32[]{:S(2)}) collective-permute-start(bf16[1536,256]{1,0:T(8,128)(2,1)} %add_convert_fusion.5), channel_id=1, source_target_pairs={{0,16},{16,0},{1,17},{17,1},{2,18},{18,2},{3,19},{19,3},{4,20},{20... | collective-permute-start | bytes 2359304 | tf_op jit(solution)/shard_map/ppermute | solution.py:48
  621.5 51.7 %collective-permute-start.65 = (bf16[1536,256]{1,0:T(8,128)(2,1)S(1)}, bf16[1536,256]{1,0:T(8,128)(2,1)}, u32[]{:S(2)}, u32[]{:S(2)}) collective-permute-start(bf16[1536,256]{1,0:T(8,128)(2,1)S(1)} %copy-done.37), channel_id=1, source_target_pairs={{0,8},{4,12},{8,0},{12,4},{1,9},{5,13},{9,1},{13,5},{2,10},{6,14},... | collective-permute-start | bytes 2359304 | tf_op jit(solution)/shard_map/ppermute | solution.py:44
  670.9 18.5 %collective-permute-start.70 = (bf16[1536,256]{1,0:T(8,128)(2,1)}, bf16[1536,256]{1,0:T(8,128)(2,1)S(1)}, u32[]{:S(2)}, u32[]{:S(2)}) collective-permute-start(bf16[1536,256]{1,0:T(8,128)(2,1)} %add_convert_fusion.6), channel_id=1, source_target_pairs={{0,8},{4,12},{8,0},{12,4},{1,9},{5,13},{9,1},{13,5},{2,10},{6,14},... | collective-permute-start | bytes 2359304 | tf_op jit(solution)/shard_map/ppermute | solution.py:44
  671.5 23.0 %collective-permute-start.87 = (bf16[8,192,256]{2,1,0:T(8,128)(2,1)S(1)}, bf16[8,192,256]{2,1,0:T(8,128)(2,1)S(1)}, u32[]{:S(2)}, u32[]{:S(2)}) collective-permute-start(bf16[8,192,256]{2,1,0:T(8,128)(2,1)S(1)} %dynamic-slice_convert_fusion.2), channel_id=1, source_target_pairs={{0,4},{4,0},{8,12},{12,8},{1,5},{5,1},{9,13},{13,9},{2,6},{6,2},{1... | collective-permute-start | bytes 2359304 | tf_op jit(solution)/shard_map/ppermute | solution.py:40
  672.7 24.3 %collective-permute-start.63 = (bf16[1024,1280]{1,0:T(8,128)(2,1)}, bf16[1024,1280]{1,0:T(8,128)(2,1)S(1)}, u32[]{:S(2)}, u32[]{:S(2)}) collective-permute-start(bf16[1024,1280]{1,0:T(8,128)(2,1)} %convolution_convert_fusion), channel_id=1, source_target_pairs={{0,4},{4,0},{8,12},{12,8},{1,5},{5,1},{9,13},{13,9},{2,6},{6,2},{1... | collective-permute-start | bytes 7864328 | tf_op jit(solution)/shard_map/ppermute | solution.py:40
  673.2 28.8 %collective-permute-start.69 = (bf16[1024,1024]{1,0:T(8,128)(2,1)}, bf16[1024,1024]{1,0:T(8,128)(2,1)S(1)}, u32[]{:S(2)}, u32[]{:S(2)}) collective-permute-start(bf16[1024,1024]{1,0:T(8,128)(2,1)} %convolution_convert_fusion.13), channel_id=1, source_target_pairs={{0,4},{4,0},{8,12},{12,8},{1,5},{5,1},{9,13},{13,9},{2,6},{6,2},{1... | collective-permute-start | bytes 6291464 | tf_op jit(solution)/shard_map/ppermute | solution.py:40
  704.3 15.6 %collective-permute-start.80 = (bf16[512,256]{1,0:T(8,128)(2,1)S(1)}, bf16[512,256]{1,0:T(8,128)(2,1)S(1)}, u32[]{:S(2)}, u32[]{:S(2)}) collective-permute-start(bf16[512,256]{1,0:T(8,128)(2,1)S(1)} %get-tuple-element.202), channel_id=1, source_target_pairs={{0,8},{4,12},{8,0},{12,4},{1,9},{5,13},{9,1},{13,5},{2,10},{6,14},... | collective-permute-start | bytes 786440 | tf_op jit(solution)/shard_map/ppermute | solution.py:44
  712.1 17.5 %collective-permute-start.82 = (bf16[128,1280]{1,0:T(8,128)(2,1)S(1)}, bf16[128,1280]{1,0:T(8,128)(2,1)}, u32[]{:S(2)}, u32[]{:S(2)}) collective-permute-start(bf16[128,1280]{1,0:T(8,128)(2,1)S(1)} %get-tuple-element.211), channel_id=1, source_target_pairs={{0,16},{16,0},{1,17},{17,1},{2,18},{18,2},{3,19},{19,3},{4,20},{20... | collective-permute-start | bytes 983048 | tf_op jit(solution)/shard_map/ppermute | solution.py:48
  717.7 13.9 %collective-permute-start.79 = (bf16[128,1280]{1,0:T(8,128)(2,1)}, bf16[128,1280]{1,0:T(8,128)(2,1)}, u32[]{:S(2)}, u32[]{:S(2)}) collective-permute-start(bf16[128,1280]{1,0:T(8,128)(2,1)} %get-tuple-element.212), channel_id=1, source_target_pairs={{0,16},{16,0},{1,17},{17,1},{2,18},{18,2},{3,19},{19,3},{4,20},{20... | collective-permute-start | bytes 983048 | tf_op jit(solution)/shard_map/ppermute | solution.py:48
  719.9 14.0 %collective-permute-start.81 = (bf16[128,1280]{1,0:T(8,128)(2,1)}, bf16[128,1280]{1,0:T(8,128)(2,1)}, u32[]{:S(2)}, u32[]{:S(2)}) collective-permute-start(bf16[128,1280]{1,0:T(8,128)(2,1)} %get-tuple-element.213), channel_id=1, source_target_pairs={{0,8},{4,12},{8,0},{12,4},{1,9},{5,13},{9,1},{13,5},{2,10},{6,14},... | collective-permute-start | bytes 983048 | tf_op jit(solution)/shard_map/ppermute | solution.py:44
  729.6 15.3 %collective-permute-start.86 = (bf16[512,256]{1,0:T(8,128)(2,1)}, bf16[512,256]{1,0:T(8,128)(2,1)S(1)}, u32[]{:S(2)}, u32[]{:S(2)}) collective-permute-start(bf16[512,256]{1,0:T(8,128)(2,1)} %get-tuple-element.215), channel_id=1, source_target_pairs={{0,16},{16,0},{1,17},{17,1},{2,18},{18,2},{3,19},{19,3},{4,20},{20... | collective-permute-start | bytes 786440 | tf_op jit(solution)/shard_map/ppermute | solution.py:48
  (116 other events, 812.4 us)
Sparse Core Ops, SparseCore 0:
  132.1 82.6 all-reduce.5
  388.4 79.4 all-reduce.7
  470.3 40.4 reduce-scatter.1
  600.2 81.0 all-reduce.9
  682.7 42.5 all-gather.1

commit v2 on v1

v2 whole, which is shorter than its diff:
```python
import functools
import math

import jax
import jax.numpy as jnp
from jax import lax
from jax.experimental import pallas as pl
from jax.experimental.pallas import tpu as pltpu
from jax.sharding import PartitionSpec as P

HEADS_Q = 32
HEADS_KV = 4
HEAD = 128
TOP = 8
EXPERTS = 16

EPS = 1e-06
THETA = 1000000.0
LOG2E = 1.4426950408889634
HIDE = -1e30

F32 = jnp.float32
BF16 = jnp.bfloat16
VMEM_BYTES = 58 * 1024 * 1024


def rounded(v):
    return v.astype(BF16)


def dot(a, b, contract):
    return lax.dot_general(a, b, ((contract[:1], contract[1:]), ((), ())), preferred_element_type=F32)


def after(value, *others):
    return lax.optimization_barrier((value,) + others)[0]


def to_core(v):
    return lax.ppermute(v, "ctx", [(i, i ^ 1) for i in range(4)])


def to_x(v):
    return lax.ppermute(v, "ctx", [(i, i ^ 2) for i in range(4)])


def to_dp(v):
    return lax.ppermute(v, "dp", [(0, 1), (1, 0)])


def exchange(x_value, y_value, *gate):
    x_value, y_value = after((x_value, y_value), *gate) if gate else lax.optimization_barrier((x_value, y_value))
    return lax.optimization_barrier((to_x(x_value), to_dp(y_value)))


def sum_z(v):
    size = lax.axis_size("tensor")
    one, two, three = (lax.ppermute(v, "tensor", [(i, i ^ k) for i in range(size)]) for k in (1, 2, 3))
    return (v + one) + (two + three)


def place():
    ctx = lax.axis_index("ctx")
    return lax.axis_index("dp"), ctx // 2, ctx % 2


def flips():
    dp, x, _ = place()
    return x + 2 * dp if lax.axis_size("dp") == 2 else x


def flip(v, axis, bit):
    return jnp.where(bit == 0, v, jnp.flip(v, axis))


def relative(v):
    dp, x, _ = place()
    count = lax.axis_size("dp")
    cut = v.reshape(v.shape[:-1] + (count, 2, v.shape[-1] // (2 * count)))
    cut = flip(cut, cut.ndim - 2, x)
    if count == 2:
        cut = flip(cut, cut.ndim - 3, dp)
    return cut.reshape(v.shape)


def halves(v, axis):
    return jnp.split(v, 2, axis)


def gather_whole(block, axis):
    pair = jnp.concatenate([block, to_x(block)], axis)
    return lax.all_gather(pair, "dp", axis=axis, tiled=True)


def scatter_whole(blocks):
    kept = jnp.stack(blocks[0::2]).astype(F32) + to_x(jnp.stack(blocks[1::2])).astype(F32)
    return lax.psum_scatter(rounded(kept), "dp", scatter_dimension=0, tiled=False).astype(F32)


def whole(array):
    dims = len(array.shape)
    return pl.BlockSpec(array.shape, lambda *_: (0,) * dims)


SCALARS = pl.BlockSpec(memory_space=pltpu.SMEM)


TIMES = {
    "permute_kernel": 4.6, "half_kernel": 4, "block_kernel": 6, "qkv_kernel": 11.7,
    "attend_kernel": 16.3, "attend_back_kernel": 30, "project_kernel": 6.6, "project_back_kernel": 6.5,
    "kv_pass_kernel": 2, "qkv_back_kernel": 9.8, "products_kernel": 11.8, "experts_kernel": 20,
    "spread_kernel": 10, "join_kernel": 4.6, "weight_grad_kernel": 50, "met_kernel": 0.5, "total_kernel": 0.5,
    "lay_kernel": 0.5, "pair_grad_kernel": 0.5, "columns_grad_kernel": 0.5, "cut_kernel": 0.3, "end_kernel": 0.3,
    "route_kernel": 6.3, "route_back_kernel": 8.6, "add_kernel": 2.2, "last_kernel": 6.2,
}


def cost(body):
    name = getattr(body, "func", body).__name__
    return pl.CostEstimate(flops=int(TIMES.get(name, 0.3) * 1e9), bytes_accessed=0, transcendentals=0)


def kernel_call(body, grid, in_specs, out_specs, out_shape, flops, moved, scratch=()):
    return pl.pallas_call(
        body,
        grid=grid,
        in_specs=in_specs,
        out_specs=out_specs,
        out_shape=out_shape,
        scratch_shapes=list(scratch),
        compiler_params=pltpu.CompilerParams(vmem_limit_bytes=VMEM_BYTES),
        cost_estimate=cost(body),
    )


def sds(shape, dtype):
    return jax.ShapeDtypeStruct(shape, dtype)


def piece_starts(scal, places, shard):
    core = scal[1]
    shift = {0: 0, 1: core * shard, 2: (1 - core) * shard}
    return [
        (start if kind == 0 else pl.multiple_of(start + shift[kind], length), length)
        for start, length, kind in places
    ]


def kernel_inverse_rms(v):
    return lax.rsqrt(jnp.mean(v * v, axis=-1, keepdims=True) + EPS)


def permute_kernel(scal, in_ref, out_ref):
    out_ref[...] = in_ref[...]


def permute_width(v, scal, blocks):
    rows, width = v.shape
    span = width // blocks
    return pl.pallas_call(
        permute_kernel,
        grid_spec=pltpu.PrefetchScalarGridSpec(
            num_scalar_prefetch=1,
            grid=(blocks,),
            in_specs=[pl.BlockSpec((rows, span), lambda j, s: (0, j ^ s[0]))],
            out_specs=pl.BlockSpec((rows, span), lambda j, s: (0, j)),
        ),
        out_shape=sds(v.shape, v.dtype),
        cost_estimate=cost(permute_kernel),
    )(scal, v)


def pick_columns(v, scal, shard, other):
    rows, width = v.shape
    count = width // (2 * shard)
    which = 1 - scal[1] if other else scal[1]
    cut = v.reshape(rows, count, 2, shard)
    return lax.dynamic_index_in_dim(cut, which, 2, keepdims=False).reshape(rows, count * shard)


def prefetch_call(body, scal, grid, in_specs, out_specs, out_shape, arrays, scratch=()):
    return pl.pallas_call(
        body,
        grid_spec=pltpu.PrefetchScalarGridSpec(
            num_scalar_prefetch=1,
            grid=grid,
            in_specs=in_specs,
            out_specs=out_specs,
            scratch_shapes=list(scratch),
        ),
        out_shape=out_shape,
        compiler_params=pltpu.CompilerParams(vmem_limit_bytes=VMEM_BYTES),
        cost_estimate=cost(body),
    )(scal, *arrays)


def half_kernel(scal, *refs):
    ins, out = refs[:3], refs[3]
    for m in range(3):

        @pl.when(pl.program_id(0) == m)
        def _():
            out[0] = ins[m][...]


def other_half_call(scal, weights):
    experts, hid, shard = weights[0].shape
    half = experts // 2
    return prefetch_call(
        half_kernel,
        scal,
        (3,),
        [pl.BlockSpec((half, hid, shard), lambda m, s: (1 - s[1], 0, 0))] * 3,
        pl.BlockSpec((1, half, hid, shard), lambda m, s: (m, 0, 0, 0)),
        sds((3, half, hid, shard), BF16),
        weights,
    )


def block_kernel(scal, *refs):
    ins, got, out = refs[:3], refs[3], refs[4]
    shard = got.shape[3]
    rows = out.shape[0]
    other = pl.ds(pl.multiple_of((1 - scal[1]) * shard, shard), shard)
    out[:, other] = got[0].reshape(rows, shard)
    for m in range(3):

        @pl.when(pl.program_id(0) == m)
        def _():
            out[:, pl.ds(pl.multiple_of(scal[1] * shard, shard), shard)] = ins[m][...].reshape(rows, shard)


def block_call(scal, weights, got):
    experts, hid, shard = weights[0].shape
    half = experts // 2
    return prefetch_call(
        block_kernel,
        scal,
        (3,),
        [pl.BlockSpec((half, hid, shard), lambda m, s: (s[1], 0, 0))] * 3
        + [pl.BlockSpec((1, half, hid, shard), lambda m, s: (m, 0, 0, 0))],
        pl.BlockSpec((half * hid, 2 * shard), lambda m, s: (m, 0)),
        sds((3 * half * hid, 2 * shard), BF16),
        [*weights, got],
    )


def read_small(places, shard, per, scal, pieces, gain_one, gain_two, router_t, gain_q, gain_k):
    gain_q[...] = jnp.zeros(gain_q.shape, F32)
    gain_k[...] = jnp.zeros(gain_k.shape, F32)
    lane = lax.broadcasted_iota(jnp.int32, (shard // 2, HEAD), 0)
    target = lax.broadcasted_iota(jnp.int32, (shard // 2, HEAD), 1)
    for (start, length), (fixed, _, kind), ref in zip(piece_starts(scal, places, shard), places, pieces):
        value = ref[...].astype(F32).T
        lanes = pl.ds(start, length)
        router_t[:, lanes] = rounded(value[:EXPERTS])
        gain_one[:, lanes] = value[EXPERTS : EXPERTS + 1]
        gain_two[:, lanes] = value[EXPERTS + 1 : EXPERTS + 2]
        if fixed % shard:
            continue
        half = scal[1] if kind == 1 else 1 - scal[1]
        heads = rounded(value[EXPERTS + 2 : EXPERTS + 3, : shard // 2])
        first = (2 * ((fixed // (2 * shard)) ^ scal[0]) + half) * per
        in_q = (target == first + lane) & (lane < per)
        in_k = (target == first + lane - per) & (lane >= per) & (lane < 2 * per)
        gain_q[...] += dot(heads, jnp.where(in_q, 1.0, 0.0).astype(BF16), (1, 0))
        gain_k[...] += dot(heads, jnp.where(in_k, 1.0, 0.0).astype(BF16), (1, 0))


def qkv_kernel(places, shard, per, blocks, given, scal, hid, cos, sin, *refs):
    n = len(places)
    weights, refs = refs[:n], refs[n:]
    if given:
        gain, gain_q, gain_k, normed, hid_rel, raw, rot = refs
    else:
        smalls, (gain, gain_two, router_t, gain_q, gain_k, normed, hid_rel, raw, rot) = refs[:n], refs[n:]
    step, last = pl.program_id(0), pl.num_programs(0) - 1
    width = hid.shape[1]
    span = width // blocks

    @pl.when(step == 0)
    def _():
        if not given:
            read_small(places, shard, per, scal, smalls, gain, gain_two, router_t, gain_q, gain_k)
        for j in range(blocks):
            source = pl.multiple_of((scal[0] ^ j) * span, span)
            hid_rel[:, j * span : (j + 1) * span] = hid[:, pl.ds(source, span)]
        tokens = hid_rel[...].astype(F32)
        normed[...] = rounded(tokens * kernel_inverse_rms(tokens) * gain[...])

    total = jnp.zeros(raw.shape, F32)
    for (start, length), weight in zip(piece_starts(scal, places, shard), weights):
        total += dot(normed[:, pl.ds(start, length)], weight[...], (1, 0))
    raw[...] = total
    vector = jnp.where(step == last, gain_k[...], gain_q[...])
    for head in range(2):
        cut = total[:, head * HEAD : (head + 1) * HEAD]
        scaled = cut * kernel_inverse_rms(cut) * vector
        turned = scaled * cos[...] + pltpu.roll(scaled, HEAD // 2, 1) * sin[...]
        if head == 1:
            turned = jnp.where(step == last, cut, turned)
        rot[:, head * HEAD : (head + 1) * HEAD] = rounded(turned)


def qkv_call(scal, hid, gains, cos, sin, pieces, places, shard, per, blocks, columns):
    rows, width = hid.shape
    pair = 2 * HEAD
    block = pl.BlockSpec((rows, pair), lambda i: (0, i))
    weights = [pl.BlockSpec((p.shape[0], pair), lambda i: (0, i)) for p in pieces]
    outs = [sds(hid.shape, BF16), sds(hid.shape, BF16), sds((rows, columns), F32), sds((rows, columns), BF16)]
    specs = [whole(hid), whole(hid), block, block]
    if gains:
        more, more_specs = list(gains), [whole(g) for g in gains]
    else:
        more = pieces
        more_specs = [pl.BlockSpec((p.shape[0], HEAD), lambda i: (0, columns // HEAD)) for p in pieces]
        found = [
            sds((1, width), F32),
            sds((1, width), F32),
            sds((EXPERTS, width), BF16),
            sds((1, HEAD), F32),
            sds((1, HEAD), F32),
        ]
        outs, specs = found + outs, [whole(v) for v in found] + specs
    return kernel_call(
        functools.partial(qkv_kernel, places, shard, per, blocks, bool(gains)),
        (columns // pair,),
        [SCALARS, whole(hid), whole(cos), whole(sin)] + weights + more_specs,
        specs,
        outs,
        0,
        0,
    )(scal, hid, cos, sin, *pieces, *more)


def write_bias(bias, key_side, query_side):
    seg = key_side[:, 0:1]
    seen = (seg == query_side[0:1]) | (seg == query_side[1:2]) | (seg == query_side[2:3])
    seen = seen & (key_side[:, 1:2] <= query_side[3:4])
    bias[...] = jnp.where(seen, 0.0, HIDE)


def key_tiles(count):
    tile = next(t for t in (384, 320, 256, 128) if count % t == 0)
    return [(s, tile) for s in range(0, count, tile)]


def attend_kernel(query, keys, values, key_side, query_side, mixed, inverse, bias, values_t):
    @pl.when(pl.program_id(0) == 0)
    def _():
        write_bias(bias, key_side[...], query_side[...])
        values_t[...] = values[...].T

    rows = query.shape[0]
    total = jnp.zeros((HEAD, rows), F32)
    row_sum = jnp.zeros((1, rows), F32)
    factor = LOG2E * HEAD**-0.5
    for start, tile in key_tiles(keys.shape[0]):
        raw = dot(keys[start : start + tile], query[...], (1, 1))
        weight = jnp.exp2(raw * factor + bias[start : start + tile])
        row_sum += jnp.sum(weight, 0, keepdims=True)
        total += dot(values_t[:, start : start + tile], rounded(weight), (1, 0))
    scale = 1.0 / row_sum
    mixed[...] = rounded((total * scale).T)
    inverse[0] = scale


def attend_call(rot, kv_all, key_side, query_side, heads):
    rows, count = rot.shape[0], kv_all.shape[0]
    column = pl.BlockSpec((rows, HEAD), lambda h: (0, h))
    return kernel_call(
        attend_kernel,
        (heads,),
        [
            column,
            pl.BlockSpec((count, HEAD), lambda h: (0, 0)),
            pl.BlockSpec((count, HEAD), lambda h: (0, 1)),
            whole(key_side),
            whole(query_side),
        ],
        [column, pl.BlockSpec((1, 1, rows), lambda h: (h, 0, 0))],
        [sds((rows, heads * HEAD), BF16), sds((heads, 1, rows), F32)],
        4 * heads * rows * count * HEAD,
        4 * rows * heads * HEAD + 4 * count * HEAD,
        [pltpu.VMEM((count, rows), F32), pltpu.VMEM((HEAD, count), BF16)],
    )(rot, kv_all, kv_all, key_side, query_side)


def attend_back_kernel(
    query, keys, values, key_side, query_side, grad, mixed, inverse, raw_query, cos, sin, gain,
    query_back, kv_own, kv_sent, kv_mid, grad_gain, bias, keys_t, grad_kv,
):
    @pl.when(pl.program_id(0) == 0)
    def _():
        write_bias(bias, key_side[...], query_side[...])
        keys_t[...] = keys[...].T
        grad_kv[...] = jnp.zeros(grad_kv.shape, F32)
        grad_gain[...] = jnp.zeros(grad_gain.shape, F32)

    rows = query.shape[0]
    scale = HEAD**-0.5
    factor = LOG2E * scale
    both = grad[...].astype(F32) * mixed[...].astype(F32)
    mean = jnp.sum(both.T, 0, keepdims=True)
    norm = inverse[0]
    total = jnp.zeros((HEAD, rows), F32)
    for start, tile in key_tiles(keys.shape[0]):
        span = slice(start, start + tile)
        raw = dot(keys[span], query[...], (1, 1))
        prob = jnp.exp2(raw * factor + bias[span]) * norm
        grad_prob = dot(values[span], grad[...], (1, 1))
        grad_raw = rounded(prob * (grad_prob - mean) * scale)
        total += dot(keys_t[:, span], grad_raw, (1, 0))
        grad_kv[span, :HEAD] += dot(grad_raw, query[...], (1, 0))
        grad_kv[span, HEAD:] += dot(rounded(prob), grad[...], (1, 0))
    turned = total.T
    turned = turned * cos[...] - pltpu.roll(turned, HEAD // 2, 1) * sin[...]
    value = raw_query[...]
    shrink = kernel_inverse_rms(value)
    normal = value * shrink
    grad_gain[...] += jnp.sum(turned * normal, 0, keepdims=True)
    scaled = turned * gain[...]
    middle = jnp.mean(scaled * normal, axis=-1, keepdims=True)
    query_back[...] = rounded(shrink * (scaled - normal * middle))

    @pl.when(pl.program_id(0) == pl.num_programs(0) - 1)
    def _():
        kv_own[...] = grad_kv[:rows]
        kv_sent[:rows] = rounded(grad_kv[rows : 2 * rows])
        kv_mid[...] = grad_kv[2 * rows : 3 * rows]
        kv_sent[rows:] = rounded(grad_kv[3 * rows :])


def attend_back_call(rot, kv_all, key_side, query_side, grad, mixed, inverse, raw, cos, sin, gain, heads):
    rows, count = rot.shape[0], kv_all.shape[0]
    column = pl.BlockSpec((rows, HEAD), lambda h: (0, h))
    return kernel_call(
        attend_back_kernel,
        (heads,),
        [
            column,
            pl.BlockSpec((count, HEAD), lambda h: (0, 0)),
            pl.BlockSpec((count, HEAD), lambda h: (0, 1)),
            whole(key_side),
            whole(query_side),
            column,
            column,
            pl.BlockSpec((1, 1, rows), lambda h: (h, 0, 0)),
            column,
            whole(cos),
            whole(sin),
            whole(gain),
        ],
        [
            column,
            pl.BlockSpec((rows, 2 * HEAD), lambda h: (0, 0)),
            pl.BlockSpec((2 * rows, 2 * HEAD), lambda h: (0, 0)),
            pl.BlockSpec((rows, 2 * HEAD), lambda h: (0, 0)),
            pl.BlockSpec((1, HEAD), lambda h: (0, 0)),
        ],
        [
            sds((rows, heads * HEAD), BF16),
            sds((rows, 2 * HEAD), F32),
            sds((2 * rows, 2 * HEAD), BF16),
            sds((rows, 2 * HEAD), F32),
            sds((1, HEAD), F32),
        ],
        10 * heads * rows * count * HEAD,
        12 * rows * heads * HEAD + 12 * count * HEAD,
        [
            pltpu.VMEM((count, rows), F32),
            pltpu.VMEM((HEAD, count), BF16),
            pltpu.VMEM((count, 2 * HEAD), F32),
        ],
    )(rot, kv_all, kv_all, key_side, query_side, grad, mixed, inverse, raw, cos, sin, gain)


def project_kernel(places, shard, scal, mixed, *refs):
    out = refs[-1]
    for (start, length), weight in zip(piece_starts(scal, places, shard), refs[:-1]):
        out[:, pl.ds(start, length)] = rounded(dot(mixed[...], weight[...], (1, 0)))


def project_call(scal, mixed, pieces, places, shard, width):
    rows, inner = mixed.shape
    return kernel_call(
        functools.partial(project_kernel, places, shard),
        (1,),
        [SCALARS, whole(mixed)] + [whole(p) for p in pieces],
        pl.BlockSpec((rows, width), lambda i: (0, 0)),
        sds((rows, width), BF16),
        2 * rows * inner * width,
        2 * inner * width + 2 * rows * (inner + width),
    )(scal, mixed, *pieces)


def project_back_kernel(places, shard, scal, grad, *refs):
    out = refs[-1]
    total = jnp.zeros(out.shape, F32)
    for (start, length), weight in zip(piece_starts(scal, places, shard), refs[:-1]):
        total += dot(grad[:, pl.ds(start, length)], weight[...], (1, 1))
    out[...] = rounded(total)


def project_back_call(scal, grad, pieces, places, shard, inner):
    rows, width = grad.shape
    tile = inner // 2
    return kernel_call(
        functools.partial(project_back_kernel, places, shard),
        (2,),
        [SCALARS, whole(grad)] + [pl.BlockSpec((tile, p.shape[1]), lambda i: (i, 0)) for p in pieces],
        pl.BlockSpec((rows, tile), lambda i: (0, i)),
        sds((rows, inner), BF16),
        2 * rows * inner * width,
        2 * inner * width + 2 * rows * (inner + width),
    )(scal, grad, *pieces)


def kv_pass_kernel(own, mid, got, part, sent):
    rows = own.shape[0]
    part[...] = own[...] + got[:rows].astype(F32)
    sent[...] = rounded(mid[...] + got[rows:].astype(F32))


def kv_pass_call(own, mid, got):
    return kernel_call(
        kv_pass_kernel,
        (1,),
        [whole(own), whole(mid), whole(got)],
        [whole(own), whole(own)],
        [sds(own.shape, F32), sds(own.shape, BF16)],
        0,
        0,
    )(own, mid, got)


def qkv_back_kernel(
    places, shard, scal, query_back, kv_part, kv_far, raw_key, cos, sin, gain_k, hid, *refs
):
    weights, (part, grad_gain, kv_back, grad_gain_k) = refs[: len(places)], refs[len(places) :]
    inner = query_back.shape[1]
    total = kv_part[...] + kv_far[...].astype(F32)
    turned = total[:, :HEAD]
    turned = turned * cos[...] - pltpu.roll(turned, HEAD // 2, 1) * sin[...]
    value = raw_key[...]
    shrink = kernel_inverse_rms(value)
    normal = value * shrink
    grad_gain_k[...] = jnp.sum(turned * normal, 0, keepdims=True)
    scaled = turned * gain_k[...]
    middle = jnp.mean(scaled * normal, axis=-1, keepdims=True)
    kv_back[:, :HEAD] = rounded(shrink * (scaled - normal * middle))
    kv_back[:, HEAD:] = rounded(total[:, HEAD:])

    tokens = hid[...].astype(F32)
    shrink = kernel_inverse_rms(tokens)
    for (start, length), weight in zip(piece_starts(scal, places, shard), weights):
        lanes = pl.ds(start, length)
        value = dot(query_back[...], weight[:, :inner], (1, 1))
        value += dot(kv_back[...], weight[:, inner : inner + 2 * HEAD], (1, 1))
        part[:, lanes] = rounded(value)
        normal = hid[:, lanes].astype(F32) * shrink
        grad_gain[:, lanes] = jnp.sum(value * normal, 0, keepdims=True)


def qkv_back_call(scal, query_back, kv_part, kv_far, raw, cos, sin, gain_k, hid, pieces, places, shard):
    rows, width = hid.shape
    inner = query_back.shape[1]
    arrays = (cos, sin, gain_k, hid)
    outs = [sds((rows, width), BF16), sds((1, width), F32), sds((rows, 2 * HEAD), BF16), sds((1, HEAD), F32)]
    return kernel_call(
        functools.partial(qkv_back_kernel, places, shard),
        (1,),
        [SCALARS, whole(query_back), whole(kv_part), whole(kv_far)]
        + [pl.BlockSpec((rows, HEAD), lambda i: (0, inner // HEAD))]
        + [whole(a) for a in arrays]
        + [whole(p) for p in pieces],
        [whole(o) for o in outs],
        outs,
        0,
        0,
    )(scal, query_back, kv_part, kv_far, raw, *arrays, *pieces)


def join_rows(own, other, scratch):
    rows = own.shape[0]

    @pl.when(pl.program_id(0) == 0)
    def _():
        scratch[:rows] = own[...]
        scratch[rows:] = other[...]


def product(weights, rows_ref):
    return dot(jnp.concatenate([w[...] for w in weights], 1), rows_ref[...], (1, 1))


def single(shape):
    dims = len(shape)
    return pl.BlockSpec(shape, lambda *_: (0,) * dims, pipeline_mode=pl.Buffered(1))


def products_kernel(own, other, *refs):
    weights, (out, both, pair) = refs[:-3], refs[-3:]
    join_rows(own, other, both)
    out[...] = product(weights, both)

    @pl.when(pl.program_id(0) == 0)
    def _():
        pair[...] = both[...]


def row_pieces(pieces, tile, hidden):
    step = hidden // tile
    return [pl.BlockSpec((tile, a.shape[1]), lambda i, m=m: (i + m * step, 0)) for a, m in pieces]


def products_call(own, other, pieces, hidden):
    rows, width = own.shape
    tile = hidden // 4
    return kernel_call(
        products_kernel,
        (4,),
        [single(own.shape), single(own.shape)] + row_pieces(pieces, tile, hidden),
        [pl.BlockSpec((tile, 2 * rows), lambda i: (i, 0)), single((2 * rows, width))],
        [sds((hidden, 2 * rows), F32), sds((2 * rows, width), BF16)],
        0,
        0,
        [pltpu.VMEM((2 * rows, width), BF16)],
    )(own, other, *[a for a, _ in pieces])


def experts_kernel(hid, both, gate_ref, grad_act, gates, *refs):
    weights, (acts, acts_t, gate_part) = refs[:-3], refs[-3:]
    gate_pre, up_pre = gate_ref[...], product(weights, both)
    sig = 1.0 / (1.0 + jnp.exp(-gate_pre))
    silu = gate_pre * sig
    act = silu * up_pre
    slope = sig * (1.0 + gate_pre * (1.0 - sig))
    count = gates.shape[0]
    for e in range(count):
        rows = slice(e * hid, (e + 1) * hid)
        gate = gates[e]
        raw = grad_act[rows, :]
        back = gate * raw
        acts[0, rows, :] = rounded(gate * act[rows])
        acts[1, rows, :] = rounded(back * up_pre[rows] * slope[rows])
        acts[2, rows, :] = rounded(back * silu[rows])
        gate_part[e] = jnp.sum(act[rows] * raw, 0, keepdims=True)
    for k in range(3):
        acts_t[k] = acts[k].T


def experts_call(pair, gate_pre, grad_act, gates, pieces, hid):
    both, width = pair.shape
    experts = gates.shape[0]
    per = 2
    tile = per * hid
    hidden = experts * hid
    act = pl.BlockSpec((tile, both), lambda i: (i, 0))
    gate = pl.BlockSpec((per, 1, both), lambda i: (i, 0, 0))
    return kernel_call(
        functools.partial(experts_kernel, hid),
        (experts // per,),
        [single(pair.shape), act, act, gate] + row_pieces(pieces, tile, hidden),
        [
            pl.BlockSpec((3, tile, both), lambda i: (0, i, 0)),
            pl.BlockSpec((3, both, tile), lambda i: (0, 0, i)),
            gate,
        ],
        [sds((3, hidden, both), BF16), sds((3, both, hidden), BF16), sds((experts, 1, both), F32)],
        0,
        0,
    )(pair, gate_pre, grad_act, gates, *[a for a, _ in pieces])


def gate_sum_kernel(first, second, third, fourth, own, sent):
    rows = own.shape[1]
    for e in range(own.shape[0]):
        total = (first[e] + second[e]) + (third[e] + fourth[e])
        own[e : e + 1] = total[:, :rows]
        sent[e : e + 1] = total[:, rows:]


def gate_sum_call(part):
    size = lax.axis_size("tensor")
    there = [lax.ppermute(part, "tensor", [(i, i ^ k) for i in range(size)]) for k in (1, 2, 3)]
    out = sds((part.shape[0], part.shape[2] // 2), F32)
    own, sent = kernel_call(
        gate_sum_kernel, (1,), [whole(part)] * 4, [whole(out)] * 2, [out, out], 0, 0
    )(part, *there)
    return own, to_core(sent)


def gate_join_kernel(scal, own, got, out):
    first = jnp.where(scal[1] == 0, own[...], got[...])
    second = jnp.where(scal[1] == 0, got[...], own[...])
    out[...] = jnp.concatenate([first, second]).T


def gate_join_call(scal, own, got):
    out = sds((own.shape[1], 2 * own.shape[0]), F32)
    return kernel_call(gate_join_kernel, (1,), [SCALARS, whole(own), whole(got)], whole(out), out, 0, 0)(
        scal, own, got
    )


def backward_tiles(places, tile):
    return [(p, k) for p, (_, length, _) in enumerate(places) for k in range(length // tile)]


def spread_kernel(tiles, terms, joined, *refs):
    acts, out = refs[:terms], refs[-1]
    weights = refs[terms + joined : -1]
    n = len(weights) // terms
    step = pl.program_id(0)
    for p in range(n):
        steps = [t for t, (q, _) in enumerate(tiles) if q == p]

        @pl.when((step >= steps[0]) & (step <= steps[-1]))
        def _():
            value = sum(dot(acts[k][0], weights[k * n + p][...], (1, 0)) for k in range(terms))
            if joined:
                value += refs[terms][...].astype(F32)
            out[...] = rounded(value)


def spread_call(acts_t, which, tokens, weights, places, got=None):
    _, both, hidden = acts_t.shape
    rows = both // 2
    width = sum(length for _, length, _ in places)
    tile = 256
    tiles = backward_tiles(places, tile)

    def spec(p, m):
        steps = [t for t, (q, _) in enumerate(tiles) if q == p]
        first, last = steps[0], steps[-1]
        return pl.BlockSpec((hidden, tile), lambda t: (m, jnp.clip(t, first, last) - first))

    out = pl.BlockSpec((rows, tile), lambda t: (0, t))
    return kernel_call(
        functools.partial(spread_kernel, tiles, len(which), got is not None),
        (len(tiles),),
        [
            pl.BlockSpec((1, rows, hidden), lambda t, k=k: (k, tokens, 0), pipeline_mode=pl.Buffered(1))
            for k in which
        ]
        + ([] if got is None else [out])
        + [spec(p, m) for pieces in weights for p, (_, m) in enumerate(pieces)],
        out,
        sds((rows, width), BF16),
        0,
        0,
    )(*[acts_t] * len(which), *([] if got is None else [got]), *[a for pieces in weights for a, _ in pieces])


def weight_grad_kernel(left, first, second, *outs):
    def write(right):
        value = dot(left[0], right[...], (1, 0))
        start = 0
        for out in outs:
            length = out.shape[1]
            out[...] = rounded(value[:, start : start + length])
            start += length

    pl.when(pl.program_id(0) == 0)(lambda: write(first))
    pl.when(pl.program_id(0) > 0)(lambda: write(second))


def weight_grad_call(acts, first, second, lengths):
    _, hidden, both = acts.shape
    tile = hidden // 4
    return kernel_call(
        weight_grad_kernel,
        (3, 4),
        [pl.BlockSpec((1, tile, both), lambda m, i: (m, i, 0)), single(first.shape), single(second.shape)],
        [pl.BlockSpec((tile, n), lambda m, i: (4 * m + i, 0)) for n in lengths],
        [sds((3 * hidden, n), BF16) for n in lengths],
        0,
        0,
    )(acts, first, second)


def met_kernel(a, b, c, d, first, second):
    first[...] = rounded(a[...].astype(F32) + b[...].astype(F32))
    second[...] = rounded(c[...].astype(F32) + d[...].astype(F32))


def met_call(a, b, c, d):
    steps = 6 if a.shape[0] % 96 == 0 else 1
    left = pl.BlockSpec((a.shape[0] // steps, a.shape[1]), lambda i: (i, 0))
    return kernel_call(
        met_kernel, (steps,), [left] * 4, [left] * 2, [sds(a.shape, BF16)] * 2, 0, 0
    )(a, b, c, d)


def total_kernel(scal, own, x_first, y_first, x_second, y_second, mine, sent):
    shard = mine.shape[1]
    first = own[:, :shard].astype(F32) + x_first[...].astype(F32) + y_first[...].astype(F32)
    second = own[:, shard:].astype(F32) + x_second[...].astype(F32) + y_second[...].astype(F32)
    core = scal[1]
    mine[...] = jnp.where(core == 0, first, second)
    sent[...] = rounded(jnp.where(core == 0, second, first))


def total_call(scal, own, near):
    rows, span = own.shape
    tile = rows // 12
    half = pl.BlockSpec((tile, span // 2), lambda i: (i, 0))
    return kernel_call(
        total_kernel,
        (12,),
        [SCALARS, pl.BlockSpec((tile, span), lambda i: (i, 0))] + [half] * 4,
        [half] * 2,
        [sds((rows, span // 2), F32), sds((rows, span // 2), BF16)],
        0,
        0,
    )(scal, own, *near)


def lay_kernel(scal, *refs):
    mine, got, outs = refs[:3], refs[3:6], refs[6:]

    @pl.when(pl.program_id(0) == 0)
    def _():
        for m in range(3):
            outs[m][...] = mine[m][...]

    @pl.when(pl.program_id(0) == 1)
    def _():
        for m in range(3):
            outs[m][...] = got[m][...].astype(F32)


def lay_call(scal, mine, got):
    rows, shard = mine.shape
    part = rows // 3
    return prefetch_call(
        lay_kernel,
        scal,
        (2,),
        [pl.BlockSpec((part, shard), lambda i, s, m=m: (m, 0)) for m in range(3)] * 2,
        [pl.BlockSpec((part, shard), lambda i, s: (jnp.where(i == 0, s[1], 1 - s[1]), 0))] * 3,
        [sds((2 * part, shard), F32)] * 3,
        [mine] * 3 + [got] * 3,
    )


def pair_grad_kernel(scal, left_own, left_sent, first, second, own, sent):
    inner = first.shape[1]
    own[:, :inner] = dot(left_own[...], first[...], (0, 0))
    own[:, inner:] = dot(left_own[...], second[...], (0, 0))
    sent[:, :inner] = rounded(dot(left_sent[...], first[...], (0, 0)))
    sent[:, inner:] = rounded(dot(left_sent[...], second[...], (0, 0)))


def rows_grad_call(scal, left, first, second, shard):
    rows, width = left.shape
    columns = first.shape[1] + second.shape[1]
    count = width // (2 * shard)
    return prefetch_call(
        pair_grad_kernel,
        scal,
        (count,),
        [
            pl.BlockSpec((rows, shard), lambda r, s: (0, 2 * r + s[1])),
            pl.BlockSpec((rows, shard), lambda r, s: (0, 2 * r + 1 - s[1])),
            pl.BlockSpec(first.shape, lambda r, s: (0, 0)),
            pl.BlockSpec(second.shape, lambda r, s: (0, 0)),
        ],
        [pl.BlockSpec((shard, columns), lambda r, s: (r, 0))] * 2,
        [sds((count * shard, columns), F32), sds((count * shard, columns), BF16)],
        [left, left, first, second],
    )


def columns_grad_kernel(scal, left, right_own, right_sent, own, sent, left_t):
    @pl.when(pl.program_id(0) == 0)
    def _():
        left_t[...] = left[...].T

    own[...] = dot(left_t[...], right_own[...], (1, 0))
    sent[...] = rounded(dot(left_t[...], right_sent[...], (1, 0)))


def columns_grad_call(scal, left, right, shard):
    rows, inner = left.shape
    count = right.shape[1] // (2 * shard)
    return pl.pallas_call(
        columns_grad_kernel,
        grid_spec=pltpu.PrefetchScalarGridSpec(
            num_scalar_prefetch=1,
            grid=(count,),
            in_specs=[
                pl.BlockSpec((rows, inner), lambda r, s: (0, 0)),
                pl.BlockSpec((rows, shard), lambda r, s: (0, 2 * r + s[1])),
                pl.BlockSpec((rows, shard), lambda r, s: (0, 2 * r + 1 - s[1])),
            ],
            out_specs=[pl.BlockSpec((inner, shard), lambda r, s: (0, r))] * 2,
            scratch_shapes=[pltpu.VMEM((inner, rows), BF16)],
        ),
        out_shape=[sds((inner, count * shard), F32), sds((inner, count * shard), BF16)],
        compiler_params=pltpu.CompilerParams(vmem_limit_bytes=VMEM_BYTES),
        cost_estimate=cost(columns_grad_kernel),
    )(scal, left, right, right)


def cut_kernel(axis, mine, got, *outs):
    value = rounded(mine[...] + got[...].astype(F32))
    start = 0
    for out in outs:
        length = out.shape[axis]
        out[...] = lax.slice_in_dim(value, start, start + length, axis=axis)
        start += length


def cut_call(mine, got, axis):
    eighth = mine.shape[axis] // 8
    shapes = []
    for length in [2 * eighth] + [eighth] * 6:
        shape = list(mine.shape)
        shape[axis] = length
        shapes.append(sds(tuple(shape), BF16))
    return kernel_call(
        functools.partial(cut_kernel, axis),
        (1,),
        [whole(mine), whole(got)],
        [whole(v) for v in shapes],
        shapes,
        0,
        0,
    )(mine, got)


def end_kernel(axis, own, x_first, y_first, x_second, y_second, *outs):
    value = own[...].astype(F32)
    size = x_first.shape[axis]
    first = lax.slice_in_dim(value, 0, size, axis=axis) + x_first[...].astype(F32) + y_first[...].astype(F32)
    second = lax.slice_in_dim(value, size, 2 * size, axis=axis)
    second = second + x_second[...].astype(F32) + y_second[...].astype(F32)
    value = jnp.concatenate([first, second], axis)
    start = 0
    for out in outs:
        length = out.shape[1]
        out[...] = value[:, start : start + length]
        start += length


def end_call(own, near, axis, lengths):
    outs = [sds((own.shape[0], n), F32) for n in lengths]
    return kernel_call(
        functools.partial(end_kernel, axis),
        (1,),
        [whole(own)] + [whole(v) for v in near],
        [whole(v) for v in outs],
        outs,
        0,
        0,
    )(own, *near)


def route_kernel(top_count, hid, attn_add, gain, router_t, routes, resid, moe_low, gates):
    value = hid[...].astype(F32) + attn_add[...].astype(F32)
    resid[...] = value
    moe_low[...] = rounded(value * kernel_inverse_rms(value) * gain[...])
    logits = dot(moe_low[...], router_t[...], (1, 1))
    numbers = lax.broadcasted_iota(jnp.int32, logits.shape, 1)
    chosen = routes[:, 0:1] == numbers
    for k in range(1, top_count):
        chosen = chosen | (routes[:, k : k + 1] == numbers)
    top = jnp.max(jnp.where(chosen, logits, HIDE), -1, keepdims=True)
    lift = jnp.where(chosen, jnp.exp(jnp.where(chosen, logits, top) - top), 0.0)
    gates[...] = lift / jnp.sum(lift, -1, keepdims=True)


def row_specs(arrays, rows, tile):
    return [
        pl.BlockSpec((tile, a.shape[1]), lambda i: (i, 0)) if a.shape[0] == rows else whole(a) for a in arrays
    ]


def route_call(hid, attn_add, gain, router_t, routes):
    rows, width = hid.shape
    tile = rows // 3
    arrays = (hid, attn_add, gain, router_t, routes)
    outs = [sds((rows, width), F32), sds((rows, width), BF16), sds((rows, router_t.shape[0]), F32)]
    return kernel_call(
        functools.partial(route_kernel, routes.shape[1]),
        (3,),
        row_specs(arrays, rows, tile),
        row_specs(outs, rows, tile),
        outs,
        40 * rows * width,
        10 * rows * width,
    )(*arrays)


def route_back_kernel(
    grad_moe, gate_grads, gates, resid, cot, router_t, gain, grad_resid, resid_low, grad_logits, grad_gain
):
    chosen = gates[...]
    part = gate_grads[...]
    middle = jnp.sum(chosen * part, -1, keepdims=True)
    grad_logits[...] = rounded(chosen * (part - middle))
    total = grad_moe[...].astype(F32) + dot(grad_logits[...], router_t[...], (1, 0))
    value = resid[...]
    shrink = kernel_inverse_rms(value)
    normal = value * shrink

    @pl.when(pl.program_id(0) == 0)
    def _():
        grad_gain[...] = jnp.zeros(grad_gain.shape, F32)

    grad_gain[...] += jnp.sum(total * normal, 0, keepdims=True)
    scaled = total * gain[...]
    mean = jnp.mean(scaled * normal, axis=-1, keepdims=True)
    out = cot[...].astype(F32) + shrink * (scaled - normal * mean)
    grad_resid[...] = out
    resid_low[...] = rounded(out)


def route_back_call(grad_moe, gate_grads, gates, resid, cot, router_t, gain):
    rows, width = resid.shape
    tile = rows // 3
    arrays = (grad_moe, gate_grads, gates, resid, cot, router_t, gain)
    outs = [
        sds((rows, width), F32),
        sds((rows, width), BF16),
        sds(gates.shape, BF16),
        sds((1, width), F32),
    ]
    return kernel_call(
        route_back_kernel,
        (3,),
        row_specs(arrays, rows, tile),
        row_specs(outs, rows, tile),
        outs,
        50 * rows * width,
        14 * rows * width,
    )(*arrays)


def to_whole_order(scal, blocks, value, out):
    span = value.shape[1] // blocks
    for j in range(blocks):
        target = pl.multiple_of((scal[0] ^ j) * span, span)
        out[:, pl.ds(target, span)] = value[:, j * span : (j + 1) * span]


def add_kernel(blocks, scal, first, second, out):
    value = rounded(first[...] + second[...].astype(F32))
    to_whole_order(scal, blocks, value, out)


def add_call(scal, resid, part, blocks):
    rows, width = part.shape
    return prefetch_call(
        functools.partial(add_kernel, blocks),
        scal,
        (1,),
        [pl.BlockSpec((rows, width), lambda i, s: (s[2], 0)), pl.BlockSpec((rows, width), lambda i, s: (0, 0))],
        pl.BlockSpec((rows, width), lambda i, s: (0, 0)),
        sds((rows, width), BF16),
        [resid, part],
    )


def last_kernel(blocks, scal, hid, grad_resid, grad_normed, gain, out, wide):
    wide[...] = hid[...].astype(F32)
    rows = out.shape[0]
    tokens = wide[pl.ds(pl.multiple_of(scal[2] * rows, 8), rows)]
    shrink = kernel_inverse_rms(tokens)
    normal = tokens * shrink
    scaled = grad_normed[...].astype(F32) * gain[...]
    middle = jnp.mean(scaled * normal, axis=-1, keepdims=True)
    value = rounded(grad_resid[...] + shrink * (scaled - normal * middle))
    to_whole_order(scal, blocks, value, out)


def last_call(scal, hid, grad_resid, grad_normed, gain, blocks):
    rows, width = grad_normed.shape
    part = pl.BlockSpec((rows, width), lambda i, s: (0, 0))
    return prefetch_call(
        functools.partial(last_kernel, blocks),
        scal,
        (1,),
        [whole(hid), pl.BlockSpec((rows, width), lambda i, s: (s[2], 0)), part, whole(gain)],
        part,
        sds((rows, width), BF16),
        [hid, grad_resid, grad_normed, gain],
        [pltpu.VMEM(hid.shape, F32)],
    )


def angle_tables(positions):
    half_size = HEAD // 2
    frequency = jnp.exp(jnp.arange(half_size, dtype=F32) * (-2.0 * math.log(THETA) / HEAD))
    angles = positions.astype(F32)[..., None] * frequency
    sine = jnp.sin(angles)
    cosine = jnp.cos(angles)
    return jnp.concatenate([cosine, cosine], -1), jnp.concatenate([-sine, sine], -1)


def lookup_parent(segment_ids, parent):
    seg_table = jnp.arange(parent.shape[-1], dtype=jnp.int32)
    return jnp.sum(jnp.where(segment_ids[..., None] == seg_table, parent, 0), -1)


def shards(
    hidden,
    cotangent,
    gain_attn,
    query_weight,
    key_weight,
    value_weight,
    gain_query,
    gain_key,
    out_weight,
    gain_moe,
    router_weight,
    gate_weight,
    up_weight,
    down_weight,
    segment,
    parent,
    tree_depth,
    routes,
):
    _, rows, width = hidden.shape
    dp, x, core = place()
    ctx = lax.axis_index("ctx")
    count = lax.axis_size("dp")
    paired = count == 2
    chips = 2 * count
    tensor = lax.axis_size("tensor")
    heads = HEADS_Q // tensor
    shard = query_weight.shape[0]
    span = 2 * shard
    inner = heads * HEAD
    columns = inner + 2 * HEAD
    half = EXPERTS // 2
    hid = down_weight.shape[1]
    scal = jnp.stack([flips(), core, lax.axis_index("tensor")]).astype(jnp.int32)
    hidden_rows = half * hid

    def by_core(own, other, axis):
        return jnp.where(core == 0, jnp.stack([own, other], axis), jnp.stack([other, own], axis))

    def five_places(size):
        starts = [0, span, 2 * span, 3 * span, 3 * span + size // 2]
        return list(zip(starts, [size, size, size, size // 2, size // 2], [0] * 5))

    def both_cores(own, size):
        return own + [to_core(a) for a in own], [(s, n, k) for k in (1, 2) for s, n, _ in five_places(size)]

    def whole_piece(block, axis):
        own = gather_whole(block, axis)
        cut = own.shape[:axis] + (chips, shard) + own.shape[axis + 1 :]
        full = by_core(own.reshape(cut), to_core(own).reshape(cut), axis + 1)
        return [full.reshape(own.shape[:axis] + (width,) + own.shape[axis + 1 :])], [(0, width, 0)]

    per = gain_query.shape[0]
    heads_column = jnp.pad(jnp.concatenate([gain_query, gain_key]), (0, shard - 2 * per))
    small = [router_weight, gain_attn[:, None], gain_moe[:, None], heads_column[:, None]]
    small.append(jnp.zeros((shard, HEAD - EXPERTS - 3), BF16))
    qkv_shard = jnp.concatenate([query_weight, key_weight, value_weight] + small, 1)
    expert_weights = [down_weight, gate_weight.transpose(0, 2, 1), up_weight.transpose(0, 2, 1)]
    if paired:
        qkv_x, qkv_y = exchange(qkv_shard, qkv_shard)
        expert_block = block_call(scal, expert_weights, to_core(other_half_call(scal, expert_weights)))
        far_second, far_first = exchange(halves(qkv_y, 0)[1], halves(qkv_x, 0)[0], expert_block)
        qkv_pieces, qkv_places = both_cores([qkv_shard, qkv_x, qkv_y, far_first, far_second], shard)
        out_x, out_y = exchange(out_weight, out_weight, far_first, far_second)
        out_far_second, out_far_first = exchange(halves(out_y, 1)[1], halves(out_x, 1)[0])
        out_pieces, out_places = both_cores([out_weight, out_x, out_y, out_far_first, out_far_second], shard)
        gains = ()
    else:
        qkv_pieces, qkv_places = whole_piece(qkv_shard, 0)
        small_t = qkv_pieces[0][:, columns:].T
        router_t = small_t[:EXPERTS]
        gain_one, gain_two = (small_t[EXPERTS + i][None].astype(F32) for i in range(2))
        gain_heads = relative(small_t[EXPERTS + 2]).reshape(2 * chips, shard).astype(F32)
        gain_q = gain_heads[:, :per].reshape(1, HEAD)
        gain_k = gain_heads[:, per : 2 * per].reshape(1, HEAD)
        gains = (gain_one, gain_q, gain_k)
        out_pieces, out_places = whole_piece(out_weight, 1)
        sent = [lax.dynamic_slice_in_dim(w, (1 - core) * half, half, 0) for w in expert_weights]
        own = [lax.dynamic_slice_in_dim(w, core * half, half, 0) for w in expert_weights]
        expert_block = by_core(jnp.stack(own), to_core(jnp.stack(sent)), 3).reshape(3 * hidden_rows, span)

    cosine, sine = angle_tables(tree_depth[0])
    *found, normed, tokens_low, raw, rot = qkv_call(
        scal, hidden[0], gains, cosine, sine, qkv_pieces, qkv_places, shard, per, chips, columns
    )
    if found:
        gain_one, gain_two, router_t, gain_q, gain_k = found
    key_value = rot[:, inner:]
    kv_x = to_x(key_value)
    kv_other = to_core(key_value)
    kv_all = jnp.concatenate([key_value, kv_other, kv_x, to_core(kv_x)])
    if paired:
        near_x, near_y = exchange(expert_block, expert_block, kv_x, out_far_first)
        forwarded, expert_pieces = [], []
        gate = ()
        for m in range(3):
            rows_of = slice(m * hidden_rows, (m + 1) * hidden_rows)
            forwarded.append((near_y[rows_of, shard:], near_x[rows_of, :shard]))
            far_second, far_first = exchange(*forwarded[-1], *gate)
            gate = (far_first, far_second)
            expert_pieces.append([(expert_block, m), (near_x, m), (near_y, m), (far_first, 0), (far_second, 0)])
        expert_places = five_places(span)
    else:
        gathered = gather_whole(expert_block, 1)
        expert_pieces = [[(gathered, m)] for m in range(3)]
        expert_places = [(0, width, 0)]
    down_pieces, gate_pieces, up_pieces = expert_pieces

    seg = segment[0].reshape(2, 2, rows)
    seg_rel = flip(flip(seg, 0, x), 1, core).reshape(4 * rows)
    position = jnp.arange(4 * rows, dtype=jnp.int32).reshape(2, 2, rows)
    key_pos = flip(flip(position, 0, x), 1, core).reshape(4 * rows)
    first_up = lookup_parent(seg_rel[:rows], parent[0])
    second_up = lookup_parent(first_up, parent[0])
    key_side = jnp.stack([seg_rel, key_pos], 1)
    query_side = jnp.stack([seg_rel[:rows], first_up, second_up, key_pos[:rows]])

    mixed_low, inverse = attend_call(rot, kv_all, key_side, query_side, heads)
    attn_part = project_call(scal, mixed_low, out_pieces, out_places, shard, width)
    attn_add = lax.psum(attn_part, "tensor")

    cot = permute_width(cotangent[0], scal, chips)
    cot_other = to_core(cot)
    grad_act, pair_dy = products_call(cot, cot_other, down_pieces, hidden_rows)
    if paired:
        attn_add = after(attn_add, down_pieces[3][0], down_pieces[4][0])
    resid, moe_low, gates = route_call(tokens_low, attn_add, gain_two, router_t, routes[0])
    moe_other = to_core(moe_low)
    gate_pre, pair_x = products_call(moe_low, moe_other, gate_pieces, hidden_rows)
    gates_t = gates.T
    gates_own = lax.dynamic_slice_in_dim(gates_t, core * half, half, 0)
    gates_sent = lax.dynamic_slice_in_dim(gates_t, (1 - core) * half, half, 0)
    gate_pair = jnp.concatenate([gates_own, to_core(gates_sent)], 1)[:, None, :]

    acts, acts_t, gate_part = experts_call(pair_x, gate_pre, grad_act, gate_pair, up_pieces, hid)
    weights = [gate_pieces, up_pieces]
    part_other = to_core(spread_call(acts_t, (1, 2), 1, weights, expert_places))
    moe_sum = spread_call(acts_t, (1, 2), 0, weights, expert_places, part_other)
    grad_moe_in = lax.psum(moe_sum, "tensor")
    acts, acts_t, gate_part = lax.optimization_barrier((acts, acts_t, gate_part, moe_sum))[:3]
    gate_grads = gate_join_call(scal, *gate_sum_call(gate_part))

    lengths = [span] + [shard] * 6 if paired else [span] * chips
    grad_blocks = weight_grad_call(acts, pair_dy, pair_x, lengths)
    acts_t = after(acts_t, grad_blocks[0])
    grad_moe_in = after(grad_moe_in, grad_blocks[0])
    if paired:
        own_grads, x_first, x_second, y_first, y_second, far_first, far_second = grad_blocks
        far_x, far_y = exchange(far_first, far_second)
        x_first, y_second = exchange(x_first, y_second)
        grad_moe_in = after(grad_moe_in, far_x, far_y)
    out_other = to_core(spread_call(acts_t, (0,), 1, [down_pieces], expert_places))
    out_sum = spread_call(acts_t, (0,), 0, [down_pieces], expert_places, out_other)
    grad_moe_in = after(grad_moe_in, out_sum)
    out_sum = after(out_sum, grad_moe_in, gate_grads)
    moe_add = lax.psum_scatter(out_sum, "tensor", scatter_dimension=0, tiled=True)
    output_rows = add_call(scal, resid, moe_add, chips)
    output = lax.all_gather(output_rows, "tensor", axis=0, tiled=True)[None]

    grad_resid, resid_low, grad_logits, grad_gain_two = route_back_call(
        grad_moe_in, gate_grads, gates, resid, cot, router_t, gain_two
    )

    grad_mixed = project_back_call(scal, after(resid_low, out_sum), out_pieces, out_places, shard, inner)
    query_back, kv_own, kv_sent, kv_mid, grad_gain_q = attend_back_call(
        rot, kv_all, key_side, query_side, grad_mixed, mixed_low, inverse, raw, cosine, sine, gain_q, heads
    )
    if paired:
        kv_mid = after(kv_mid, x_first, y_second)
    kv_part, kv_on = kv_pass_call(kv_own, after(kv_mid, output_rows), to_core(kv_sent))
    kv_far = to_x(kv_on)
    if paired:
        x_second, y_first = met_call(after(x_second, kv_far), far_y, y_first, far_x)
        x_second, y_first = exchange(x_second, y_first)
        near_grads = (x_first, y_first, x_second, y_second)
    back_part, grad_gain_one, kv_back, grad_gain_k = qkv_back_call(
        scal, query_back, kv_part, kv_far, raw, cosine, sine, gain_k, tokens_low, qkv_pieces, qkv_places, shard
    )
    grad_normed = lax.psum_scatter(back_part, "tensor", scatter_dimension=0, tiled=True)
    hidden_rows_out = last_call(scal, tokens_low, grad_resid, grad_normed, gain_one, chips)
    grad_hidden = lax.all_gather(hidden_rows_out, "tensor", axis=0, tiled=True)[None]

    late_resid, late_mixed, late_normed, late_moe = lax.optimization_barrier(
        (resid_low, mixed_low, normed, moe_low, back_part)
    )[:4]
    grad_router_t = dot(grad_logits, late_moe, (0, 0))
    if paired:
        qkv_mine, qkv_sent = rows_grad_call(scal, late_normed, query_back, kv_back, shard)
        out_mine, out_sent = columns_grad_call(scal, late_mixed, late_resid, shard)
        qkv_blocks = cut_call(qkv_mine, to_core(qkv_sent), 0)
        out_blocks = cut_call(out_mine, to_core(out_sent), 1)

        def plane_sum(blocks, axis, lengths):
            own, x_first, x_second, y_first, y_second, far_first, far_second = blocks
            far_x, far_y = exchange(far_first, far_second)
            x_first, y_second = exchange(x_first, y_second)
            x_second, y_first = exchange(*met_call(x_second, far_y, y_first, far_x))
            near = (x_first, y_first, x_second, y_second)
            return end_call(own, near, axis, lengths)

        grad_query, grad_key, grad_value = plane_sum(qkv_blocks, 0, [inner, HEAD, HEAD])
        (grad_out_weight,) = plane_sum(out_blocks, 1, [shard])
        own_grads = after(own_grads, qkv_blocks[0], out_blocks[0])
        mine, sent = total_call(scal, own_grads, near_grads)
    else:
        qkv_back = jnp.concatenate([query_back, kv_back], 1)
        sides = [
            (pick_columns(late_normed, scal, shard, o), pick_columns(late_resid, scal, shard, o))
            for o in (False, True)
        ]
        qkv_mine, qkv_sent = (dot(n, qkv_back, (0, 0)) for n, _ in sides)
        out_mine, out_sent = (dot(late_mixed, r, (0, 0)) for _, r in sides)
        qkv_sum = rounded(qkv_mine + to_core(rounded(qkv_sent)).astype(F32))
        out_sum = rounded(out_mine + to_core(rounded(out_sent)).astype(F32))
        grad_qkv = scatter_whole([qkv_sum[r * shard : (r + 1) * shard] for r in range(chips)])
        grad_query, grad_key, grad_value = jnp.split(grad_qkv, [inner, inner + HEAD], 1)
        grad_out_weight = scatter_whole([out_sum[:, r * shard : (r + 1) * shard] for r in range(chips)])
        total = scatter_whole(grad_blocks)
        mine = lax.dynamic_slice_in_dim(total, core * shard, shard, 1)
        sent = rounded(lax.dynamic_slice_in_dim(total, (1 - core) * shard, shard, 1))
    grad_down, grad_gate, grad_up = (
        v.reshape(EXPERTS, hid, shard) for v in lay_call(scal, mine, to_core(sent))
    )
    grad_gate, grad_up = grad_gate.transpose(0, 2, 1), grad_up.transpose(0, 2, 1)

    share = 1.0 / tensor
    head_rows = jnp.concatenate(
        [grad_gain_q.reshape(2 * chips, per), grad_gain_k.reshape(2 * chips, per)], 1
    )
    head_rows = relative(jnp.pad(head_rows, ((0, 0), (0, shard - 2 * per))).reshape(width))
    table = jnp.concatenate(
        [
            grad_gain_one,
            grad_gain_two * share,
            grad_router_t * share,
            head_rows[None],
            jnp.zeros((5, width), F32),
        ]
    ).reshape(24, chips, 2, shard)
    table_own = lax.dynamic_index_in_dim(table, core, 2, keepdims=False)
    table_sent = lax.dynamic_index_in_dim(table, 1 - core, 2, keepdims=False)
    table = table_own + to_core(table_sent)
    table = table.reshape(24, count, 2, shard)
    table = table[:, :, 0] + to_x(table[:, :, 1])
    if paired:
        table = table[:, 0] + to_dp(table[:, 1])
    else:
        table = lax.psum_scatter(table, "dp", scatter_dimension=1, tiled=False)
    mine = sum_z(table)
    gains = mine[2 + EXPERTS, : 2 * per]

    return (
        output,
        grad_hidden,
        mine[0],
        grad_query,
        grad_key,
        grad_value,
        gains[:per],
        gains[per:],
        grad_out_weight,
        mine[1],
        mine[2 : 2 + EXPERTS].T,
        grad_gate,
        grad_up,
        grad_down,
    )


def solution(mesh):
    plane = ("dp", "ctx")
    in_specs = (
        P("dp", "ctx", None),
        P("dp", "ctx", None),
        P(plane),
        P(plane, "tensor"),
        P(plane, "tensor"),
        P(plane, "tensor"),
        P(plane),
        P(plane),
        P("tensor", plane),
        P(plane),
        P(plane, None),
        P(None, plane, "tensor"),
        P(None, plane, "tensor"),
        P(None, "tensor", plane),
        P("dp", None),
        P("dp", None),
        P("dp", "ctx"),
        P("dp", "ctx", None),
    )
    out_specs = (
        P("dp", "ctx", None),
        P("dp", "ctx", None),
        P(plane),
        P(plane, "tensor"),
        P(plane, "tensor"),
        P(plane, "tensor"),
        P(plane),
        P(plane),
        P("tensor", plane),
        P(plane),
        P(plane, None),
        P(None, plane, "tensor"),
        P(None, plane, "tensor"),
        P(None, "tensor", plane),
    )
    return jax.shard_map(shards, mesh=mesh, in_specs=in_specs, out_specs=out_specs, check_vma=False)
```

time: 766 us -> 659 us (0.86)
  Pallas kernels: 202 us -> 304 us
  other arithmetic: 64.9 us -> 6.67 us
  local copies, waits for them, and re-layouts: 83.1 us -> 27.9 us
  matrix products: 52 us -> 0.39 us
  waiting for transfers between devices: 268 us -> 240 us
  starting transfers between devices: 69.8 us -> 53.9 us
    pallas_call x10 -> x25, Pallas kernels: 90.1 us -> 191 us  [the longest x4 48.4 us: spread_call(): kernel_call(functools.partial(spread_kernel, tiles, len(which), got is no...]
    dot_general x17 -> x1, matrix products: 52 us -> 0.39 us  [dot(): lax.dot_general(a, b, ((contract[:1], contract[1:]), ((), ())), preferred...]
    ppermute x29 -> x20, waiting for transfers between devices: 141 us -> 171 us  [to_x(): return lax.ppermute(v, 'ctx', [(i, i ^ 2) for i in range(4)])]
    ppermute x28 -> x18, waiting for transfers between devices: 42 us -> 16.8 us  [to_dp(): return lax.ppermute(v, 'dp', [(0, 1), (1, 0)])]
    split x21 -> x4, local copies, waits for them, and re-layouts: 24.3 us -> 0.09 us  [halves(): return jnp.split(v, 2, axis)]
    psum x1, waiting for transfers between devices: 50.4 us -> 27.4 us  [shards(): grad_moe_in = lax.psum(moe_sum, 'tensor')]
    convert_element_type x15 -> x0, other arithmetic: 22.5 us -> none  [the longest x12 22.4 us: rounded(): return v.astype(BF16)]
    ppermute x4 -> x6, waiting for transfers between devices: 20.1 us -> 5.57 us  [the longest x3 3.42 us: sum_z(): lax.ppermute(v, 'tensor', [(i, i ^ k) for i in range(size)])]
  transfers between devices with their start and end apart: 95 -> 74, of which waited for: 29 -> 38; matrix products, arithmetic and copies ran while one was open for 23% -> 3% of each run, Pallas kernels for 20% -> 34%
where the time goes in v2:
time: 659 us; the launch traced here: 649 us
  Pallas kernels  304 us (46%)
  waiting for transfers between devices  240 us (36%)
  starting transfers between devices  53.9 us (8%)
  local copies, waits for them, and re-layouts  27.9 us (4%)
  between operations  15.4 us (2%)
  other arithmetic  6.67 us (1%)
    ppermute x20, waiting for transfers between devices, to_x(): return lax.ppermute(v, 'ctx', [(i, i ^ 2) for i in range(4)])  171 us
    pallas_call x4, Pallas kernels, spread_call(): kernel_call(functools.partial(spread_kernel, tiles, len(which), got is no...  48.4 us
    pallas_call x6, Pallas kernels, prefetch_call(): pl.pallas_call(body, grid_spec=pltpu.PrefetchScalarGridSpec(num_scalar_pr...  32.8 us
    pallas_call x1, Pallas kernels, attend_back_call(): kernel_call(attend_back_kernel, (heads,), [column, pl.BlockSpec((count, H...  30.2 us
    psum x1, waiting for transfers between devices, shards(): grad_moe_in = lax.psum(moe_sum, 'tensor')  27.4 us
    pallas_call x1, Pallas kernels, weight_grad_call(): kernel_call(weight_grad_kernel, (3, 4), [pl.BlockSpec((1, tile, both), la...  27 us
    pallas_call x2, Pallas kernels, products_call(): kernel_call(products_kernel, (4,), [single(own.shape), single(own.shape)]...  23.8 us
    ppermute x20, starting transfers between devices, to_x(): return lax.ppermute(v, 'ctx', [(i, i ^ 2) for i in range(4)])  20.9 us
  transfers between devices with their start and end apart: 74, of which 38 were waited for; matrix products, arithmetic and copies ran while one was open for 3% of the time, Pallas kernels for 34%

profile of v2, /device:TPU:0, one launch (start us, length us, event | category | flops | bytes accessed | tf_op | source)
XLA Modules:
  0.0 649.0 jit_solution(16474527587598077656)
XLA Ops:
  7.9 4.3 shard_map.281
  13.6 2.6 collective-permute-start
  17.7 15.3 %collective-permute-done.refs_1_.refs_11_ = bf16[256,1408]{1,0:T(8,128)(2,1)S(1)} collective-permute-done((bf16[256,1408]{1,0:T(8,128)(2,1)S(1)}, bf16[256,1408]{1,0:T(8,128)(2,1)S(1)}, u32[]{:S(2)}, u32[]{:S(2)}) %collective-permute-start) | collective-permute-done | bytes 720928 | tf_op jit(solution)/shard_map/ppermute | solution.py:44
  34.5 5.9 shard_map.282.refs_0_.refs_2_.refs_7_.refs_3_.refs_8_.refs_1_
  40.8 1.7 collective-permute-start.4
  42.5 7.7 %collective-permute-done.3.refs_4_.refs_14_ = bf16[128,1408]{1,0:T(8,128)(2,1)S(1)} collective-permute-done((bf16[128,1408]{1,0:T(8,128)(2,1)S(1)}, bf16[128,1408]{1,0:T(8,128)(2,1)S(1)}, u32[]{:S(2)}, u32[]{:S(2)}) %collective-permute-start.3) | collective-permute-done | bytes 360480 | tf_op jit(solution)/shard_map/ppermute | solution.py:44
  54.0 9.1 %collective-permute-done.13.refs_1_ = bf16[1024,256]{1,0:T(8,128)(2,1)S(1)} collective-permute-done((bf16[1024,256]{1,0:T(8,128)(2,1)}, bf16[1024,256]{1,0:T(8,128)(2,1)S(1)}, u32[]{:S(2)}, u32[]{:S(2)}) %collective-permute-start.13) | collective-permute-done | bytes 524320 | tf_op jit(solution)/shard_map/ppermute | solution.py:44
  69.5 12.2 %shard_map.283 = (f32[1,2048]{1,0:T(1,128)}, f32[1,2048]{1,0:T(1,128)}, bf16[16,2048]{1,0:T(8,128)(2,1)}, f32[1,128]{1,0:T(1,128)}, f32[1,128]{1,0:T(1,128)}, /*...) custom-call(s32[3]{0:T(128)} %pad_add_fusion.2.scal, ...), custom_call_target="tpu_custom_call" | custom-call | flops 11699999744 | tf_op jit(solution)/shard_map/pallas_call | solution.py:325
  83.9 6.4 collective-permute-done.11
  98.7 16.2 %shard_map.284 = (bf16[480,1024]{1,0:T(8,128)(2,1)}, f32[8,1,480]{2,1,0:T(1,128)}) custom-call(bf16[480,1280]{1,0:T(8,128)(2,1)} %get-tuple-element.180.query, bf16[1920,256]{1,0:T(8,128)(2,1)} %pad_maximum_fusion.keys.values, bf16[1920,256]{1,0:T(8,128)(2,1)} %pad_maximum_fusion.keys.values, s32[1920,2]{1,0:T(8,128)} %copy.64.key_side, ...), custom_call_target="tpu_custom_call" | custom-call | flops 16300000256 | tf_op jit(solution)/shard_map/pallas_call | solution.py:371
  115.9 6.6 %shard_map.285 = bf16[480,2048]{1,0:T(8,128)(2,1)} custom-call(s32[3]{0:T(128)} %pad_add_fusion.2.scal, bf16[480,1024]{1,0:T(8,128)(2,1)} %get-tuple-element.292.mixed.left, bf16[1024,256]{1,0:T(8,128)(2,1)} %refs_0_.7, bf16[1024,256]{1,0:T(8,128)(2,1)} %copy-done.21, bf16[1024,256]{1,0:T(8,128)(2,1)} %copy-done.22, bf16[1024,128]{1,0:T(8,128)(2,1)} %copy-done.51, ...), custom_call_target="tpu_custom_call" | custom-call | flops 6600000000 | tf_op jit(solution)/shard_map/pallas_call | solution.py:486
  123.1 70.2 %collective-permute-done.22.refs_1_.refs_3_.refs_8_.refs_4_.refs_9_.refs_2_ = bf16[4608,512]{1,0:T(8,128)(2,1)} collective-permute-done((bf16[4608,512]{1,0:T(8,128)(2,1)}, bf16[4608,512]{1,0:T(8,128)(2,1)}, u32[]{:S(2)}, u32[]{:S(2)}) %collective-permute-start.22) | collective-permute-done | bytes 4718624 | tf_op jit(solution)/shard_map/ppermute | solution.py:44
  194.5 2.7 fusion.7
  197.2 2.6 fusion.6
  201.4 4.6 shard_map.288.own.cot
  206.8 10.5 %collective-permute-done.24.refs_4_.refs_5_.refs_6_ = bf16[1536,256]{1,0:T(8,128)(2,1)} collective-permute-done((bf16[1536,256]{1,0:T(8,128)(2,1)S(1)}, bf16[1536,256]{1,0:T(8,128)(2,1)}, u32[]{:S(2)}, u32[]{:S(2)}) %collective-permute-start.24) | collective-permute-done | bytes 786464 | tf_op jit(solution)/shard_map/ppermute | solution.py:44
  219.6 6.4 shard_map.286
  227.5 7.3 %collective-permute-done.27.refs_4_.refs_6_.refs_7_ = bf16[1536,256]{1,0:T(8,128)(2,1)S(1)} collective-permute-done((bf16[1536,256]{1,0:T(8,128)(2,1)}, bf16[1536,256]{1,0:T(8,128)(2,1)S(1)}, u32[]{:S(2)}, u32[]{:S(2)}) %collective-permute-start.27) | collective-permute-done | bytes 786464 | tf_op jit(solution)/shard_map/ppermute | solution.py:44
  234.8 1.6 collective-permute-done.28.refs_3_.refs_5_.refs_6_
  237.6 11.8 %shard_map.289 = (f32[1536,960]{1,0:T(8,128)}, bf16[960,2048]{1,0:T(8,128)(2,1)}) custom-call(bf16[480,2048]{1,0:T(8,128)(2,1)} %shard_map.288.own.cot, bf16[480,2048]{1,0:T(8,128)(2,1)} %collective-permute-done.29.other, bf16[4608,512]{1,0:T(8,128)(2,1)} %shard_map.282.refs_0_.refs_2_.refs_7_.refs_3_.refs_8_.refs_1_, ...), custom_call_target="tpu_custom_call" | custom-call | flops 11800000512 | tf_op jit(solution)/shard_map/pallas_call | solution.py:620
  251.9 12.0 %shard_map.287 = (f32[1536,960]{1,0:T(8,128)}, bf16[960,2048]{1,0:T(8,128)(2,1)}) custom-call(bf16[480,2048]{1,0:T(8,128)(2,1)} %get-tuple-element.263.own, bf16[480,2048]{1,0:T(8,128)(2,1)} %collective-permute-done.26.other, bf16[4608,512]{1,0:T(8,128)(2,1)} %shard_map.282.refs_0_.refs_2_.refs_7_.refs_3_.refs_8_.refs_1_, ...), custom_call_target="tpu_custom_call" | custom-call | flops 11800000512 | tf_op jit(solution)/shard_map/pallas_call | solution.py:620
  263.9 19.9 %shard_map.290 = (bf16[3,1536,960]{2,1,0:T(8,128)(2,1)}, bf16[3,960,1536]{2,1,0:T(8,128)(2,1)}, f32[8,1,960]{2,1,0:T(1,128)}) custom-call(bf16[960,2048]{1,0:T(8,128)(2,1)} %get-tuple-element.207.both.second, f32[1536,960]{1,0:T(8,128)} %get-tuple-element.208.gate_ref, f32[1536,960]{1,0:T(8,128)} %get-tuple-element.209.grad_act, ...), custom_call_target="tpu_custom_call" | custom-call | flops 20000000000 | tf_op jit(solution)/shard_map/pallas_call | solution.py:661
  283.8 14.1 %shard_map.291 = bf16[480,2048]{1,0:T(8,128)(2,1)} custom-call(bf16[3,960,1536]{2,1,0:T(8,128)(2,1)} %get-tuple-element.222.refs_0_.refs_1_, bf16[3,960,1536]{2,1,0:T(8,128)(2,1)} %get-tuple-element.222.refs_0_.refs_1_, bf16[4608,512]{1,0:T(8,128)(2,1)} %shard_map.282.refs_0_.refs_2_.refs_7_.refs_3_.refs_8_.refs_1_, ...), custom_call_target="tpu_custom_call" | custom-call | flops 10000000000 | tf_op jit(solution)/shard_map/pallas_call | solution.py:740
  298.0 4.2 collective-permute-done.33.refs_2_
  303.4 14.5 %shard_map.292 = bf16[480,2048]{1,0:T(8,128)(2,1)} custom-call(bf16[3,960,1536]{2,1,0:T(8,128)(2,1)} %get-tuple-element.222.refs_0_.refs_1_, bf16[3,960,1536]{2,1,0:T(8,128)(2,1)} %get-tuple-element.222.refs_0_.refs_1_, bf16[480,2048]{1,0:T(8,128)(2,1)} %copy-done.9, bf16[4608,512]{1,0:T(8,128)(2,1)} %shard_map.282.refs_0_.refs_2_.refs_7_.refs_3_.refs_8_.refs_1_, ...), custom_call_target="tpu_custom_call" | custom-call | flops 10000000000 | tf_op jit(solution)/shard_map/pallas_call | solution.py:740
  318.1 27.0 %shard_map.293 = (bf16[4608,512]{1,0:T(8,128)(2,1)}, bf16[4608,256]{1,0:T(8,128)(2,1)}, bf16[4608,256]{1,0:T(8,128)(2,1)}, bf16[4608,256]{1,0:T(8,128)(2,1)}, bf...) custom-call(bf16[3,1536,960]{2,1,0:T(8,128)(2,1)} %get-tuple-element.219.left, ...), custom_call_target="tpu_custom_call" | custom-call | flops 49999998976 | tf_op jit(solution)/shard_map/pallas_call | solution.py:772
  345.1 9.5 %shard_map.294 = bf16[480,2048]{1,0:T(8,128)(2,1)} custom-call(bf16[3,960,1536]{2,1,0:T(8,128)(2,1)} %get-tuple-element.222.refs_0_.refs_1_, bf16[4608,512]{1,0:T(8,128)(2,1)} %shard_map.282.refs_0_.refs_2_.refs_7_.refs_3_.refs_8_.refs_1_, bf16[4608,512]{1,0:T(8,128)(2,1)} %collective-permute-done.22.refs_1_.refs_3_.refs_8_.refs_4_.refs_9_.refs_2_, ...), custom_call_target="tpu_custom_call" | custom-call | flops 10000000000 | tf_op jit(solution)/shard_map/pallas_call | solution.py:740
  357.7 2.6 collective-permute-start.38
  360.4 3.6 collective-permute-start.39
  363.9 2.1 collective-permute-done.39.fourth
  370.9 1.6 shard_map.297.gate_grads
  372.4 27.4 %all-reduce.7.cloned.1.call-done.grad_moe = bf16[480,2048]{1,0:T(8,128)(2,1)} async-done(((bf16[480,2048]{1,0:T(8,128)(2,1)}), bf16[480,2048]{1,0:T(8,128)(2,1)}) %all-reduce.7.cloned.1.call-update) | async-done | bytes 1966096 | tf_op jit(solution)/shard_map/psum | solution.py:1247
  399.8 10.3 %shard_map.295 = bf16[480,2048]{1,0:T(8,128)(2,1)} custom-call(bf16[3,960,1536]{2,1,0:T(8,128)(2,1)} %get-tuple-element.222.refs_0_.refs_1_, bf16[480,2048]{1,0:T(8,128)(2,1)} %collective-permute-done.34.refs_1_, bf16[4608,512]{1,0:T(8,128)(2,1)} %shard_map.282.refs_0_.refs_2_.refs_7_.refs_3_.refs_8_.refs_1_, ...), custom_call_target="tpu_custom_call" | custom-call | flops 10000000000 | tf_op jit(solution)/shard_map/pallas_call | solution.py:740
  410.2 8.9 %shard_map.299 = (f32[480,2048]{1,0:T(8,128)}, bf16[480,2048]{1,0:T(8,128)(2,1)}, bf16[480,16]{1,0:T(8,128)(2,1)}, f32[1,2048]{1,0:T(1,128)}) custom-call(bf16[480,2048]{1,0:T(8,128)(2,1)} %all-reduce.7.cloned.1.call-done.grad_moe, f32[480,16]{1,0:T(8,128)} %shard_map.297.gate_grads, f32[480,16]{1,0:T(8,128)} %get-tuple-element.210.gates, ...), custom_call_target="tpu_custom_call" | custom-call | flops 8600000512 | tf_op jit(solution)/shard_map/pallas_call | solution.py:1031
  419.1 6.4 shard_map.300.grad
  425.6 30.2 %shard_map.301 = (bf16[480,1024]{1,0:T(8,128)(2,1)}, f32[480,256]{1,0:T(8,128)}, bf16[960,256]{1,0:T(8,128)(2,1)}, f32[480,256]{1,0:T(8,128)}, f32[1,128]{1,0:T(1,128)}) custom-call(bf16[480,1280]{1,0:T(8,128)(2,1)} %get-tuple-element.180.query, bf16[1920,256]{1,0:T(8,128)(2,1)} %pad_maximum_fusion.keys.values, ...), custom_call_target="tpu_custom_call" | custom-call | flops 30000001024 | tf_op jit(solution)/shard_map/pallas_call | solution.py:437
  455.9 3.1 collective-permute-done.41.x_first
  459.5 2.9 shard_map.298
  463.2 2.2 shard_map.302
  466.8 6.1 collective-permute-done.44.kv_far
  473.6 10.1 %shard_map.303 = (bf16[480,2048]{1,0:T(8,128)(2,1)}, f32[1,2048]{1,0:T(1,128)}, bf16[480,256]{1,0:T(8,128)(2,1)}, f32[1,128]{1,0:T(1,128)}) custom-call(s32[3]{0:T(128)} %pad_add_fusion.2.scal, bf16[480,1024]{1,0:T(8,128)(2,1)} %get-tuple-element.242.query_back.first, f32[480,256]{1,0:T(8,128)} %get-tuple-element.254.kv_part, bf16[480,256]{1,0:T(8,128)(2,1)} %copy-done.60, ...), custom_call_target="tpu_custom_call" | custom-call | flops 9799999488 | tf_op jit(solution)/shard_map/pallas_call | solution.py:570
  484.4 7.7 %shard_map.305 = (f32[1024,1280]{1,0:T(8,128)}, bf16[1024,1280]{1,0:T(8,128)(2,1)}) custom-call(s32[3]{0:T(128)} %pad_add_fusion.2.scal, bf16[480,2048]{1,0:T(8,128)(2,1)} %get-tuple-element.266.left_own.left_sent, bf16[480,2048]{1,0:T(8,128)(2,1)} %get-tuple-element.266.left_own.left_sent, bf16[480,1024]{1,0:T(8,128)(2,1)} %get-tuple-element.242.query_back.first, ...), custom_call_target="tpu_custom_call" | custom-call | flops 500000000 | tf_op jit(solution)/shard_map/pallas_call | solution.py:182
  492.2 7.1 %shard_map.313 = (bf16[4608,256]{1,0:T(8,128)(2,1)}, bf16[4608,256]{1,0:T(8,128)(2,1)}) custom-call(bf16[4608,256]{1,0:T(8,128)(2,1)} %get-tuple-element.317.a, bf16[4608,256]{1,0:T(8,128)(2,1)} %collective-permute-done.36.b, bf16[4608,256]{1,0:T(8,128)(2,1)} %get-tuple-element.318.c, bf16[4608,256]{1,0:T(8,128)(2,1)} %collective-permute-done.35.d), custom_call_target="tpu_custom_call" | custom-call | flops 500000000 | tf_op jit(solution)/shard_map/pallas_call | solution.py:791
  503.0 7.7 %shard_map.309 = (f32[1024,1024]{1,0:T(8,128)}, bf16[1024,1024]{1,0:T(8,128)(2,1)}) custom-call(s32[3]{0:T(128)} %pad_add_fusion.2.scal, bf16[480,1024]{1,0:T(8,128)(2,1)} %get-tuple-element.292.mixed.left, bf16[480,2048]{1,0:T(8,128)(2,1)} %get-tuple-element.293.grad.right_own.right_sent, bf16[480,2048]{1,0:T(8,128)(2,1)} %get-tuple-element.293.grad.right_own.right_sent), custom_call_target="tpu_custom_call" | custom-call | flops 500000000 | tf_op jit(solution)/shard_map/pallas_call | solution.py:888
  512.4 13.0 %reduce-scatter.5.cloned.1.call-done.grad_normed = bf16[120,2048]{1,0:T(8,128)(2,1)} async-done(((bf16[480,2048]{1,0:T(8,128)(2,1)}), bf16[120,2048]{1,0:T(8,128)(2,1)}) %reduce-scatter.5.cloned.1.call-update) | async-done | bytes 491536 | tf_op jit(solution)/shard_map/reduce_scatter | solution.py:1287
  525.4 4.2 shard_map.304
  530.0 4.4 shard_map.310
  534.4 18.9 %collective-permute-done.65.x_second = bf16[4608,256]{1,0:T(8,128)(2,1)} collective-permute-done((bf16[4608,256]{1,0:T(8,128)(2,1)}, bf16[4608,256]{1,0:T(8,128)(2,1)}, u32[]{:S(2)}, u32[]{:S(2)}) %collective-permute-start.65) | collective-permute-done | bytes 2359328 | tf_op jit(solution)/shard_map/ppermute | solution.py:44
  555.7 4.9 shard_map.306
  560.6 12.1 %shard_map.314 = (f32[4608,256]{1,0:T(8,128)}, bf16[4608,256]{1,0:T(8,128)(2,1)}) custom-call(s32[3]{0:T(128)} %pad_add_fusion.2.scal, bf16[4608,512]{1,0:T(8,128)(2,1)} %get-tuple-element.315.own, bf16[4608,256]{1,0:T(8,128)(2,1)} %copy-done.6, bf16[4608,256]{1,0:T(8,128)(2,1)} %collective-permute-done.66.y_first, ...), custom_call_target="tpu_custom_call" | custom-call | flops 500000000 | tf_op jit(solution)/shard_map/pallas_call | solution.py:809
  573.6 3.4 collective-permute-done.46
  577.5 3.4 collective-permute-done.47
  580.9 2.5 collective-permute-start.49
  585.7 2.3 collective-permute-done.49
  591.0 7.2 %collective-permute-done.61.d = bf16[1024,128]{1,0:T(8,128)(2,1)S(1)} collective-permute-done((bf16[1024,128]{1,0:T(8,128)(2,1)S(1)}, bf16[1024,128]{1,0:T(8,128)(2,1)S(1)}, u32[]{:S(2)}, u32[]{:S(2)}) %collective-permute-start.61) | collective-permute-done | bytes 262176 | tf_op jit(solution)/shard_map/ppermute | solution.py:44
  599.0 2.2 collective-permute-done.62.b
  601.9 2.0 shard_map.311
  606.9 2.2 shard_map.307
  610.8 2.6 collective-permute-done.63.x_second
  617.5 2.5 shard_map.312
  621.7 2.5 collective-permute-done.56.x_second
  625.4 2.7 shard_map.308
  629.5 7.7 %shard_map.315 = (f32[3072,256]{1,0:T(8,128)}, f32[3072,256]{1,0:T(8,128)}, f32[3072,256]{1,0:T(8,128)}) custom-call(s32[3]{0:T(128)} %pad_add_fusion.2.scal, f32[4608,256]{1,0:T(8,128)} %get-tuple-element.323.refs_0_.refs_1_.refs_2_, f32[4608,256]{1,0:T(8,128)} %get-tuple-element.323.refs_0_.refs_1_.refs_2_, ...), custom_call_target="tpu_custom_call" | custom-call | flops 500000000 | tf_op jit(solution)/shard_map/pallas_call | solution.py:182
  637.2 3.2 copy.84
  (344 shorter events, 82.9 us)
Async XLA Ops:
  7.2 210.4 %all-reduce.5.cloned.1.call-start = ((), (), s32[]{:S(2)}) async-start(), calls=%async_computation.2 | async-start | bytes 3932160 | tf_op jit(solution)/shard_map/psum | solution.py:1228
  12.2 22.3 %collective-permute-start.2 = (bf16[3,8,192,256]{3,2,1,0:T(8,128)(2,1)}, bf16[3,8,192,256]{3,2,1,0:T(8,128)(2,1)}, u32[]{:S(2)}, u32[]{:S(2)}) collective-permute-start(bf16[3,8,192,256]{3,2,1,0:T(8,128)(2,1)} %shard_map.281), channel_id=1, source_target_pairs={{0,4},{4,0},{8,12},{12,8},{1,5},{5,1},{9,13},{13,9},{2,6},{6,2},{1... | collective-permute-start | bytes 7077896 | tf_op jit(solution)/shard_map/ppermute | solution.py:40
  13.6 19.4 %collective-permute-start = (bf16[256,1408]{1,0:T(8,128)(2,1)S(1)}, bf16[256,1408]{1,0:T(8,128)(2,1)S(1)}, u32[]{:S(2)}, u32[]{:S(2)}) collective-permute-start(bf16[256,1408]{1,0:T(8,128)(2,1)S(1)} %concatenate.36.refs_0_.refs_10_), channel_id=1, source_target_pairs={{0,8},{4,12},{8,0},{12,4},{1,9},{5,13},{9,1},{13,5},{2,10},{6,14},... | collective-permute-start | bytes 2162696 | tf_op jit(solution)/shard_map/ppermute | solution.py:44
  16.2 18.3 %collective-permute-start.1 = (bf16[256,1408]{1,0:T(8,128)(2,1)S(1)}, bf16[256,1408]{1,0:T(8,128)(2,1)S(1)}, u32[]{:S(2)}, u32[]{:S(2)}) collective-permute-start(bf16[256,1408]{1,0:T(8,128)(2,1)S(1)} %concatenate.36.refs_0_.refs_10_), channel_id=1, source_target_pairs={{0,16},{16,0},{1,17},{17,1},{2,18},{18,2},{3,19},{19,3},{4,20},{20... | collective-permute-start | bytes 2162696 | tf_op jit(solution)/shard_map/ppermute | solution.py:48
  40.4 9.7 %collective-permute-start.3 = (bf16[128,1408]{1,0:T(8,128)(2,1)S(1)}, bf16[128,1408]{1,0:T(8,128)(2,1)S(1)}, u32[]{:S(2)}, u32[]{:S(2)}) collective-permute-start(bf16[128,1408]{1,0:T(8,128)(2,1)S(1)} %split.12), channel_id=1, source_target_pairs={{0,8},{4,12},{8,0},{12,4},{1,9},{5,13},{9,1},{13,5},{2,10},{6,14},... | collective-permute-start | bytes 1081352 | tf_op jit(solution)/shard_map/ppermute | solution.py:44
  40.8 9.8 %collective-permute-start.4 = (bf16[128,1408]{1,0:T(8,128)(2,1)S(1)}, bf16[128,1408]{1,0:T(8,128)(2,1)S(1)}, u32[]{:S(2)}, u32[]{:S(2)}) collective-permute-start(bf16[128,1408]{1,0:T(8,128)(2,1)S(1)} %split.13), channel_id=1, source_target_pairs={{0,16},{16,0},{1,17},{17,1},{2,18},{18,2},{3,19},{19,3},{4,20},{20... | collective-permute-start | bytes 1081352 | tf_op jit(solution)/shard_map/ppermute | solution.py:48
  50.5 12.6 %collective-permute-start.13 = (bf16[1024,256]{1,0:T(8,128)(2,1)}, bf16[1024,256]{1,0:T(8,128)(2,1)S(1)}, u32[]{:S(2)}, u32[]{:S(2)}) collective-permute-start(bf16[1024,256]{1,0:T(8,128)(2,1)} %refs_0_.7), channel_id=1, source_target_pairs={{0,8},{4,12},{8,0},{12,4},{1,9},{5,13},{9,1},{13,5},{2,10},{6,14},... | collective-permute-start | bytes 1572872 | tf_op jit(solution)/shard_map/ppermute | solution.py:44
  51.9 12.0 %collective-permute-start.14 = (bf16[1024,256]{1,0:T(8,128)(2,1)}, bf16[1024,256]{1,0:T(8,128)(2,1)S(1)}, u32[]{:S(2)}, u32[]{:S(2)}) collective-permute-start(bf16[1024,256]{1,0:T(8,128)(2,1)} %refs_0_.7), channel_id=1, source_target_pairs={{0,16},{16,0},{1,17},{17,1},{2,18},{18,2},{3,19},{19,3},{4,20},{20... | collective-permute-start | bytes 1572872 | tf_op jit(solution)/shard_map/ppermute | solution.py:48
  53.4 12.4 %collective-permute-start.5 = (bf16[256,1408]{1,0:T(8,128)(2,1)S(1)}, bf16[256,1408]{1,0:T(8,128)(2,1)S(1)}, u32[]{:S(2)}, u32[]{:S(2)}) collective-permute-start(bf16[256,1408]{1,0:T(8,128)(2,1)S(1)} %concatenate.36.refs_0_.refs_10_), channel_id=1, source_target_pairs={{0,4},{4,0},{8,12},{12,8},{1,5},{5,1},{9,13},{13,9},{2,6},{6,2},{1... | collective-permute-start | bytes 2162696 | tf_op jit(solution)/shard_map/ppermute | solution.py:40
  53.4 13.5 %collective-permute-start.6 = (bf16[256,1408]{1,0:T(8,128)(2,1)S(1)}, bf16[256,1408]{1,0:T(8,128)(2,1)S(1)}, u32[]{:S(2)}, u32[]{:S(2)}) collective-permute-start(bf16[256,1408]{1,0:T(8,128)(2,1)S(1)} %collective-permute-done.refs_1_.refs_11_), channel_id=1, source_target_pairs={{0,4},{4,0},{8,12},{12,8},{1,5},{5,1},{9,13},{13,9},{2,6},{6,2},{1... | collective-permute-start | bytes 2162696 | tf_op jit(solution)/shard_map/ppermute | solution.py:40
  53.9 14.3 %collective-permute-start.7 = (bf16[256,1408]{1,0:T(8,128)(2,1)S(1)}, bf16[256,1408]{1,0:T(8,128)(2,1)S(1)}, u32[]{:S(2)}, u32[]{:S(2)}) collective-permute-start(bf16[256,1408]{1,0:T(8,128)(2,1)S(1)} %collective-permute-done.1.refs_2_.refs_12_), channel_id=1, source_target_pairs={{0,4},{4,0},{8,12},{12,8},{1,5},{5,1},{9,13},{13,9},{2,6},{6,2},{1... | collective-permute-start | bytes 2162696 | tf_op jit(solution)/shard_map/ppermute | solution.py:40
  65.9 18.1 %collective-permute-start.15 = (bf16[1024,128]{1,0:T(8,128)(2,1)S(1)}, bf16[1024,128]{1,0:T(8,128)(2,1)S(1)}, u32[]{:S(2)}, u32[]{:S(2)}) collective-permute-start(bf16[1024,128]{1,0:T(8,128)(2,1)S(1)} %split.14), channel_id=1, source_target_pairs={{0,8},{4,12},{8,0},{12,4},{1,9},{5,13},{9,1},{13,5},{2,10},{6,14},... | collective-permute-start | bytes 786440 | tf_op jit(solution)/shard_map/ppermute | solution.py:44
  66.9 17.0 %collective-permute-start.16 = (bf16[1024,128]{1,0:T(8,128)(2,1)S(1)}, bf16[1024,128]{1,0:T(8,128)(2,1)S(1)}, u32[]{:S(2)}, u32[]{:S(2)}) collective-permute-start(bf16[1024,128]{1,0:T(8,128)(2,1)S(1)} %split.15), channel_id=1, source_target_pairs={{0,16},{16,0},{1,17},{17,1},{2,18},{18,2},{3,19},{19,3},{4,20},{20... | collective-permute-start | bytes 786440 | tf_op jit(solution)/shard_map/ppermute | solution.py:48
  82.6 7.7 %collective-permute-start.11 = (bf16[480,256]{1,0:T(8,128)(2,1)S(1)}, bf16[480,256]{1,0:T(8,128)(2,1)S(1)}, u32[]{:S(2)}, u32[]{:S(2)}) collective-permute-start(bf16[480,256]{1,0:T(8,128)(2,1)S(1)} %slice.64), channel_id=1, source_target_pairs={{0,8},{4,12},{8,0},{12,4},{1,9},{5,13},{9,1},{13,5},{2,10},{6,14},... | collective-permute-start | bytes 737288 | tf_op jit(solution)/shard_map/ppermute | solution.py:44
  90.4 102.9 %collective-permute-start.22 = (bf16[4608,512]{1,0:T(8,128)(2,1)}, bf16[4608,512]{1,0:T(8,128)(2,1)}, u32[]{:S(2)}, u32[]{:S(2)}) collective-permute-start(bf16[4608,512]{1,0:T(8,128)(2,1)} %shard_map.282.refs_0_.refs_2_.refs_7_.refs_3_.refs_8_.refs_1_), channel_id=1, source_target_pairs={{0,8},{4,12},{8,0},{12,4},{1,9},{5,13},{9,1},{13,5},{2,10},{6,14},... | collective-permute-start | bytes 14155784 | tf_op jit(solution)/shard_map/ppermute | solution.py:44
  91.7 102.8 %collective-permute-start.23 = (bf16[4608,512]{1,0:T(8,128)(2,1)}, bf16[4608,512]{1,0:T(8,128)(2,1)}, u32[]{:S(2)}, u32[]{:S(2)}) collective-permute-start(bf16[4608,512]{1,0:T(8,128)(2,1)} %shard_map.282.refs_0_.refs_2_.refs_7_.refs_3_.refs_8_.refs_1_), channel_id=1, source_target_pairs={{0,16},{16,0},{1,17},{17,1},{2,18},{18,2},{3,19},{19,3},{4,20},{20... | collective-permute-start | bytes 14155784 | tf_op jit(solution)/shard_map/ppermute | solution.py:48
  92.2 6.0 collective-permute-start.17
  97.0 18.0 %collective-permute-start.19 = (bf16[1024,256]{1,0:T(8,128)(2,1)S(1)}, bf16[1024,256]{1,0:T(8,128)(2,1)S(1)}, u32[]{:S(2)}, u32[]{:S(2)}) collective-permute-start(bf16[1024,256]{1,0:T(8,128)(2,1)S(1)} %collective-permute-done.14.refs_2_), channel_id=1, source_target_pairs={{0,4},{4,0},{8,12},{12,8},{1,5},{5,1},{9,13},{13,9},{2,6},{6,2},{1... | collective-permute-start | bytes 1572872 | tf_op jit(solution)/shard_map/ppermute | solution.py:40
  98.2 16.8 %collective-permute-start.20 = (bf16[1024,128]{1,0:T(8,128)(2,1)}, bf16[1024,128]{1,0:T(8,128)(2,1)S(1)}, u32[]{:S(2)}, u32[]{:S(2)}) collective-permute-start(bf16[1024,128]{1,0:T(8,128)(2,1)} %copy-done.51), channel_id=1, source_target_pairs={{0,4},{4,0},{8,12},{12,8},{1,5},{5,1},{9,13},{13,9},{2,6},{6,2},{1... | collective-permute-start | bytes 786440 | tf_op jit(solution)/shard_map/ppermute | solution.py:40
  98.5 16.5 %collective-permute-start.21 = (bf16[1024,128]{1,0:T(8,128)(2,1)S(1)}, bf16[1024,128]{1,0:T(8,128)(2,1)S(1)}, u32[]{:S(2)}, u32[]{:S(2)}) collective-permute-start(bf16[1024,128]{1,0:T(8,128)(2,1)S(1)} %collective-permute-done.15.refs_4_), channel_id=1, source_target_pairs={{0,4},{4,0},{8,12},{12,8},{1,5},{5,1},{9,13},{13,9},{2,6},{6,2},{1... | collective-permute-start | bytes 786440 | tf_op jit(solution)/shard_map/ppermute | solution.py:40
  122.6 277.2 %all-reduce.7.cloned.1.call-start = ((), (), s32[]{:S(2)}) async-start(), calls=%async_computation.3 | async-start | bytes 3932160 | tf_op jit(solution)/shard_map/psum | solution.py:1247
  199.8 17.4 %collective-permute-start.24 = (bf16[1536,256]{1,0:T(8,128)(2,1)S(1)}, bf16[1536,256]{1,0:T(8,128)(2,1)}, u32[]{:S(2)}, u32[]{:S(2)}) collective-permute-start(bf16[1536,256]{1,0:T(8,128)(2,1)S(1)} %get-tuple-element.194), channel_id=1, source_target_pairs={{0,8},{4,12},{8,0},{12,4},{1,9},{5,13},{9,1},{13,5},{2,10},{6,14},... | collective-permute-start | bytes 2359304 | tf_op jit(solution)/shard_map/ppermute | solution.py:44
  200.4 17.2 %collective-permute-start.25 = (bf16[1536,256]{1,0:T(8,128)(2,1)S(1)}, bf16[1536,256]{1,0:T(8,128)(2,1)}, u32[]{:S(2)}, u32[]{:S(2)}) collective-permute-start(bf16[1536,256]{1,0:T(8,128)(2,1)S(1)} %get-tuple-element.195), channel_id=1, source_target_pairs={{0,16},{16,0},{1,17},{17,1},{2,18},{18,2},{3,19},{19,3},{4,20},{20... | collective-permute-start | bytes 2359304 | tf_op jit(solution)/shard_map/ppermute | solution.py:48
  206.0 31.6 %collective-permute-start.29 = (bf16[480,2048]{1,0:T(8,128)(2,1)}, bf16[480,2048]{1,0:T(8,128)(2,1)}, u32[]{:S(2)}, u32[]{:S(2)}) collective-permute-start(bf16[480,2048]{1,0:T(8,128)(2,1)} %shard_map.288.own.cot), channel_id=1, source_target_pairs={{0,4},{4,0},{8,12},{12,8},{1,5},{5,1},{9,13},{13,9},{2,6},{6,2},{1... | collective-permute-start | bytes 5898248 | tf_op jit(solution)/shard_map/ppermute | solution.py:40
  217.6 17.2 %collective-permute-start.27 = (bf16[1536,256]{1,0:T(8,128)(2,1)}, bf16[1536,256]{1,0:T(8,128)(2,1)S(1)}, u32[]{:S(2)}, u32[]{:S(2)}) collective-permute-start(bf16[1536,256]{1,0:T(8,128)(2,1)} %get-tuple-element.203), channel_id=1, source_target_pairs={{0,8},{4,12},{8,0},{12,4},{1,9},{5,13},{9,1},{13,5},{2,10},{6,14},... | collective-permute-start | bytes 2359304 | tf_op jit(solution)/shard_map/ppermute | solution.py:44
  219.0 17.4 %collective-permute-start.28 = (bf16[1536,256]{1,0:T(8,128)(2,1)}, bf16[1536,256]{1,0:T(8,128)(2,1)S(1)}, u32[]{:S(2)}, u32[]{:S(2)}) collective-permute-start(bf16[1536,256]{1,0:T(8,128)(2,1)} %get-tuple-element.204), channel_id=1, source_target_pairs={{0,16},{16,0},{1,17},{17,1},{2,18},{18,2},{3,19},{19,3},{4,20},{20... | collective-permute-start | bytes 2359304 | tf_op jit(solution)/shard_map/ppermute | solution.py:48
  225.9 26.0 %collective-permute-start.26 = (bf16[480,2048]{1,0:T(8,128)(2,1)}, bf16[480,2048]{1,0:T(8,128)(2,1)}, u32[]{:S(2)}, u32[]{:S(2)}) collective-permute-start(bf16[480,2048]{1,0:T(8,128)(2,1)} %get-tuple-element.263.own), channel_id=1, source_target_pairs={{0,4},{4,0},{8,12},{12,8},{1,5},{5,1},{9,13},{13,9},{2,6},{6,2},{1... | collective-permute-start | bytes 5898248 | tf_op jit(solution)/shard_map/ppermute | solution.py:40
  227.0 22.5 %collective-permute-start.30 = (f32[8,480]{1,0:T(8,128)S(1)}, f32[8,480]{1,0:T(8,128)S(1)}, u32[]{:S(2)}, u32[]{:S(2)}) collective-permute-start(f32[8,480]{1,0:T(8,128)S(1)} %get-tuple-element.337), channel_id=1, source_target_pairs={{0,4},{4,0},{8,12},{12,8},{1,5},{5,1},{9,13},{13,9},{2,6},{6,2},{1... | collective-permute-start | bytes 46088 | tf_op jit(solution)/shard_map/ppermute | solution.py:40
  236.4 14.5 %collective-permute-start.31 = (bf16[1536,256]{1,0:T(8,128)(2,1)S(1)}, bf16[1536,256]{1,0:T(8,128)(2,1)S(1)}, u32[]{:S(2)}, u32[]{:S(2)}) collective-permute-start(bf16[1536,256]{1,0:T(8,128)(2,1)S(1)} %get-tuple-element.211), channel_id=1, source_target_pairs={{0,8},{4,12},{8,0},{12,4},{1,9},{5,13},{9,1},{13,5},{2,10},{6,14},... | collective-permute-start | bytes 2359304 | tf_op jit(solution)/shard_map/ppermute | solution.py:44
  236.8 15.2 %collective-permute-start.32 = (bf16[1536,256]{1,0:T(8,128)(2,1)S(1)}, bf16[1536,256]{1,0:T(8,128)(2,1)S(1)}, u32[]{:S(2)}, u32[]{:S(2)}) collective-permute-start(bf16[1536,256]{1,0:T(8,128)(2,1)S(1)} %get-tuple-element.212), channel_id=1, source_target_pairs={{0,16},{16,0},{1,17},{17,1},{2,18},{18,2},{3,19},{19,3},{4,20},{20... | collective-permute-start | bytes 2359304 | tf_op jit(solution)/shard_map/ppermute | solution.py:48
  318.0 141.5 %reduce-scatter.3.cloned.1.call-start = ((), (), s32[]{:S(2)}) async-start(), calls=%async_computation.4 | async-start | bytes 2457600 | tf_op jit(solution)/shard_map/reduce_scatter | solution.py:1264
  354.6 45.2 %collective-permute-start.34 = (bf16[480,2048]{1,0:T(8,128)(2,1)}, bf16[480,2048]{1,0:T(8,128)(2,1)}, u32[]{:S(2)}, u32[]{:S(2)}) collective-permute-start(bf16[480,2048]{1,0:T(8,128)(2,1)} %shard_map.294), channel_id=1, source_target_pairs={{0,4},{4,0},{8,12},{12,8},{1,5},{5,1},{9,13},{13,9},{2,6},{6,2},{1... | collective-permute-start | bytes 5898248 | tf_op jit(solution)/shard_map/ppermute | solution.py:40
  354.7 55.4 %collective-permute-start.35 = (bf16[4608,256]{1,0:T(8,128)(2,1)}, bf16[4608,256]{1,0:T(8,128)(2,1)}, u32[]{:S(2)}, u32[]{:S(2)}) collective-permute-start(bf16[4608,256]{1,0:T(8,128)(2,1)} %get-tuple-element.226), channel_id=1, source_target_pairs={{0,8},{4,12},{8,0},{12,4},{1,9},{5,13},{9,1},{13,5},{2,10},{6,14},... | collective-permute-start | bytes 7077896 | tf_op jit(solution)/shard_map/ppermute | solution.py:44
  355.4 54.7 %collective-permute-start.36 = (bf16[4608,256]{1,0:T(8,128)(2,1)}, bf16[4608,256]{1,0:T(8,128)(2,1)}, u32[]{:S(2)}, u32[]{:S(2)}) collective-permute-start(bf16[4608,256]{1,0:T(8,128)(2,1)} %get-tuple-element.227), channel_id=1, source_target_pairs={{0,16},{16,0},{1,17},{17,1},{2,18},{18,2},{3,19},{19,3},{4,20},{20... | collective-permute-start | bytes 7077896 | tf_op jit(solution)/shard_map/ppermute | solution.py:48
  357.7 6.2 collective-permute-start.38
  360.4 5.7 collective-permute-start.39
  368.2 90.9 %collective-permute-start.41 = (bf16[4608,256]{1,0:T(8,128)(2,1)}, bf16[4608,256]{1,0:T(8,128)(2,1)S(1)}, u32[]{:S(2)}, u32[]{:S(2)}) collective-permute-start(bf16[4608,256]{1,0:T(8,128)(2,1)} %get-tuple-element.247), channel_id=1, source_target_pairs={{0,8},{4,12},{8,0},{12,4},{1,9},{5,13},{9,1},{13,5},{2,10},{6,14},... | collective-permute-start | bytes 7077896 | tf_op jit(solution)/shard_map/ppermute | solution.py:44
  369.6 89.9 %collective-permute-start.42 = (bf16[4608,256]{1,0:T(8,128)(2,1)}, bf16[4608,256]{1,0:T(8,128)(2,1)}, u32[]{:S(2)}, u32[]{:S(2)}) collective-permute-start(bf16[4608,256]{1,0:T(8,128)(2,1)} %get-tuple-element.248), channel_id=1, source_target_pairs={{0,16},{16,0},{1,17},{17,1},{2,18},{18,2},{3,19},{19,3},{4,20},{20... | collective-permute-start | bytes 7077896 | tf_op jit(solution)/shard_map/ppermute | solution.py:48
  410.1 115.2 %reduce-scatter.5.cloned.1.call-start = ((), (), s32[]{:S(2)}) async-start(), calls=%async_computation.6 | async-start | bytes 2457600 | tf_op jit(solution)/shard_map/reduce_scatter | solution.py:1287
  455.8 6.6 %collective-permute-start.43 = (bf16[960,256]{1,0:T(8,128)(2,1)}, bf16[960,256]{1,0:T(8,128)(2,1)S(1)}, u32[]{:S(2)}, u32[]{:S(2)}) collective-permute-start(bf16[960,256]{1,0:T(8,128)(2,1)} %get-tuple-element.253), channel_id=1, source_target_pairs={{0,4},{4,0},{8,12},{12,8},{1,5},{5,1},{9,13},{13,9},{2,6},{6,2},{1... | collective-permute-start | bytes 1474568 | tf_op jit(solution)/shard_map/ppermute | solution.py:40
  465.4 7.5 %collective-permute-start.44 = (bf16[480,256]{1,0:T(8,128)(2,1)}, bf16[480,256]{1,0:T(8,128)(2,1)S(1)}, u32[]{:S(2)}, u32[]{:S(2)}) collective-permute-start(bf16[480,256]{1,0:T(8,128)(2,1)} %get-tuple-element.255), channel_id=1, source_target_pairs={{0,8},{4,12},{8,0},{12,4},{1,9},{5,13},{9,1},{13,5},{2,10},{6,14},... | collective-permute-start | bytes 737288 | tf_op jit(solution)/shard_map/ppermute | solution.py:44
  483.8 136.2 %all-gather.3.cloned.1.call-start = ((), (), s32[]{:S(2)}) async-start(), calls=%async_computation.5 | async-start | bytes 2457600 | tf_op jit(solution)/shard_map/all_gather | solution.py:1266
  484.4 152.8 %all-gather.5.cloned.1.call-start = ((), (), s32[]{:S(2)}) async-start(), calls=%async_computation.7 | async-start | bytes 2457600 | tf_op jit(solution)/shard_map/all_gather | solution.py:1289
  492.1 62.1 %collective-permute-start.51 = (bf16[1024,1280]{1,0:T(8,128)(2,1)}, bf16[1024,1280]{1,0:T(8,128)(2,1)S(1)}, u32[]{:S(2)}, u32[]{:S(2)}) collective-permute-start(bf16[1024,1280]{1,0:T(8,128)(2,1)} %get-tuple-element.269), channel_id=1, source_target_pairs={{0,4},{4,0},{8,12},{12,8},{1,5},{5,1},{9,13},{13,9},{2,6},{6,2},{1... | collective-permute-start | bytes 7864328 | tf_op jit(solution)/shard_map/ppermute | solution.py:40
  499.3 54.0 %collective-permute-start.65 = (bf16[4608,256]{1,0:T(8,128)(2,1)}, bf16[4608,256]{1,0:T(8,128)(2,1)}, u32[]{:S(2)}, u32[]{:S(2)}) collective-permute-start(bf16[4608,256]{1,0:T(8,128)(2,1)} %get-tuple-element.319), channel_id=1, source_target_pairs={{0,8},{4,12},{8,0},{12,4},{1,9},{5,13},{9,1},{13,5},{2,10},{6,14},... | collective-permute-start | bytes 7077896 | tf_op jit(solution)/shard_map/ppermute | solution.py:44
  500.5 53.7 %collective-permute-start.66 = (bf16[4608,256]{1,0:T(8,128)(2,1)}, bf16[4608,256]{1,0:T(8,128)(2,1)}, u32[]{:S(2)}, u32[]{:S(2)}) collective-permute-start(bf16[4608,256]{1,0:T(8,128)(2,1)} %get-tuple-element.320), channel_id=1, source_target_pairs={{0,16},{16,0},{1,17},{17,1},{2,18},{18,2},{3,19},{19,3},{4,20},{20... | collective-permute-start | bytes 7077896 | tf_op jit(solution)/shard_map/ppermute | solution.py:48
  510.7 19.3 %collective-permute-start.58 = (bf16[1024,1024]{1,0:T(8,128)(2,1)}, bf16[1024,1024]{1,0:T(8,128)(2,1)}, u32[]{:S(2)}, u32[]{:S(2)}) collective-permute-start(bf16[1024,1024]{1,0:T(8,128)(2,1)} %get-tuple-element.295), channel_id=1, source_target_pairs={{0,4},{4,0},{8,12},{12,8},{1,5},{5,1},{9,13},{13,9},{2,6},{6,2},{1... | collective-permute-start | bytes 6291464 | tf_op jit(solution)/shard_map/ppermute | solution.py:40
  529.9 42.8 %collective-permute-start.45 = (f32[24,4,256]{2,0,1:T(8,128)S(1)}, f32[24,4,256]{2,0,1:T(8,128)S(1)}, u32[]{:S(2)}, u32[]{:S(2)}) collective-permute-start(f32[24,4,256]{2,0,1:T(8,128)S(1)} %bitcast.62), channel_id=1, source_target_pairs={{0,4},{4,0},{8,12},{12,8},{1,5},{5,1},{9,13},{13,9},{2,6},{6,2},{1... | collective-permute-start | bytes 294920 | tf_op jit(solution)/shard_map/ppermute | solution.py:40
  572.7 55.3 %collective-permute-start.67 = (bf16[4608,256]{1,0:T(8,128)(2,1)}, bf16[4608,256]{1,0:T(8,128)(2,1)S(1)}, u32[]{:S(2)}, u32[]{:S(2)}) collective-permute-start(bf16[4608,256]{1,0:T(8,128)(2,1)} %get-tuple-element.324), channel_id=1, source_target_pairs={{0,4},{4,0},{8,12},{12,8},{1,5},{5,1},{9,13},{13,9},{2,6},{6,2},{1... | collective-permute-start | bytes 7077896 | tf_op jit(solution)/shard_map/ppermute | solution.py:40
  580.9 7.1 %collective-permute-start.49 = (f32[24,256]{1,0:T(8,128)S(1)}, f32[24,256]{1,0:T(8,128)S(1)}, u32[]{:S(2)}, u32[]{:S(2)}) collective-permute-start(f32[24,256]{1,0:T(8,128)S(1)} %fusion.2), channel_id=1, source_target_pairs={{0,2},{1,3},{2,0},{3,1},{4,6},{5,7},{6,4},{7,5},{8,10},{9,11},{10,... | collective-permute-start | bytes 73736 | tf_op jit(solution)/shard_map/ppermute | solution.py:58
  583.3 6.2 collective-permute-start.50
  584.7 5.6 collective-permute-start.48
  585.0 18.9 %collective-permute-start.54 = (bf16[128,1280]{1,0:T(8,128)(2,1)S(1)}, bf16[128,1280]{1,0:T(8,128)(2,1)S(1)}, u32[]{:S(2)}, u32[]{:S(2)}) collective-permute-start(bf16[128,1280]{1,0:T(8,128)(2,1)S(1)} %copy-done.47), channel_id=1, source_target_pairs={{0,8},{4,12},{8,0},{12,4},{1,9},{5,13},{9,1},{13,5},{2,10},{6,14},... | collective-permute-start | bytes 983048 | tf_op jit(solution)/shard_map/ppermute | solution.py:44
  588.0 17.0 %collective-permute-start.55 = (bf16[128,1280]{1,0:T(8,128)(2,1)S(1)}, bf16[128,1280]{1,0:T(8,128)(2,1)S(1)}, u32[]{:S(2)}, u32[]{:S(2)}) collective-permute-start(bf16[128,1280]{1,0:T(8,128)(2,1)S(1)} %copy-done.46), channel_id=1, source_target_pairs={{0,16},{16,0},{1,17},{17,1},{2,18},{18,2},{3,19},{19,3},{4,20},{20... | collective-permute-start | bytes 983048 | tf_op jit(solution)/shard_map/ppermute | solution.py:48
  589.5 8.7 %collective-permute-start.61 = (bf16[1024,128]{1,0:T(8,128)(2,1)S(1)}, bf16[1024,128]{1,0:T(8,128)(2,1)S(1)}, u32[]{:S(2)}, u32[]{:S(2)}) collective-permute-start(bf16[1024,128]{1,0:T(8,128)(2,1)S(1)} %copy-done.57), channel_id=1, source_target_pairs={{0,8},{4,12},{8,0},{12,4},{1,9},{5,13},{9,1},{13,5},{2,10},{6,14},... | collective-permute-start | bytes 786440 | tf_op jit(solution)/shard_map/ppermute | solution.py:44
  590.4 10.8 %collective-permute-start.62 = (bf16[1024,128]{1,0:T(8,128)(2,1)S(1)}, bf16[1024,128]{1,0:T(8,128)(2,1)S(1)}, u32[]{:S(2)}, u32[]{:S(2)}) collective-permute-start(bf16[1024,128]{1,0:T(8,128)(2,1)S(1)} %copy-done.56), channel_id=1, source_target_pairs={{0,16},{16,0},{1,17},{17,1},{2,18},{18,2},{3,19},{19,3},{4,20},{20... | collective-permute-start | bytes 786440 | tf_op jit(solution)/shard_map/ppermute | solution.py:48
  598.3 10.8 %collective-permute-start.59 = (bf16[1024,128]{1,0:T(8,128)(2,1)S(1)}, bf16[1024,128]{1,0:T(8,128)(2,1)S(1)}, u32[]{:S(2)}, u32[]{:S(2)}) collective-permute-start(bf16[1024,128]{1,0:T(8,128)(2,1)S(1)} %copy-done.55), channel_id=1, source_target_pairs={{0,8},{4,12},{8,0},{12,4},{1,9},{5,13},{9,1},{13,5},{2,10},{6,14},... | collective-permute-start | bytes 786440 | tf_op jit(solution)/shard_map/ppermute | solution.py:44
  601.2 9.0 %collective-permute-start.60 = (bf16[1024,128]{1,0:T(8,128)(2,1)S(1)}, bf16[1024,128]{1,0:T(8,128)(2,1)S(1)}, u32[]{:S(2)}, u32[]{:S(2)}) collective-permute-start(bf16[1024,128]{1,0:T(8,128)(2,1)S(1)} %copy-done.54), channel_id=1, source_target_pairs={{0,16},{16,0},{1,17},{17,1},{2,18},{18,2},{3,19},{19,3},{4,20},{20... | collective-permute-start | bytes 786440 | tf_op jit(solution)/shard_map/ppermute | solution.py:48
  603.9 9.5 %collective-permute-start.63 = (bf16[1024,128]{1,0:T(8,128)(2,1)}, bf16[1024,128]{1,0:T(8,128)(2,1)S(1)}, u32[]{:S(2)}, u32[]{:S(2)}) collective-permute-start(bf16[1024,128]{1,0:T(8,128)(2,1)} %get-tuple-element.310), channel_id=1, source_target_pairs={{0,8},{4,12},{8,0},{12,4},{1,9},{5,13},{9,1},{13,5},{2,10},{6,14},... | collective-permute-start | bytes 786440 | tf_op jit(solution)/shard_map/ppermute | solution.py:44
  605.0 10.1 %collective-permute-start.64 = (bf16[1024,128]{1,0:T(8,128)(2,1)}, bf16[1024,128]{1,0:T(8,128)(2,1)S(1)}, u32[]{:S(2)}, u32[]{:S(2)}) collective-permute-start(bf16[1024,128]{1,0:T(8,128)(2,1)} %get-tuple-element.311), channel_id=1, source_target_pairs={{0,16},{16,0},{1,17},{17,1},{2,18},{18,2},{3,19},{19,3},{4,20},{20... | collective-permute-start | bytes 786440 | tf_op jit(solution)/shard_map/ppermute | solution.py:48
  609.1 11.4 %collective-permute-start.52 = (bf16[128,1280]{1,0:T(8,128)(2,1)}, bf16[128,1280]{1,0:T(8,128)(2,1)S(1)}, u32[]{:S(2)}, u32[]{:S(2)}) collective-permute-start(bf16[128,1280]{1,0:T(8,128)(2,1)} %get-tuple-element.273), channel_id=1, source_target_pairs={{0,8},{4,12},{8,0},{12,4},{1,9},{5,13},{9,1},{13,5},{2,10},{6,14},... | collective-permute-start | bytes 983048 | tf_op jit(solution)/shard_map/ppermute | solution.py:44
  610.1 11.6 %collective-permute-start.53 = (bf16[128,1280]{1,0:T(8,128)(2,1)}, bf16[128,1280]{1,0:T(8,128)(2,1)S(1)}, u32[]{:S(2)}, u32[]{:S(2)}) collective-permute-start(bf16[128,1280]{1,0:T(8,128)(2,1)} %get-tuple-element.274), channel_id=1, source_target_pairs={{0,16},{16,0},{1,17},{17,1},{2,18},{18,2},{3,19},{19,3},{4,20},{20... | collective-permute-start | bytes 983048 | tf_op jit(solution)/shard_map/ppermute | solution.py:48
  613.4 10.9 %collective-permute-start.56 = (bf16[128,1280]{1,0:T(8,128)(2,1)}, bf16[128,1280]{1,0:T(8,128)(2,1)S(1)}, u32[]{:S(2)}, u32[]{:S(2)}) collective-permute-start(bf16[128,1280]{1,0:T(8,128)(2,1)} %get-tuple-element.284), channel_id=1, source_target_pairs={{0,8},{4,12},{8,0},{12,4},{1,9},{5,13},{9,1},{13,5},{2,10},{6,14},... | collective-permute-start | bytes 983048 | tf_op jit(solution)/shard_map/ppermute | solution.py:44
  615.1 10.3 %collective-permute-start.57 = (bf16[128,1280]{1,0:T(8,128)(2,1)}, bf16[128,1280]{1,0:T(8,128)(2,1)}, u32[]{:S(2)}, u32[]{:S(2)}) collective-permute-start(bf16[128,1280]{1,0:T(8,128)(2,1)} %get-tuple-element.285), channel_id=1, source_target_pairs={{0,16},{16,0},{1,17},{17,1},{2,18},{18,2},{3,19},{19,3},{4,20},{20... | collective-permute-start | bytes 983048 | tf_op jit(solution)/shard_map/ppermute | solution.py:48
  (80 other events, 774.2 us)
Sparse Core Ops, SparseCore 0:
  122.7 82.3 all-reduce.4
  318.1 81.6 all-reduce.6
  410.3 41.3 reduce-scatter.2
  483.9 41.4 reduce-scatter.4
  526.8 42.8 all-gather.2
  571.1 44.4 all-gather.4

commit v3 on v2

--- a/solution.py
+++ b/solution.py
@@ -109,7 +109,7 @@
     "permute_kernel": 4.6, "half_kernel": 4, "block_kernel": 6, "qkv_kernel": 11.7,
     "attend_kernel": 16.3, "attend_back_kernel": 30, "project_kernel": 6.6, "project_back_kernel": 6.5,
     "kv_pass_kernel": 2, "qkv_back_kernel": 9.8, "products_kernel": 11.8, "experts_kernel": 20,
-    "spread_kernel": 10, "join_kernel": 4.6, "weight_grad_kernel": 50, "met_kernel": 0.5, "total_kernel": 0.5,
+    "spread_kernel": 10, "join_kernel": 1, "weight_grad_kernel": 50, "met_kernel": 0.5, "total_kernel": 0.5,
     "lay_kernel": 0.5, "pair_grad_kernel": 0.5, "columns_grad_kernel": 0.5, "cut_kernel": 0.3, "end_kernel": 0.3,
     "route_kernel": 6.3, "route_back_kernel": 8.6, "add_kernel": 2.2, "last_kernel": 6.2,
 }
@@ -753,6 +753,16 @@
     )(*[acts_t] * len(which), *([] if got is None else [got]), *[a for pieces in weights for a, _ in pieces])
 
 
+def join_kernel(own, other, out):
+    out[...] = rounded(own[...].astype(F32) + other[...].astype(F32))
+
+
+def join_call(own, other):
+    rows, width = own.shape
+    spec = pl.BlockSpec((rows // 3, width), lambda i: (i, 0))
+    return kernel_call(join_kernel, (3,), [spec, spec], spec, sds(own.shape, BF16), 0, 0)(own, other)
+
+
 def weight_grad_kernel(left, first, second, *outs):
     def write(right):
         value = dot(left[0], right[...], (1, 0))
@@ -789,7 +799,13 @@
     steps = 6 if a.shape[0] % 96 == 0 else 1
     left = pl.BlockSpec((a.shape[0] // steps, a.shape[1]), lambda i: (i, 0))
     return kernel_call(
-        met_kernel, (steps,), [left] * 4, [left] * 2, [sds(a.shape, BF16)] * 2, 0, 0
+        met_kernel,
+        (steps,),
+        [left] * 4,
+        [left] * 2,
+        [sds(a.shape, BF16)] * 2,
+        0,
+        0,
     )(a, b, c, d)
 
 
@@ -1166,8 +1182,9 @@
     expert_weights = [down_weight, gate_weight.transpose(0, 2, 1), up_weight.transpose(0, 2, 1)]
     if paired:
         qkv_x, qkv_y = exchange(qkv_shard, qkv_shard)
-        expert_block = block_call(scal, expert_weights, to_core(other_half_call(scal, expert_weights)))
-        far_second, far_first = exchange(halves(qkv_y, 0)[1], halves(qkv_x, 0)[0], expert_block)
+        far_second, far_first = exchange(halves(qkv_y, 0)[1], halves(qkv_x, 0)[0])
+        expert_got = to_core(other_half_call(after(scal, qkv_x), expert_weights))
+        expert_block = block_call(scal, expert_weights, expert_got)
         qkv_pieces, qkv_places = both_cores([qkv_shard, qkv_x, qkv_y, far_first, far_second], shard)
         out_x, out_y = exchange(out_weight, out_weight, far_first, far_second)
         out_far_second, out_far_first = exchange(halves(out_y, 1)[1], halves(out_x, 1)[0])
@@ -1258,12 +1275,10 @@
         x_first, y_second = exchange(x_first, y_second)
         grad_moe_in = after(grad_moe_in, far_x, far_y)
     out_other = to_core(spread_call(acts_t, (0,), 1, [down_pieces], expert_places))
-    out_sum = spread_call(acts_t, (0,), 0, [down_pieces], expert_places, out_other)
+    out_sum = join_call(spread_call(acts_t, (0,), 0, [down_pieces], expert_places), out_other)
     grad_moe_in = after(grad_moe_in, out_sum)
     out_sum = after(out_sum, grad_moe_in, gate_grads)
     moe_add = lax.psum_scatter(out_sum, "tensor", scatter_dimension=0, tiled=True)
-    output_rows = add_call(scal, resid, moe_add, chips)
-    output = lax.all_gather(output_rows, "tensor", axis=0, tiled=True)[None]
 
     grad_resid, resid_low, grad_logits, grad_gain_two = route_back_call(
         grad_moe_in, gate_grads, gates, resid, cot, router_t, gain_two
@@ -1273,26 +1288,28 @@
     query_back, kv_own, kv_sent, kv_mid, grad_gain_q = attend_back_call(
         rot, kv_all, key_side, query_side, grad_mixed, mixed_low, inverse, raw, cosine, sine, gain_q, heads
     )
+    output_rows = add_call(after(scal, query_back), resid, moe_add, chips)
+    output = lax.all_gather(output_rows, "tensor", axis=0, tiled=True)[None]
     if paired:
         kv_mid = after(kv_mid, x_first, y_second)
     kv_part, kv_on = kv_pass_call(kv_own, after(kv_mid, output_rows), to_core(kv_sent))
     kv_far = to_x(kv_on)
     if paired:
-        x_second, y_first = met_call(after(x_second, kv_far), far_y, y_first, far_x)
-        x_second, y_first = exchange(x_second, y_first)
+        x_second, y_first = lax.optimization_barrier(met_call(after(x_second, kv_on), far_y, y_first, far_x))
+        kv_part = after(kv_part, x_second)
+        x_second, y_first = lax.optimization_barrier((to_x(x_second), to_dp(y_first)))
         near_grads = (x_first, y_first, x_second, y_second)
     back_part, grad_gain_one, kv_back, grad_gain_k = qkv_back_call(
         scal, query_back, kv_part, kv_far, raw, cosine, sine, gain_k, tokens_low, qkv_pieces, qkv_places, shard
     )
     grad_normed = lax.psum_scatter(back_part, "tensor", scatter_dimension=0, tiled=True)
-    hidden_rows_out = last_call(scal, tokens_low, grad_resid, grad_normed, gain_one, chips)
-    grad_hidden = lax.all_gather(hidden_rows_out, "tensor", axis=0, tiled=True)[None]
-
     late_resid, late_mixed, late_normed, late_moe = lax.optimization_barrier(
         (resid_low, mixed_low, normed, moe_low, back_part)
     )[:4]
     grad_router_t = dot(grad_logits, late_moe, (0, 0))
     if paired:
+        mine, sent = total_call(scal, own_grads, near_grads)
+        late_normed = after(late_normed, mine)
         qkv_mine, qkv_sent = rows_grad_call(scal, late_normed, query_back, kv_back, shard)
         out_mine, out_sent = columns_grad_call(scal, late_mixed, late_resid, shard)
         qkv_blocks = cut_call(qkv_mine, to_core(qkv_sent), 0)
@@ -1302,14 +1319,13 @@
             own, x_first, x_second, y_first, y_second, far_first, far_second = blocks
             far_x, far_y = exchange(far_first, far_second)
             x_first, y_second = exchange(x_first, y_second)
-            x_second, y_first = exchange(*met_call(x_second, far_y, y_first, far_x))
+            x_second, y_first = met_call(x_second, far_y, y_first, far_x)
+            x_second, y_first = exchange(x_second, y_first)
             near = (x_first, y_first, x_second, y_second)
             return end_call(own, near, axis, lengths)
 
         grad_query, grad_key, grad_value = plane_sum(qkv_blocks, 0, [inner, HEAD, HEAD])
         (grad_out_weight,) = plane_sum(out_blocks, 1, [shard])
-        own_grads = after(own_grads, qkv_blocks[0], out_blocks[0])
-        mine, sent = total_call(scal, own_grads, near_grads)
     else:
         qkv_back = jnp.concatenate([query_back, kv_back], 1)
         sides = [
@@ -1330,6 +1346,11 @@
         v.reshape(EXPERTS, hid, shard) for v in lay_call(scal, mine, to_core(sent))
     )
     grad_gate, grad_up = grad_gate.transpose(0, 2, 1), grad_up.transpose(0, 2, 1)
+
+    if paired:
+        grad_normed = after(grad_normed, qkv_sent)
+    hidden_rows_out = last_call(scal, tokens_low, grad_resid, grad_normed, gain_one, chips)
+    grad_hidden = lax.all_gather(hidden_rows_out, "tensor", axis=0, tiled=True)[None]
 
     share = 1.0 / tensor
     head_rows = jnp.concatenate(

time: 659 us -> 641 us (0.973)
  waiting for transfers between devices: 240 us -> 209 us
    reduce_scatter x1, waiting for transfers between devices: 13 us -> 0.02 us  [shards(): lax.psum_scatter(back_part, 'tensor', scatter_dimension=0, tiled=True)]
    psum x1, waiting for transfers between devices: 27.4 us -> 18 us  [shards(): grad_moe_in = lax.psum(moe_sum, 'tensor')]
    unnamed x148 -> x116, local copies, waits for them, and re-layouts: 14.3 us -> 13.7 us
  transfers between devices with their start and end apart: 74 -> 74, of which waited for: 38 -> 27; matrix products, arithmetic and copies ran while one was open for 3% -> 4% of each run, Pallas kernels for 34% -> 37%
where the time goes in v3:
time: 641 us; the launch traced here: 631 us
  Pallas kernels  308 us (48%)
  waiting for transfers between devices  209 us (33%)
  starting transfers between devices  60 us (9%)
  local copies, waits for them, and re-layouts  29.6 us (5%)
  between operations  15.3 us (2%)
  other arithmetic  7.38 us (1%)
    ppermute x20, waiting for transfers between devices, to_x(): return lax.ppermute(v, 'ctx', [(i, i ^ 2) for i in range(4)])  172 us
    pallas_call x4, Pallas kernels, spread_call(): kernel_call(functools.partial(spread_kernel, tiles, len(which), got is no...  47.5 us
    pallas_call x6, Pallas kernels, prefetch_call(): pl.pallas_call(body, grid_spec=pltpu.PrefetchScalarGridSpec(num_scalar_pr...  32.5 us
    pallas_call x1, Pallas kernels, attend_back_call(): kernel_call(attend_back_kernel, (heads,), [column, pl.BlockSpec((count, H...  30.2 us
    pallas_call x1, Pallas kernels, weight_grad_call(): kernel_call(weight_grad_kernel, (3, 4), [pl.BlockSpec((1, tile, both), la...  27 us
    pallas_call x2, Pallas kernels, products_call(): kernel_call(products_kernel, (4,), [single(own.shape), single(own.shape)]...  23.8 us
    ppermute x20, starting transfers between devices, to_x(): return lax.ppermute(v, 'ctx', [(i, i ^ 2) for i in range(4)])  22.9 us
    ppermute x18, starting transfers between devices, to_dp(): return lax.ppermute(v, 'dp', [(0, 1), (1, 0)])  20.8 us
  transfers between devices with their start and end apart: 74, of which 27 were waited for; matrix products, arithmetic and copies ran while one was open for 4% of the time, Pallas kernels for 37%

profile of v3, /device:TPU:0, one launch (start us, length us, event | category | flops | bytes accessed | tf_op | source)
XLA Modules:
  0.0 630.8 jit_solution(6765271333903216702)
XLA Ops:
  11.7 3.0 collective-permute-start
  16.9 14.0 %collective-permute-done.refs_1_.refs_11_ = bf16[256,1408]{1,0:T(8,128)(2,1)S(1)} collective-permute-done((bf16[256,1408]{1,0:T(8,128)(2,1)S(1)}, bf16[256,1408]{1,0:T(8,128)(2,1)S(1)}, u32[]{:S(2)}, u32[]{:S(2)}) %collective-permute-start) | collective-permute-done | bytes 720928 | tf_op jit(solution)/shard_map/ppermute | solution.py:44
  32.3 4.3 shard_map.284
  37.1 1.7 collective-permute-start.3
  38.8 8.8 %collective-permute-done.2.refs_4_.refs_14_ = bf16[128,1408]{1,0:T(8,128)(2,1)S(1)} collective-permute-done((bf16[128,1408]{1,0:T(8,128)(2,1)S(1)}, bf16[128,1408]{1,0:T(8,128)(2,1)S(1)}, u32[]{:S(2)}, u32[]{:S(2)}) %collective-permute-start.2) | collective-permute-done | bytes 360480 | tf_op jit(solution)/shard_map/ppermute | solution.py:44
  47.7 1.7 collective-permute-start.12
  51.4 10.0 %collective-permute-done.12.refs_1_ = bf16[1024,256]{1,0:T(8,128)(2,1)S(1)} collective-permute-done((bf16[1024,256]{1,0:T(8,128)(2,1)}, bf16[1024,256]{1,0:T(8,128)(2,1)S(1)}, u32[]{:S(2)}, u32[]{:S(2)}) %collective-permute-start.12) | collective-permute-done | bytes 524320 | tf_op jit(solution)/shard_map/ppermute | solution.py:44
  68.0 12.1 %shard_map.281 = (f32[1,2048]{1,0:T(1,128)}, f32[1,2048]{1,0:T(1,128)}, bf16[16,2048]{1,0:T(8,128)(2,1)}, f32[1,128]{1,0:T(1,128)}, f32[1,128]{1,0:T(1,128)}, /*...) custom-call(s32[3]{0:T(128)} %pad_add_fusion.2.scal, ...), custom_call_target="tpu_custom_call" | custom-call | flops 11699999744 | tf_op jit(solution)/shard_map/pallas_call | solution.py:325
  82.4 5.7 shard_map.285.refs_0_.refs_2_.refs_7_.refs_3_.refs_8_.refs_1_
  97.1 16.2 %shard_map.282 = (bf16[480,1024]{1,0:T(8,128)(2,1)}, f32[8,1,480]{2,1,0:T(1,128)}) custom-call(bf16[480,1280]{1,0:T(8,128)(2,1)} %get-tuple-element.183.query, bf16[1920,256]{1,0:T(8,128)(2,1)} %pad_maximum_fusion.keys.values, bf16[1920,256]{1,0:T(8,128)(2,1)} %pad_maximum_fusion.keys.values, s32[1920,2]{1,0:T(8,128)} %copy.68.key_side, ...), custom_call_target="tpu_custom_call" | custom-call | flops 16300000256 | tf_op jit(solution)/shard_map/pallas_call | solution.py:371
  114.5 6.6 %shard_map.283 = bf16[480,2048]{1,0:T(8,128)(2,1)} custom-call(s32[3]{0:T(128)} %pad_add_fusion.2.scal, bf16[480,1024]{1,0:T(8,128)(2,1)} %get-tuple-element.309.mixed.left, bf16[1024,256]{1,0:T(8,128)(2,1)} %refs_0_.7, bf16[1024,256]{1,0:T(8,128)(2,1)} %copy-done.20, bf16[1024,256]{1,0:T(8,128)(2,1)} %copy-done.21, ...), custom_call_target="tpu_custom_call" | custom-call | flops 6600000000 | tf_op jit(solution)/shard_map/pallas_call | solution.py:486
  121.6 70.2 %collective-permute-done.22.refs_1_.refs_3_.refs_8_.refs_4_.refs_9_.refs_2_ = bf16[4608,512]{1,0:T(8,128)(2,1)} collective-permute-done((bf16[4608,512]{1,0:T(8,128)(2,1)}, bf16[4608,512]{1,0:T(8,128)(2,1)}, u32[]{:S(2)}, u32[]{:S(2)}) %collective-permute-start.22) | collective-permute-done | bytes 4718624 | tf_op jit(solution)/shard_map/ppermute | solution.py:44
  193.0 2.6 fusion.6
  195.7 2.6 fusion.7
  199.4 4.6 shard_map.288.own.cot
  204.9 10.9 %collective-permute-done.24.refs_4_.refs_5_ = bf16[1536,256]{1,0:T(8,128)(2,1)} collective-permute-done((bf16[1536,256]{1,0:T(8,128)(2,1)S(1)}, bf16[1536,256]{1,0:T(8,128)(2,1)}, u32[]{:S(2)}, u32[]{:S(2)}) %collective-permute-start.24) | collective-permute-done | bytes 786464 | tf_op jit(solution)/shard_map/ppermute | solution.py:44
  218.1 6.4 %shard_map.286 = (f32[480,2048]{1,0:T(8,128)}, bf16[480,2048]{1,0:T(8,128)(2,1)}, f32[480,16]{1,0:T(8,128)}) custom-call(bf16[480,2048]{1,0:T(8,128)(2,1)} %get-tuple-element.184.hid, bf16[480,2048]{1,0:T(8,128)(2,1)} %all-reduce.5.cloned.1.call-done.attn_add, f32[1,2048]{1,0:T(1,128)} %get-tuple-element.204.gain, ...), custom_call_target="tpu_custom_call" | custom-call | flops 6300000256 | tf_op jit(solution)/shard_map/pallas_call | solution.py:1002
  226.1 7.3 %collective-permute-done.27.refs_4_.refs_6_.refs_7_ = bf16[1536,256]{1,0:T(8,128)(2,1)S(1)} collective-permute-done((bf16[1536,256]{1,0:T(8,128)(2,1)}, bf16[1536,256]{1,0:T(8,128)(2,1)S(1)}, u32[]{:S(2)}, u32[]{:S(2)}) %collective-permute-start.27) | collective-permute-done | bytes 786464 | tf_op jit(solution)/shard_map/ppermute | solution.py:44
  233.3 1.6 collective-permute-done.28.refs_3_.refs_5_.refs_6_
  235.7 11.8 %shard_map.289 = (f32[1536,960]{1,0:T(8,128)}, bf16[960,2048]{1,0:T(8,128)(2,1)}) custom-call(bf16[480,2048]{1,0:T(8,128)(2,1)} %shard_map.288.own.cot, bf16[480,2048]{1,0:T(8,128)(2,1)} %collective-permute-done.29.other, bf16[4608,512]{1,0:T(8,128)(2,1)} %shard_map.285.refs_0_.refs_2_.refs_7_.refs_3_.refs_8_.refs_1_, ...), custom_call_target="tpu_custom_call" | custom-call | flops 11800000512 | tf_op jit(solution)/shard_map/pallas_call | solution.py:620
  250.4 12.0 %shard_map.287 = (f32[1536,960]{1,0:T(8,128)}, bf16[960,2048]{1,0:T(8,128)(2,1)}) custom-call(bf16[480,2048]{1,0:T(8,128)(2,1)} %get-tuple-element.283.own, bf16[480,2048]{1,0:T(8,128)(2,1)} %collective-permute-done.26.other, bf16[4608,512]{1,0:T(8,128)(2,1)} %shard_map.285.refs_0_.refs_2_.refs_7_.refs_3_.refs_8_.refs_1_, ...), custom_call_target="tpu_custom_call" | custom-call | flops 11800000512 | tf_op jit(solution)/shard_map/pallas_call | solution.py:620
  262.5 20.0 %shard_map.290 = (bf16[3,1536,960]{2,1,0:T(8,128)(2,1)}, bf16[3,960,1536]{2,1,0:T(8,128)(2,1)}, f32[8,1,960]{2,1,0:T(1,128)}) custom-call(bf16[960,2048]{1,0:T(8,128)(2,1)} %get-tuple-element.211.both.second, f32[1536,960]{1,0:T(8,128)} %get-tuple-element.212.gate_ref, f32[1536,960]{1,0:T(8,128)} %get-tuple-element.213.grad_act, ...), custom_call_target="tpu_custom_call" | custom-call | flops 20000000000 | tf_op jit(solution)/shard_map/pallas_call | solution.py:661
  282.5 14.1 %shard_map.291 = bf16[480,2048]{1,0:T(8,128)(2,1)} custom-call(bf16[3,960,1536]{2,1,0:T(8,128)(2,1)} %get-tuple-element.234.refs_0_.refs_1_, bf16[3,960,1536]{2,1,0:T(8,128)(2,1)} %get-tuple-element.234.refs_0_.refs_1_, bf16[4608,512]{1,0:T(8,128)(2,1)} %shard_map.285.refs_0_.refs_2_.refs_7_.refs_3_.refs_8_.refs_1_, ...), custom_call_target="tpu_custom_call" | custom-call | flops 10000000000 | tf_op jit(solution)/shard_map/pallas_call | solution.py:740
  296.6 4.2 collective-permute-done.33.refs_2_
  302.1 14.6 %shard_map.292 = bf16[480,2048]{1,0:T(8,128)(2,1)} custom-call(bf16[3,960,1536]{2,1,0:T(8,128)(2,1)} %get-tuple-element.234.refs_0_.refs_1_, bf16[3,960,1536]{2,1,0:T(8,128)(2,1)} %get-tuple-element.234.refs_0_.refs_1_, bf16[480,2048]{1,0:T(8,128)(2,1)} %copy-done.9, bf16[4608,512]{1,0:T(8,128)(2,1)} %shard_map.285.refs_0_.refs_2_.refs_7_.refs_3_.refs_8_.refs_1_, ...), custom_call_target="tpu_custom_call" | custom-call | flops 10000000000 | tf_op jit(solution)/shard_map/pallas_call | solution.py:740
  316.7 27.0 %shard_map.293 = (bf16[4608,512]{1,0:T(8,128)(2,1)}, bf16[4608,256]{1,0:T(8,128)(2,1)}, bf16[4608,256]{1,0:T(8,128)(2,1)}, bf16[4608,256]{1,0:T(8,128)(2,1)}, bf...) custom-call(bf16[3,1536,960]{2,1,0:T(8,128)(2,1)} %get-tuple-element.222.left, ...), custom_call_target="tpu_custom_call" | custom-call | flops 49999998976 | tf_op jit(solution)/shard_map/pallas_call | solution.py:782
  345.1 9.4 %shard_map.295 = bf16[480,2048]{1,0:T(8,128)(2,1)} custom-call(bf16[3,960,1536]{2,1,0:T(8,128)(2,1)} %get-tuple-element.234.refs_0_.refs_1_, bf16[4608,512]{1,0:T(8,128)(2,1)} %shard_map.285.refs_0_.refs_2_.refs_7_.refs_3_.refs_8_.refs_1_, bf16[4608,512]{1,0:T(8,128)(2,1)} %collective-permute-done.22.refs_1_.refs_3_.refs_8_.refs_4_.refs_9_.refs_2_, ...), custom_call_target="tpu_custom_call" | custom-call | flops 10000000000 | tf_op jit(solution)/shard_map/pallas_call | solution.py:740
  354.6 1.6 collective-permute-start.37
  356.1 2.6 collective-permute-start.38
  358.8 3.3 collective-permute-start.39
  362.1 2.4 collective-permute-done.39.fourth
  366.6 9.5 %shard_map.294.own = bf16[480,2048]{1,0:T(8,128)(2,1)} custom-call(bf16[3,960,1536]{2,1,0:T(8,128)(2,1)} %get-tuple-element.234.refs_0_.refs_1_, bf16[4608,512]{1,0:T(8,128)(2,1)} %shard_map.285.refs_0_.refs_2_.refs_7_.refs_3_.refs_8_.refs_1_, bf16[4608,512]{1,0:T(8,128)(2,1)} %collective-permute-done.22.refs_1_.refs_3_.refs_8_.refs_4_.refs_9_.refs_2_, ...), custom_call_target="tpu_custom_call" | custom-call | flops 10000000000 | tf_op jit(solution)/shard_map/pallas_call | solution.py:740
  377.2 1.6 collective-permute-start.42
  378.7 1.6 shard_map.298.gate_grads
  380.3 18.0 %all-reduce.7.cloned.1.call-done.grad_moe = bf16[480,2048]{1,0:T(8,128)(2,1)} async-done(((bf16[480,2048]{1,0:T(8,128)(2,1)}), bf16[480,2048]{1,0:T(8,128)(2,1)}) %all-reduce.7.cloned.1.call-update) | async-done | bytes 1966096 | tf_op jit(solution)/shard_map/psum | solution.py:1264
  398.4 4.3 shard_map.296
  402.7 9.3 %shard_map.299 = (f32[480,2048]{1,0:T(8,128)}, bf16[480,2048]{1,0:T(8,128)(2,1)}, bf16[480,16]{1,0:T(8,128)(2,1)}, f32[1,2048]{1,0:T(1,128)}) custom-call(bf16[480,2048]{1,0:T(8,128)(2,1)} %all-reduce.7.cloned.1.call-done.grad_moe, f32[480,16]{1,0:T(8,128)} %shard_map.298.gate_grads, f32[480,16]{1,0:T(8,128)} %get-tuple-element.214.gates, ...), custom_call_target="tpu_custom_call" | custom-call | flops 8600000512 | tf_op jit(solution)/shard_map/pallas_call | solution.py:1047
  412.1 6.5 %shard_map.300.grad = bf16[480,1024]{1,0:T(8,128)(2,1)} custom-call(s32[3]{0:T(128)} %pad_add_fusion.2.scal, bf16[480,2048]{1,0:T(8,128)(2,1)} %get-tuple-element.310.grad.right_own.right_sent, bf16[1024,256]{1,0:T(8,128)(2,1)} %refs_0_.7, bf16[1024,256]{1,0:T(8,128)(2,1)} %copy-done.20, bf16[1024,256]{1,0:T(8,128)(2,1)} %copy-done.21, ...), custom_call_target="tpu_custom_call" | custom-call | flops 6499999744 | tf_op jit(solution)/shard_map/pallas_call | solution.py:508
  418.5 30.2 %shard_map.301 = (bf16[480,1024]{1,0:T(8,128)(2,1)}, f32[480,256]{1,0:T(8,128)}, bf16[960,256]{1,0:T(8,128)(2,1)}, f32[480,256]{1,0:T(8,128)}, f32[1,128]{1,0:T(1,128)}) custom-call(bf16[480,1280]{1,0:T(8,128)(2,1)} %get-tuple-element.183.query, bf16[1920,256]{1,0:T(8,128)(2,1)} %pad_maximum_fusion.keys.values, ...), custom_call_target="tpu_custom_call" | custom-call | flops 30000001024 | tf_op jit(solution)/shard_map/pallas_call | solution.py:437
  448.9 3.0 shard_map.302
  452.7 2.2 shard_map.303
  456.3 7.1 %shard_map.304 = (bf16[4608,256]{1,0:T(8,128)(2,1)}, bf16[4608,256]{1,0:T(8,128)(2,1)}) custom-call(bf16[4608,256]{1,0:T(8,128)(2,1)} %get-tuple-element.263.a, bf16[4608,256]{1,0:T(8,128)(2,1)} %collective-permute-done.35.b, bf16[4608,256]{1,0:T(8,128)(2,1)} %get-tuple-element.264.c, bf16[4608,256]{1,0:T(8,128)(2,1)} %collective-permute-done.34.d), custom_call_target="tpu_custom_call" | custom-call | flops 500000000 | tf_op jit(solution)/shard_map/pallas_call | solution.py:801
  464.1 10.0 %shard_map.305 = (bf16[480,2048]{1,0:T(8,128)(2,1)}, f32[1,2048]{1,0:T(1,128)}, bf16[480,256]{1,0:T(8,128)(2,1)}, f32[1,128]{1,0:T(1,128)}) custom-call(s32[3]{0:T(128)} %pad_add_fusion.2.scal, bf16[480,1024]{1,0:T(8,128)(2,1)} %get-tuple-element.246.query_back.first, f32[480,256]{1,0:T(8,128)} %get-tuple-element.266.kv_part, bf16[480,256]{1,0:T(8,128)(2,1)} %copy-done.46, ...), custom_call_target="tpu_custom_call" | custom-call | flops 9799999488 | tf_op jit(solution)/shard_map/pallas_call | solution.py:570
  478.6 8.0 %shard_map.312 = (f32[1024,1024]{1,0:T(8,128)}, bf16[1024,1024]{1,0:T(8,128)(2,1)}) custom-call(s32[3]{0:T(128)} %pad_add_fusion.2.scal, bf16[480,1024]{1,0:T(8,128)(2,1)} %get-tuple-element.309.mixed.left, bf16[480,2048]{1,0:T(8,128)(2,1)} %get-tuple-element.310.grad.right_own.right_sent, bf16[480,2048]{1,0:T(8,128)(2,1)} %get-tuple-element.310.grad.right_own.right_sent), custom_call_target="tpu_custom_call" | custom-call | flops 500000000 | tf_op jit(solution)/shard_map/pallas_call | solution.py:904
  487.6 2.0 convolution_multiply_fusion
  489.6 38.2 %collective-permute-done.45.x_second = bf16[4608,256]{1,0:T(8,128)(2,1)S(1)} collective-permute-done((bf16[4608,256]{1,0:T(8,128)(2,1)}, bf16[4608,256]{1,0:T(8,128)(2,1)S(1)}, u32[]{:S(2)}, u32[]{:S(2)}) %collective-permute-start.45) | collective-permute-done | bytes 2359328 | tf_op jit(solution)/shard_map/ppermute | solution.py:44
  529.2 12.0 %shard_map.306 = (f32[4608,256]{1,0:T(8,128)}, bf16[4608,256]{1,0:T(8,128)(2,1)}) custom-call(s32[3]{0:T(128)} %pad_add_fusion.2.scal, bf16[4608,512]{1,0:T(8,128)(2,1)} %get-tuple-element.224.own, bf16[4608,256]{1,0:T(8,128)(2,1)} %copy-done.5, bf16[4608,256]{1,0:T(8,128)(2,1)} %collective-permute-done.46.y_first, bf16[4608,256]{1,0:T(8,128)(2,1)} %copy-done.6, ...), custom_call_target="tpu_custom_call" | custom-call | flops 500000000 | tf_op jit(solution)/shard_map/pallas_call | solution.py:825
  541.2 7.6 %shard_map.307 = (f32[1024,1280]{1,0:T(8,128)}, bf16[1024,1280]{1,0:T(8,128)(2,1)}) custom-call(s32[3]{0:T(128)} %pad_add_fusion.2.scal, bf16[480,2048]{1,0:T(8,128)(2,1)} %get-tuple-element.275.left_own.left_sent, bf16[480,2048]{1,0:T(8,128)(2,1)} %get-tuple-element.275.left_own.left_sent, bf16[480,1024]{1,0:T(8,128)(2,1)} %get-tuple-element.246.query_back.first, ...), custom_call_target="tpu_custom_call" | custom-call | flops 500000000 | tf_op jit(solution)/shard_map/pallas_call | solution.py:182
  549.7 4.2 shard_map.308
  556.8 3.1 collective-permute-done.48
  559.9 1.5 collective-permute-start.49
  561.5 2.4 collective-permute-done.49
  563.8 1.9 collective-permute-start.51
  565.7 2.5 collective-permute-start.52
  568.2 4.8 shard_map.309
  575.6 4.3 shard_map.313
  581.5 5.1 collective-permute-done.63.d
  588.8 2.0 shard_map.314
  593.3 2.2 shard_map.310
  596.5 1.5 collective-permute-start.55
  598.0 2.6 collective-permute-done.65.x_second
  604.8 2.5 shard_map.315
  608.7 7.7 %shard_map.316 = (f32[3072,256]{1,0:T(8,128)}, f32[3072,256]{1,0:T(8,128)}, f32[3072,256]{1,0:T(8,128)}) custom-call(s32[3]{0:T(128)} %pad_add_fusion.2.scal, f32[4608,256]{1,0:T(8,128)} %get-tuple-element.274.refs_0_.refs_1_.refs_2_, f32[4608,256]{1,0:T(8,128)} %get-tuple-element.274.refs_0_.refs_1_.refs_2_, ...), custom_call_target="tpu_custom_call" | custom-call | flops 500000000 | tf_op jit(solution)/shard_map/pallas_call | solution.py:182
  617.4 2.7 shard_map.311
  (313 shorter events, 80.2 us)
Async XLA Ops:
  7.2 210.9 %all-reduce.5.cloned.1.call-start = ((), (), s32[]{:S(2)}) async-start(), calls=%async_computation.2 | async-start | bytes 3932160 | tf_op jit(solution)/shard_map/psum | solution.py:1245
  11.7 19.1 %collective-permute-start = (bf16[256,1408]{1,0:T(8,128)(2,1)S(1)}, bf16[256,1408]{1,0:T(8,128)(2,1)S(1)}, u32[]{:S(2)}, u32[]{:S(2)}) collective-permute-start(bf16[256,1408]{1,0:T(8,128)(2,1)S(1)} %concatenate.36.refs_0_.refs_10_), channel_id=1, source_target_pairs={{0,8},{4,12},{8,0},{12,4},{1,9},{5,13},{9,1},{13,5},{2,10},{6,14},... | collective-permute-start | bytes 2162696 | tf_op jit(solution)/shard_map/ppermute | solution.py:44
  14.7 17.6 %collective-permute-start.1 = (bf16[256,1408]{1,0:T(8,128)(2,1)S(1)}, bf16[256,1408]{1,0:T(8,128)(2,1)S(1)}, u32[]{:S(2)}, u32[]{:S(2)}) collective-permute-start(bf16[256,1408]{1,0:T(8,128)(2,1)S(1)} %concatenate.36.refs_0_.refs_10_), channel_id=1, source_target_pairs={{0,16},{16,0},{1,17},{17,1},{2,18},{18,2},{3,19},{19,3},{4,20},{20... | collective-permute-start | bytes 2162696 | tf_op jit(solution)/shard_map/ppermute | solution.py:48
  16.2 34.6 %collective-permute-start.4 = (bf16[256,1408]{1,0:T(8,128)(2,1)S(1)}, bf16[256,1408]{1,0:T(8,128)(2,1)}, u32[]{:S(2)}, u32[]{:S(2)}) collective-permute-start(bf16[256,1408]{1,0:T(8,128)(2,1)S(1)} %concatenate.36.refs_0_.refs_10_), channel_id=1, source_target_pairs={{0,4},{4,0},{8,12},{12,8},{1,5},{5,1},{9,13},{13,9},{2,6},{6,2},{1... | collective-permute-start | bytes 2162696 | tf_op jit(solution)/shard_map/ppermute | solution.py:40
  36.6 45.8 %collective-permute-start.21 = (bf16[3,8,192,256]{3,2,1,0:T(8,128)(2,1)}, bf16[3,8,192,256]{3,2,1,0:T(8,128)(2,1)}, u32[]{:S(2)}, u32[]{:S(2)}) collective-permute-start(bf16[3,8,192,256]{3,2,1,0:T(8,128)(2,1)} %shard_map.284), channel_id=1, source_target_pairs={{0,4},{4,0},{8,12},{12,8},{1,5},{5,1},{9,13},{13,9},{2,6},{6,2},{1... | collective-permute-start | bytes 7077896 | tf_op jit(solution)/shard_map/ppermute | solution.py:40
  36.7 10.9 %collective-permute-start.2 = (bf16[128,1408]{1,0:T(8,128)(2,1)S(1)}, bf16[128,1408]{1,0:T(8,128)(2,1)S(1)}, u32[]{:S(2)}, u32[]{:S(2)}) collective-permute-start(bf16[128,1408]{1,0:T(8,128)(2,1)S(1)} %split.12), channel_id=1, source_target_pairs={{0,8},{4,12},{8,0},{12,4},{1,9},{5,13},{9,1},{13,5},{2,10},{6,14},... | collective-permute-start | bytes 1081352 | tf_op jit(solution)/shard_map/ppermute | solution.py:44
  37.1 10.5 %collective-permute-start.3 = (bf16[128,1408]{1,0:T(8,128)(2,1)S(1)}, bf16[128,1408]{1,0:T(8,128)(2,1)S(1)}, u32[]{:S(2)}, u32[]{:S(2)}) collective-permute-start(bf16[128,1408]{1,0:T(8,128)(2,1)S(1)} %split.13), channel_id=1, source_target_pairs={{0,16},{16,0},{1,17},{17,1},{2,18},{18,2},{3,19},{19,3},{4,20},{20... | collective-permute-start | bytes 1081352 | tf_op jit(solution)/shard_map/ppermute | solution.py:48
  47.7 13.8 %collective-permute-start.12 = (bf16[1024,256]{1,0:T(8,128)(2,1)}, bf16[1024,256]{1,0:T(8,128)(2,1)S(1)}, u32[]{:S(2)}, u32[]{:S(2)}) collective-permute-start(bf16[1024,256]{1,0:T(8,128)(2,1)} %refs_0_.7), channel_id=1, source_target_pairs={{0,8},{4,12},{8,0},{12,4},{1,9},{5,13},{9,1},{13,5},{2,10},{6,14},... | collective-permute-start | bytes 1572872 | tf_op jit(solution)/shard_map/ppermute | solution.py:44
  49.3 13.2 %collective-permute-start.13 = (bf16[1024,256]{1,0:T(8,128)(2,1)}, bf16[1024,256]{1,0:T(8,128)(2,1)S(1)}, u32[]{:S(2)}, u32[]{:S(2)}) collective-permute-start(bf16[1024,256]{1,0:T(8,128)(2,1)} %refs_0_.7), channel_id=1, source_target_pairs={{0,16},{16,0},{1,17},{17,1},{2,18},{18,2},{3,19},{19,3},{4,20},{20... | collective-permute-start | bytes 1572872 | tf_op jit(solution)/shard_map/ppermute | solution.py:48
  50.9 16.0 %collective-permute-start.5 = (bf16[256,1408]{1,0:T(8,128)(2,1)S(1)}, bf16[256,1408]{1,0:T(8,128)(2,1)S(1)}, u32[]{:S(2)}, u32[]{:S(2)}) collective-permute-start(bf16[256,1408]{1,0:T(8,128)(2,1)S(1)} %collective-permute-done.refs_1_.refs_11_), channel_id=1, source_target_pairs={{0,4},{4,0},{8,12},{12,8},{1,5},{5,1},{9,13},{13,9},{2,6},{6,2},{1... | collective-permute-start | bytes 2162696 | tf_op jit(solution)/shard_map/ppermute | solution.py:40
  50.9 16.0 %collective-permute-start.6 = (bf16[256,1408]{1,0:T(8,128)(2,1)S(1)}, bf16[256,1408]{1,0:T(8,128)(2,1)S(1)}, u32[]{:S(2)}, u32[]{:S(2)}) collective-permute-start(bf16[256,1408]{1,0:T(8,128)(2,1)S(1)} %collective-permute-done.1.refs_2_.refs_12_), channel_id=1, source_target_pairs={{0,4},{4,0},{8,12},{12,8},{1,5},{5,1},{9,13},{13,9},{2,6},{6,2},{1... | collective-permute-start | bytes 2162696 | tf_op jit(solution)/shard_map/ppermute | solution.py:40
  64.5 17.9 %collective-permute-start.14 = (bf16[1024,128]{1,0:T(8,128)(2,1)S(1)}, bf16[1024,128]{1,0:T(8,128)(2,1)S(1)}, u32[]{:S(2)}, u32[]{:S(2)}) collective-permute-start(bf16[1024,128]{1,0:T(8,128)(2,1)S(1)} %split.14), channel_id=1, source_target_pairs={{0,8},{4,12},{8,0},{12,4},{1,9},{5,13},{9,1},{13,5},{2,10},{6,14},... | collective-permute-start | bytes 786440 | tf_op jit(solution)/shard_map/ppermute | solution.py:44
  65.4 17.0 %collective-permute-start.15 = (bf16[1024,128]{1,0:T(8,128)(2,1)S(1)}, bf16[1024,128]{1,0:T(8,128)(2,1)}, u32[]{:S(2)}, u32[]{:S(2)}) collective-permute-start(bf16[1024,128]{1,0:T(8,128)(2,1)S(1)} %split.15), channel_id=1, source_target_pairs={{0,16},{16,0},{1,17},{17,1},{2,18},{18,2},{3,19},{19,3},{4,20},{20... | collective-permute-start | bytes 786440 | tf_op jit(solution)/shard_map/ppermute | solution.py:48
  81.1 7.7 %collective-permute-start.10 = (bf16[480,256]{1,0:T(8,128)(2,1)S(1)}, bf16[480,256]{1,0:T(8,128)(2,1)S(1)}, u32[]{:S(2)}, u32[]{:S(2)}) collective-permute-start(bf16[480,256]{1,0:T(8,128)(2,1)S(1)} %slice.64), channel_id=1, source_target_pairs={{0,8},{4,12},{8,0},{12,4},{1,9},{5,13},{9,1},{13,5},{2,10},{6,14},... | collective-permute-start | bytes 737288 | tf_op jit(solution)/shard_map/ppermute | solution.py:44
  88.8 103.0 %collective-permute-start.22 = (bf16[4608,512]{1,0:T(8,128)(2,1)}, bf16[4608,512]{1,0:T(8,128)(2,1)}, u32[]{:S(2)}, u32[]{:S(2)}) collective-permute-start(bf16[4608,512]{1,0:T(8,128)(2,1)} %shard_map.285.refs_0_.refs_2_.refs_7_.refs_3_.refs_8_.refs_1_), channel_id=1, source_target_pairs={{0,8},{4,12},{8,0},{12,4},{1,9},{5,13},{9,1},{13,5},{2,10},{6,14},... | collective-permute-start | bytes 14155784 | tf_op jit(solution)/shard_map/ppermute | solution.py:44
  90.2 102.8 %collective-permute-start.23 = (bf16[4608,512]{1,0:T(8,128)(2,1)}, bf16[4608,512]{1,0:T(8,128)(2,1)}, u32[]{:S(2)}, u32[]{:S(2)}) collective-permute-start(bf16[4608,512]{1,0:T(8,128)(2,1)} %shard_map.285.refs_0_.refs_2_.refs_7_.refs_3_.refs_8_.refs_1_), channel_id=1, source_target_pairs={{0,16},{16,0},{1,17},{17,1},{2,18},{18,2},{3,19},{19,3},{4,20},{20... | collective-permute-start | bytes 14155784 | tf_op jit(solution)/shard_map/ppermute | solution.py:48
  90.7 5.8 collective-permute-start.16
  95.4 18.0 %collective-permute-start.17 = (bf16[1024,256]{1,0:T(8,128)(2,1)S(1)}, bf16[1024,256]{1,0:T(8,128)(2,1)S(1)}, u32[]{:S(2)}, u32[]{:S(2)}) collective-permute-start(bf16[1024,256]{1,0:T(8,128)(2,1)S(1)} %collective-permute-done.12.refs_1_), channel_id=1, source_target_pairs={{0,4},{4,0},{8,12},{12,8},{1,5},{5,1},{9,13},{13,9},{2,6},{6,2},{1... | collective-permute-start | bytes 1572872 | tf_op jit(solution)/shard_map/ppermute | solution.py:40
  96.5 16.9 %collective-permute-start.18 = (bf16[1024,256]{1,0:T(8,128)(2,1)S(1)}, bf16[1024,256]{1,0:T(8,128)(2,1)S(1)}, u32[]{:S(2)}, u32[]{:S(2)}) collective-permute-start(bf16[1024,256]{1,0:T(8,128)(2,1)S(1)} %collective-permute-done.13.refs_2_), channel_id=1, source_target_pairs={{0,4},{4,0},{8,12},{12,8},{1,5},{5,1},{9,13},{13,9},{2,6},{6,2},{1... | collective-permute-start | bytes 1572872 | tf_op jit(solution)/shard_map/ppermute | solution.py:40
  97.0 16.4 %collective-permute-start.20 = (bf16[1024,128]{1,0:T(8,128)(2,1)S(1)}, bf16[1024,128]{1,0:T(8,128)(2,1)S(1)}, u32[]{:S(2)}, u32[]{:S(2)}) collective-permute-start(bf16[1024,128]{1,0:T(8,128)(2,1)S(1)} %collective-permute-done.14.refs_4_), channel_id=1, source_target_pairs={{0,4},{4,0},{8,12},{12,8},{1,5},{5,1},{9,13},{13,9},{2,6},{6,2},{1... | collective-permute-start | bytes 786440 | tf_op jit(solution)/shard_map/ppermute | solution.py:40
  121.1 277.2 %all-reduce.7.cloned.1.call-start = ((), (), s32[]{:S(2)}) async-start(), calls=%async_computation.3 | async-start | bytes 3932160 | tf_op jit(solution)/shard_map/psum | solution.py:1264
  198.3 17.5 %collective-permute-start.24 = (bf16[1536,256]{1,0:T(8,128)(2,1)S(1)}, bf16[1536,256]{1,0:T(8,128)(2,1)}, u32[]{:S(2)}, u32[]{:S(2)}) collective-permute-start(bf16[1536,256]{1,0:T(8,128)(2,1)S(1)} %get-tuple-element.199), channel_id=1, source_target_pairs={{0,8},{4,12},{8,0},{12,4},{1,9},{5,13},{9,1},{13,5},{2,10},{6,14},... | collective-permute-start | bytes 2359304 | tf_op jit(solution)/shard_map/ppermute | solution.py:44
  198.9 17.2 %collective-permute-start.25 = (bf16[1536,256]{1,0:T(8,128)(2,1)S(1)}, bf16[1536,256]{1,0:T(8,128)(2,1)}, u32[]{:S(2)}, u32[]{:S(2)}) collective-permute-start(bf16[1536,256]{1,0:T(8,128)(2,1)S(1)} %get-tuple-element.200), channel_id=1, source_target_pairs={{0,16},{16,0},{1,17},{17,1},{2,18},{18,2},{3,19},{19,3},{4,20},{20... | collective-permute-start | bytes 2359304 | tf_op jit(solution)/shard_map/ppermute | solution.py:48
  204.0 31.7 %collective-permute-start.29 = (bf16[480,2048]{1,0:T(8,128)(2,1)}, bf16[480,2048]{1,0:T(8,128)(2,1)}, u32[]{:S(2)}, u32[]{:S(2)}) collective-permute-start(bf16[480,2048]{1,0:T(8,128)(2,1)} %shard_map.288.own.cot), channel_id=1, source_target_pairs={{0,4},{4,0},{8,12},{12,8},{1,5},{5,1},{9,13},{13,9},{2,6},{6,2},{1... | collective-permute-start | bytes 5898248 | tf_op jit(solution)/shard_map/ppermute | solution.py:40
  216.1 17.2 %collective-permute-start.27 = (bf16[1536,256]{1,0:T(8,128)(2,1)}, bf16[1536,256]{1,0:T(8,128)(2,1)S(1)}, u32[]{:S(2)}, u32[]{:S(2)}) collective-permute-start(bf16[1536,256]{1,0:T(8,128)(2,1)} %get-tuple-element.207), channel_id=1, source_target_pairs={{0,8},{4,12},{8,0},{12,4},{1,9},{5,13},{9,1},{13,5},{2,10},{6,14},... | collective-permute-start | bytes 2359304 | tf_op jit(solution)/shard_map/ppermute | solution.py:44
  217.5 17.4 %collective-permute-start.28 = (bf16[1536,256]{1,0:T(8,128)(2,1)}, bf16[1536,256]{1,0:T(8,128)(2,1)S(1)}, u32[]{:S(2)}, u32[]{:S(2)}) collective-permute-start(bf16[1536,256]{1,0:T(8,128)(2,1)} %get-tuple-element.208), channel_id=1, source_target_pairs={{0,16},{16,0},{1,17},{17,1},{2,18},{18,2},{3,19},{19,3},{4,20},{20... | collective-permute-start | bytes 2359304 | tf_op jit(solution)/shard_map/ppermute | solution.py:48
  224.5 26.0 %collective-permute-start.26 = (bf16[480,2048]{1,0:T(8,128)(2,1)}, bf16[480,2048]{1,0:T(8,128)(2,1)}, u32[]{:S(2)}, u32[]{:S(2)}) collective-permute-start(bf16[480,2048]{1,0:T(8,128)(2,1)} %get-tuple-element.283.own), channel_id=1, source_target_pairs={{0,4},{4,0},{8,12},{12,8},{1,5},{5,1},{9,13},{13,9},{2,6},{6,2},{1... | collective-permute-start | bytes 5898248 | tf_op jit(solution)/shard_map/ppermute | solution.py:40
  225.5 22.1 %collective-permute-start.30 = (f32[8,480]{1,0:T(8,128)S(1)}, f32[8,480]{1,0:T(8,128)S(1)}, u32[]{:S(2)}, u32[]{:S(2)}) collective-permute-start(f32[8,480]{1,0:T(8,128)S(1)} %get-tuple-element.345), channel_id=1, source_target_pairs={{0,4},{4,0},{8,12},{12,8},{1,5},{5,1},{9,13},{13,9},{2,6},{6,2},{1... | collective-permute-start | bytes 46088 | tf_op jit(solution)/shard_map/ppermute | solution.py:40
  234.9 14.4 %collective-permute-start.31 = (bf16[1536,256]{1,0:T(8,128)(2,1)S(1)}, bf16[1536,256]{1,0:T(8,128)(2,1)S(1)}, u32[]{:S(2)}, u32[]{:S(2)}) collective-permute-start(bf16[1536,256]{1,0:T(8,128)(2,1)S(1)} %get-tuple-element.215), channel_id=1, source_target_pairs={{0,8},{4,12},{8,0},{12,4},{1,9},{5,13},{9,1},{13,5},{2,10},{6,14},... | collective-permute-start | bytes 2359304 | tf_op jit(solution)/shard_map/ppermute | solution.py:44
  235.3 15.1 %collective-permute-start.32 = (bf16[1536,256]{1,0:T(8,128)(2,1)S(1)}, bf16[1536,256]{1,0:T(8,128)(2,1)S(1)}, u32[]{:S(2)}, u32[]{:S(2)}) collective-permute-start(bf16[1536,256]{1,0:T(8,128)(2,1)S(1)} %get-tuple-element.216), channel_id=1, source_target_pairs={{0,16},{16,0},{1,17},{17,1},{2,18},{18,2},{3,19},{19,3},{4,20},{20... | collective-permute-start | bytes 2359304 | tf_op jit(solution)/shard_map/ppermute | solution.py:48
  296.5 4.2 collective-permute-start.33
  316.6 132.2 %reduce-scatter.3.cloned.1.call-start = ((), (), s32[]{:S(2)}) async-start(), calls=%async_computation.4 | async-start | bytes 2457600 | tf_op jit(solution)/shard_map/reduce_scatter | solution.py:1281
  343.7 59.0 %collective-permute-start.34 = (bf16[4608,256]{1,0:T(8,128)(2,1)}, bf16[4608,256]{1,0:T(8,128)(2,1)}, u32[]{:S(2)}, u32[]{:S(2)}) collective-permute-start(bf16[4608,256]{1,0:T(8,128)(2,1)} %get-tuple-element.228), channel_id=1, source_target_pairs={{0,8},{4,12},{8,0},{12,4},{1,9},{5,13},{9,1},{13,5},{2,10},{6,14},... | collective-permute-start | bytes 7077896 | tf_op jit(solution)/shard_map/ppermute | solution.py:44
  344.4 58.2 %collective-permute-start.35 = (bf16[4608,256]{1,0:T(8,128)(2,1)}, bf16[4608,256]{1,0:T(8,128)(2,1)}, u32[]{:S(2)}, u32[]{:S(2)}) collective-permute-start(bf16[4608,256]{1,0:T(8,128)(2,1)} %get-tuple-element.229), channel_id=1, source_target_pairs={{0,16},{16,0},{1,17},{17,1},{2,18},{18,2},{3,19},{19,3},{4,20},{20... | collective-permute-start | bytes 7077896 | tf_op jit(solution)/shard_map/ppermute | solution.py:48
  354.6 43.8 %collective-permute-start.36 = (bf16[480,2048]{1,0:T(8,128)(2,1)}, bf16[480,2048]{1,0:T(8,128)(2,1)}, u32[]{:S(2)}, u32[]{:S(2)}) collective-permute-start(bf16[480,2048]{1,0:T(8,128)(2,1)} %shard_map.295), channel_id=1, source_target_pairs={{0,4},{4,0},{8,12},{12,8},{1,5},{5,1},{9,13},{13,9},{2,6},{6,2},{1... | collective-permute-start | bytes 5898248 | tf_op jit(solution)/shard_map/ppermute | solution.py:40
  356.1 6.0 collective-permute-start.38
  358.8 5.7 collective-permute-start.39
  366.6 10.6 %collective-permute-start.40 = (f32[8,480]{1,0:T(8,128)}, f32[8,480]{1,0:T(8,128)S(1)}, u32[]{:S(2)}, u32[]{:S(2)}) collective-permute-start(f32[8,480]{1,0:T(8,128)} %get-tuple-element.238), channel_id=1, source_target_pairs={{0,4},{4,0},{8,12},{12,8},{1,5},{5,1},{9,13},{13,9},{2,6},{6,2},{1... | collective-permute-start | bytes 46088 | tf_op jit(solution)/shard_map/ppermute | solution.py:40
  376.1 72.8 %collective-permute-start.41 = (bf16[4608,256]{1,0:T(8,128)(2,1)}, bf16[4608,256]{1,0:T(8,128)(2,1)S(1)}, u32[]{:S(2)}, u32[]{:S(2)}) collective-permute-start(bf16[4608,256]{1,0:T(8,128)(2,1)} %get-tuple-element.253), channel_id=1, source_target_pairs={{0,8},{4,12},{8,0},{12,4},{1,9},{5,13},{9,1},{13,5},{2,10},{6,14},... | collective-permute-start | bytes 7077896 | tf_op jit(solution)/shard_map/ppermute | solution.py:44
  377.2 71.7 %collective-permute-start.42 = (bf16[4608,256]{1,0:T(8,128)(2,1)}, bf16[4608,256]{1,0:T(8,128)(2,1)}, u32[]{:S(2)}, u32[]{:S(2)}) collective-permute-start(bf16[4608,256]{1,0:T(8,128)(2,1)} %get-tuple-element.254), channel_id=1, source_target_pairs={{0,16},{16,0},{1,17},{17,1},{2,18},{18,2},{3,19},{19,3},{4,20},{20... | collective-permute-start | bytes 7077896 | tf_op jit(solution)/shard_map/ppermute | solution.py:48
  402.7 147.0 %reduce-scatter.5.cloned.1.call-start = ((), (), s32[]{:S(2)}) async-start(), calls=%async_computation.6 | async-start | bytes 2457600 | tf_op jit(solution)/shard_map/reduce_scatter | solution.py:1305
  454.9 8.6 %collective-permute-start.44 = (bf16[480,256]{1,0:T(8,128)(2,1)}, bf16[480,256]{1,0:T(8,128)(2,1)S(1)}, u32[]{:S(2)}, u32[]{:S(2)}) collective-permute-start(bf16[480,256]{1,0:T(8,128)(2,1)} %get-tuple-element.262), channel_id=1, source_target_pairs={{0,8},{4,12},{8,0},{12,4},{1,9},{5,13},{9,1},{13,5},{2,10},{6,14},... | collective-permute-start | bytes 737288 | tf_op jit(solution)/shard_map/ppermute | solution.py:44
  474.2 133.1 %all-gather.3.cloned.1.call-start = ((), (), s32[]{:S(2)}) async-start(), calls=%async_computation.5 | async-start | bytes 2457600 | tf_op jit(solution)/shard_map/all_gather | solution.py:1292
  474.2 53.6 %collective-permute-start.45 = (bf16[4608,256]{1,0:T(8,128)(2,1)}, bf16[4608,256]{1,0:T(8,128)(2,1)S(1)}, u32[]{:S(2)}, u32[]{:S(2)}) collective-permute-start(bf16[4608,256]{1,0:T(8,128)(2,1)} %get-tuple-element.265), channel_id=1, source_target_pairs={{0,8},{4,12},{8,0},{12,4},{1,9},{5,13},{9,1},{13,5},{2,10},{6,14},... | collective-permute-start | bytes 7077896 | tf_op jit(solution)/shard_map/ppermute | solution.py:44
  475.7 52.9 %collective-permute-start.46 = (bf16[4608,256]{1,0:T(8,128)(2,1)}, bf16[4608,256]{1,0:T(8,128)(2,1)}, u32[]{:S(2)}, u32[]{:S(2)}) collective-permute-start(bf16[4608,256]{1,0:T(8,128)(2,1)} %get-tuple-element.271), channel_id=1, source_target_pairs={{0,16},{16,0},{1,17},{17,1},{2,18},{18,2},{3,19},{19,3},{4,20},{20... | collective-permute-start | bytes 7077896 | tf_op jit(solution)/shard_map/ppermute | solution.py:48
  477.2 142.8 %all-gather.5.cloned.1.call-start = ((), (), s32[]{:S(2)}) async-start(), calls=%async_computation.7 | async-start | bytes 2457600 | tf_op jit(solution)/shard_map/all_gather | solution.py:1353
  486.6 87.5 %collective-permute-start.60 = (bf16[1024,1024]{1,0:T(8,128)(2,1)}, bf16[1024,1024]{1,0:T(8,128)(2,1)}, u32[]{:S(2)}, u32[]{:S(2)}) collective-permute-start(bf16[1024,1024]{1,0:T(8,128)(2,1)} %get-tuple-element.312), channel_id=1, source_target_pairs={{0,4},{4,0},{8,12},{12,8},{1,5},{5,1},{9,13},{13,9},{2,6},{6,2},{1... | collective-permute-start | bytes 6291464 | tf_op jit(solution)/shard_map/ppermute | solution.py:40
  548.8 16.9 %collective-permute-start.53 = (bf16[1024,1280]{1,0:T(8,128)(2,1)}, bf16[1024,1280]{1,0:T(8,128)(2,1)}, u32[]{:S(2)}, u32[]{:S(2)}) collective-permute-start(bf16[1024,1280]{1,0:T(8,128)(2,1)} %get-tuple-element.277), channel_id=1, source_target_pairs={{0,4},{4,0},{8,12},{12,8},{1,5},{5,1},{9,13},{13,9},{2,6},{6,2},{1... | collective-permute-start | bytes 7864328 | tf_op jit(solution)/shard_map/ppermute | solution.py:40
  554.8 52.6 %collective-permute-start.67 = (bf16[4608,256]{1,0:T(8,128)(2,1)}, bf16[4608,256]{1,0:T(8,128)(2,1)S(1)}, u32[]{:S(2)}, u32[]{:S(2)}) collective-permute-start(bf16[4608,256]{1,0:T(8,128)(2,1)} %get-tuple-element.332), channel_id=1, source_target_pairs={{0,4},{4,0},{8,12},{12,8},{1,5},{5,1},{9,13},{13,9},{2,6},{6,2},{1... | collective-permute-start | bytes 7077896 | tf_op jit(solution)/shard_map/ppermute | solution.py:40
  563.8 9.2 %collective-permute-start.50 = (f32[24,256]{1,0:T(8,128)S(1)}, f32[24,256]{1,0:T(8,128)S(1)}, u32[]{:S(2)}, u32[]{:S(2)}) collective-permute-start(f32[24,256]{1,0:T(8,128)S(1)} %fusion.2), channel_id=1, source_target_pairs={{0,1},{1,0},{2,3},{3,2},{4,5},{5,4},{6,7},{7,6},{8,9},{9,8},{10,11... | collective-permute-start | bytes 73736 | tf_op jit(solution)/shard_map/ppermute | solution.py:58
  563.8 16.0 %collective-permute-start.51 = (f32[24,256]{1,0:T(8,128)S(1)}, f32[24,256]{1,0:T(8,128)S(1)}, u32[]{:S(2)}, u32[]{:S(2)}) collective-permute-start(f32[24,256]{1,0:T(8,128)S(1)} %fusion.2), channel_id=1, source_target_pairs={{0,2},{1,3},{2,0},{3,1},{4,6},{5,7},{6,4},{7,5},{8,10},{9,11},{10,... | collective-permute-start | bytes 73736 | tf_op jit(solution)/shard_map/ppermute | solution.py:58
  565.7 15.2 %collective-permute-start.52 = (f32[24,256]{1,0:T(8,128)S(1)}, f32[24,256]{1,0:T(8,128)S(1)}, u32[]{:S(2)}, u32[]{:S(2)}) collective-permute-start(f32[24,256]{1,0:T(8,128)S(1)} %fusion.2), channel_id=1, source_target_pairs={{0,3},{1,2},{2,1},{3,0},{4,7},{5,6},{6,5},{7,4},{8,11},{9,10},{10,... | collective-permute-start | bytes 73736 | tf_op jit(solution)/shard_map/ppermute | solution.py:58
  573.1 17.7 %collective-permute-start.56 = (bf16[128,1280]{1,0:T(8,128)(2,1)}, bf16[128,1280]{1,0:T(8,128)(2,1)S(1)}, u32[]{:S(2)}, u32[]{:S(2)}) collective-permute-start(bf16[128,1280]{1,0:T(8,128)(2,1)} %get-tuple-element.296), channel_id=1, source_target_pairs={{0,8},{4,12},{8,0},{12,4},{1,9},{5,13},{9,1},{13,5},{2,10},{6,14},... | collective-permute-start | bytes 983048 | tf_op jit(solution)/shard_map/ppermute | solution.py:44
  574.1 17.7 %collective-permute-start.57 = (bf16[128,1280]{1,0:T(8,128)(2,1)}, bf16[128,1280]{1,0:T(8,128)(2,1)S(1)}, u32[]{:S(2)}, u32[]{:S(2)}) collective-permute-start(bf16[128,1280]{1,0:T(8,128)(2,1)} %get-tuple-element.297), channel_id=1, source_target_pairs={{0,16},{16,0},{1,17},{17,1},{2,18},{18,2},{3,19},{19,3},{4,20},{20... | collective-permute-start | bytes 983048 | tf_op jit(solution)/shard_map/ppermute | solution.py:48
  579.9 6.6 %collective-permute-start.63 = (bf16[1024,128]{1,0:T(8,128)(2,1)}, bf16[1024,128]{1,0:T(8,128)(2,1)S(1)}, u32[]{:S(2)}, u32[]{:S(2)}) collective-permute-start(bf16[1024,128]{1,0:T(8,128)(2,1)} %get-tuple-element.322), channel_id=1, source_target_pairs={{0,8},{4,12},{8,0},{12,4},{1,9},{5,13},{9,1},{13,5},{2,10},{6,14},... | collective-permute-start | bytes 786440 | tf_op jit(solution)/shard_map/ppermute | solution.py:44
  580.9 6.6 %collective-permute-start.64 = (bf16[1024,128]{1,0:T(8,128)(2,1)}, bf16[1024,128]{1,0:T(8,128)(2,1)S(1)}, u32[]{:S(2)}, u32[]{:S(2)}) collective-permute-start(bf16[1024,128]{1,0:T(8,128)(2,1)} %get-tuple-element.323), channel_id=1, source_target_pairs={{0,16},{16,0},{1,17},{17,1},{2,18},{18,2},{3,19},{19,3},{4,20},{20... | collective-permute-start | bytes 786440 | tf_op jit(solution)/shard_map/ppermute | solution.py:48
  586.5 8.9 %collective-permute-start.61 = (bf16[1024,128]{1,0:T(8,128)(2,1)}, bf16[1024,128]{1,0:T(8,128)(2,1)S(1)}, u32[]{:S(2)}, u32[]{:S(2)}) collective-permute-start(bf16[1024,128]{1,0:T(8,128)(2,1)} %get-tuple-element.316), channel_id=1, source_target_pairs={{0,8},{4,12},{8,0},{12,4},{1,9},{5,13},{9,1},{13,5},{2,10},{6,14},... | collective-permute-start | bytes 786440 | tf_op jit(solution)/shard_map/ppermute | solution.py:44
  587.5 9.0 %collective-permute-start.62 = (bf16[1024,128]{1,0:T(8,128)(2,1)}, bf16[1024,128]{1,0:T(8,128)(2,1)S(1)}, u32[]{:S(2)}, u32[]{:S(2)}) collective-permute-start(bf16[1024,128]{1,0:T(8,128)(2,1)} %get-tuple-element.317), channel_id=1, source_target_pairs={{0,16},{16,0},{1,17},{17,1},{2,18},{18,2},{3,19},{19,3},{4,20},{20... | collective-permute-start | bytes 786440 | tf_op jit(solution)/shard_map/ppermute | solution.py:48
  590.8 9.8 %collective-permute-start.65 = (bf16[1024,128]{1,0:T(8,128)(2,1)}, bf16[1024,128]{1,0:T(8,128)(2,1)S(1)}, u32[]{:S(2)}, u32[]{:S(2)}) collective-permute-start(bf16[1024,128]{1,0:T(8,128)(2,1)} %get-tuple-element.327), channel_id=1, source_target_pairs={{0,8},{4,12},{8,0},{12,4},{1,9},{5,13},{9,1},{13,5},{2,10},{6,14},... | collective-permute-start | bytes 786440 | tf_op jit(solution)/shard_map/ppermute | solution.py:44
  591.8 10.3 %collective-permute-start.66 = (bf16[1024,128]{1,0:T(8,128)(2,1)}, bf16[1024,128]{1,0:T(8,128)(2,1)S(1)}, u32[]{:S(2)}, u32[]{:S(2)}) collective-permute-start(bf16[1024,128]{1,0:T(8,128)(2,1)} %get-tuple-element.328), channel_id=1, source_target_pairs={{0,16},{16,0},{1,17},{17,1},{2,18},{18,2},{3,19},{19,3},{4,20},{20... | collective-permute-start | bytes 786440 | tf_op jit(solution)/shard_map/ppermute | solution.py:48
  595.5 20.9 %collective-permute-start.54 = (bf16[128,1280]{1,0:T(8,128)(2,1)}, bf16[128,1280]{1,0:T(8,128)(2,1)S(1)}, u32[]{:S(2)}, u32[]{:S(2)}) collective-permute-start(bf16[128,1280]{1,0:T(8,128)(2,1)} %get-tuple-element.290), channel_id=1, source_target_pairs={{0,8},{4,12},{8,0},{12,4},{1,9},{5,13},{9,1},{13,5},{2,10},{6,14},... | collective-permute-start | bytes 983048 | tf_op jit(solution)/shard_map/ppermute | solution.py:44
  596.5 19.9 %collective-permute-start.55 = (bf16[128,1280]{1,0:T(8,128)(2,1)}, bf16[128,1280]{1,0:T(8,128)(2,1)S(1)}, u32[]{:S(2)}, u32[]{:S(2)}) collective-permute-start(bf16[128,1280]{1,0:T(8,128)(2,1)} %get-tuple-element.291), channel_id=1, source_target_pairs={{0,16},{16,0},{1,17},{17,1},{2,18},{18,2},{3,19},{19,3},{4,20},{20... | collective-permute-start | bytes 983048 | tf_op jit(solution)/shard_map/ppermute | solution.py:48
  600.6 15.8 %collective-permute-start.58 = (bf16[128,1280]{1,0:T(8,128)(2,1)}, bf16[128,1280]{1,0:T(8,128)(2,1)S(1)}, u32[]{:S(2)}, u32[]{:S(2)}) collective-permute-start(bf16[128,1280]{1,0:T(8,128)(2,1)} %get-tuple-element.301), channel_id=1, source_target_pairs={{0,8},{4,12},{8,0},{12,4},{1,9},{5,13},{9,1},{13,5},{2,10},{6,14},... | collective-permute-start | bytes 983048 | tf_op jit(solution)/shard_map/ppermute | solution.py:44
  602.1 14.4 %collective-permute-start.59 = (bf16[128,1280]{1,0:T(8,128)(2,1)}, bf16[128,1280]{1,0:T(8,128)(2,1)}, u32[]{:S(2)}, u32[]{:S(2)}) collective-permute-start(bf16[128,1280]{1,0:T(8,128)(2,1)} %get-tuple-element.302), channel_id=1, source_target_pairs={{0,16},{16,0},{1,17},{17,1},{2,18},{18,2},{3,19},{19,3},{4,20},{20... | collective-permute-start | bytes 983048 | tf_op jit(solution)/shard_map/ppermute | solution.py:48
  (64 other events, 457.4 us)
Sparse Core Ops, SparseCore 0:
  121.2 82.3 all-reduce.4
  316.8 81.5 all-reduce.6
  402.8 40.4 reduce-scatter.2
  474.3 40.2 reduce-scatter.4
  516.0 42.7 all-gather.2
  560.3 42.6 all-gather.4

commit v4 on v3

--- a/solution.py
+++ b/solution.py
@@ -341,7 +341,7 @@
 
 
 def key_tiles(count):
-    tile = next(t for t in (384, 320, 256, 128) if count % t == 0)
+    tile = next(t for t in (640, 384, 256, 128) if count % t == 0)
     return [(s, tile) for s in range(0, count, tile)]
 
 
@@ -409,11 +409,11 @@
         raw = dot(keys[span], query[...], (1, 1))
         prob = jnp.exp2(raw * factor + bias[span]) * norm
         grad_prob = dot(values[span], grad[...], (1, 1))
-        grad_raw = rounded(prob * (grad_prob - mean) * scale)
+        grad_raw = rounded(prob * (grad_prob - mean))
         total += dot(keys_t[:, span], grad_raw, (1, 0))
         grad_kv[span, :HEAD] += dot(grad_raw, query[...], (1, 0))
         grad_kv[span, HEAD:] += dot(rounded(prob), grad[...], (1, 0))
-    turned = total.T
+    turned = total.T * scale
     turned = turned * cos[...] - pltpu.roll(turned, HEAD // 2, 1) * sin[...]
     value = raw_query[...]
     shrink = kernel_inverse_rms(value)
@@ -425,6 +425,7 @@
 
     @pl.when(pl.program_id(0) == pl.num_programs(0) - 1)
     def _():
+        grad_kv[:, :HEAD] = grad_kv[:, :HEAD] * scale
         kv_own[...] = grad_kv[:rows]
         kv_sent[:rows] = rounded(grad_kv[rows : 2 * rows])
         kv_mid[...] = grad_kv[2 * rows : 3 * rows]

time: 641 us -> 639 us (level)
  transfers between devices with their start and end apart: 74 -> 74, of which waited for: 27 -> 30; matrix products, arithmetic and copies ran while one was open for 4% -> 4% of each run, Pallas kernels for 37% -> 37%
where the time goes in v4:
time: 639 us; the launch traced here: 628 us
  Pallas kernels  304 us (48%)
  waiting for transfers between devices  213 us (33%)
  starting transfers between devices  56.5 us (9%)
  local copies, waits for them, and re-layouts  30.2 us (5%)
  between operations  15.3 us (2%)
  other arithmetic  7.38 us (1%)
    ppermute x20, waiting for transfers between devices, to_x(): return lax.ppermute(v, 'ctx', [(i, i ^ 2) for i in range(4)])  176 us
    pallas_call x4, Pallas kernels, spread_call(): kernel_call(functools.partial(spread_kernel, tiles, len(which), got is no...  47.5 us
    pallas_call x6, Pallas kernels, prefetch_call(): pl.pallas_call(body, grid_spec=pltpu.PrefetchScalarGridSpec(num_scalar_pr...  32.4 us
    pallas_call x1, Pallas kernels, attend_back_call(): kernel_call(attend_back_kernel, (heads,), [column, pl.BlockSpec((count, H...  28.1 us
    pallas_call x1, Pallas kernels, weight_grad_call(): kernel_call(weight_grad_kernel, (3, 4), [pl.BlockSpec((1, tile, both), la...  27 us
    ppermute x20, starting transfers between devices, to_x(): return lax.ppermute(v, 'ctx', [(i, i ^ 2) for i in range(4)])  24.1 us
    pallas_call x2, Pallas kernels, products_call(): kernel_call(products_kernel, (4,), [single(own.shape), single(own.shape)]...  23.9 us
    pallas_call x1, Pallas kernels, experts_call(): kernel_call(functools.partial(experts_kernel, hid), (experts // per,), [s...  20 us
  transfers between devices with their start and end apart: 74, of which 30 were waited for; matrix products, arithmetic and copies ran while one was open for 4% of the time, Pallas kernels for 37%

profile of v4, /device:TPU:0, one launch (start us, length us, event | category | flops | bytes accessed | tf_op | source)
XLA Modules:
  0.0 628.2 jit_solution(14505237742573021571)
XLA Ops:
  11.7 3.0 collective-permute-start
  16.9 14.0 %collective-permute-done.refs_1_.refs_11_ = bf16[256,1408]{1,0:T(8,128)(2,1)S(1)} collective-permute-done((bf16[256,1408]{1,0:T(8,128)(2,1)S(1)}, bf16[256,1408]{1,0:T(8,128)(2,1)S(1)}, u32[]{:S(2)}, u32[]{:S(2)}) %collective-permute-start) | collective-permute-done | bytes 720928 | tf_op jit(solution)/shard_map/ppermute | solution.py:44
  32.3 4.3 shard_map.284
  37.1 1.7 collective-permute-start.3
  38.8 8.8 %collective-permute-done.2.refs_4_.refs_14_ = bf16[128,1408]{1,0:T(8,128)(2,1)S(1)} collective-permute-done((bf16[128,1408]{1,0:T(8,128)(2,1)S(1)}, bf16[128,1408]{1,0:T(8,128)(2,1)S(1)}, u32[]{:S(2)}, u32[]{:S(2)}) %collective-permute-start.2) | collective-permute-done | bytes 360480 | tf_op jit(solution)/shard_map/ppermute | solution.py:44
  47.7 1.7 collective-permute-start.12
  51.4 10.0 %collective-permute-done.12.refs_1_ = bf16[1024,256]{1,0:T(8,128)(2,1)S(1)} collective-permute-done((bf16[1024,256]{1,0:T(8,128)(2,1)}, bf16[1024,256]{1,0:T(8,128)(2,1)S(1)}, u32[]{:S(2)}, u32[]{:S(2)}) %collective-permute-start.12) | collective-permute-done | bytes 524320 | tf_op jit(solution)/shard_map/ppermute | solution.py:44
  68.0 12.1 %shard_map.281 = (f32[1,2048]{1,0:T(1,128)}, f32[1,2048]{1,0:T(1,128)}, bf16[16,2048]{1,0:T(8,128)(2,1)}, f32[1,128]{1,0:T(1,128)}, f32[1,128]{1,0:T(1,128)}, /*...) custom-call(s32[3]{0:T(128)} %pad_add_fusion.2.scal, ...), custom_call_target="tpu_custom_call" | custom-call | flops 11699999744 | tf_op jit(solution)/shard_map/pallas_call | solution.py:325
  82.4 5.7 shard_map.285.refs_0_.refs_2_.refs_7_.refs_3_.refs_8_.refs_1_
  97.1 14.1 %shard_map.282 = (bf16[480,1024]{1,0:T(8,128)(2,1)}, f32[8,1,480]{2,1,0:T(1,128)}) custom-call(bf16[480,1280]{1,0:T(8,128)(2,1)} %get-tuple-element.183.query, bf16[1920,256]{1,0:T(8,128)(2,1)} %pad_maximum_fusion.keys.values, bf16[1920,256]{1,0:T(8,128)(2,1)} %pad_maximum_fusion.keys.values, s32[1920,2]{1,0:T(8,128)} %copy.68.key_side, ...), custom_call_target="tpu_custom_call" | custom-call | flops 16300000256 | tf_op jit(solution)/shard_map/pallas_call | solution.py:371
  112.3 6.6 %shard_map.283 = bf16[480,2048]{1,0:T(8,128)(2,1)} custom-call(s32[3]{0:T(128)} %pad_add_fusion.2.scal, bf16[480,1024]{1,0:T(8,128)(2,1)} %get-tuple-element.309.mixed.left, bf16[1024,256]{1,0:T(8,128)(2,1)} %refs_0_.7, bf16[1024,256]{1,0:T(8,128)(2,1)} %copy-done.20, bf16[1024,256]{1,0:T(8,128)(2,1)} %copy-done.21, ...), custom_call_target="tpu_custom_call" | custom-call | flops 6600000000 | tf_op jit(solution)/shard_map/pallas_call | solution.py:487
  119.5 72.3 %collective-permute-done.22.refs_1_.refs_3_.refs_8_.refs_4_.refs_9_.refs_2_ = bf16[4608,512]{1,0:T(8,128)(2,1)} collective-permute-done((bf16[4608,512]{1,0:T(8,128)(2,1)}, bf16[4608,512]{1,0:T(8,128)(2,1)}, u32[]{:S(2)}, u32[]{:S(2)}) %collective-permute-start.22) | collective-permute-done | bytes 4718624 | tf_op jit(solution)/shard_map/ppermute | solution.py:44
  193.0 2.6 fusion.6
  195.7 2.6 fusion.7
  199.4 4.6 shard_map.288.own.cot
  204.9 10.9 %collective-permute-done.24.refs_4_.refs_5_ = bf16[1536,256]{1,0:T(8,128)(2,1)} collective-permute-done((bf16[1536,256]{1,0:T(8,128)(2,1)S(1)}, bf16[1536,256]{1,0:T(8,128)(2,1)}, u32[]{:S(2)}, u32[]{:S(2)}) %collective-permute-start.24) | collective-permute-done | bytes 786464 | tf_op jit(solution)/shard_map/ppermute | solution.py:44
  218.1 6.4 %shard_map.286 = (f32[480,2048]{1,0:T(8,128)}, bf16[480,2048]{1,0:T(8,128)(2,1)}, f32[480,16]{1,0:T(8,128)}) custom-call(bf16[480,2048]{1,0:T(8,128)(2,1)} %get-tuple-element.184.hid, bf16[480,2048]{1,0:T(8,128)(2,1)} %all-reduce.5.cloned.1.call-done.attn_add, f32[1,2048]{1,0:T(1,128)} %get-tuple-element.204.gain, ...), custom_call_target="tpu_custom_call" | custom-call | flops 6300000256 | tf_op jit(solution)/shard_map/pallas_call | solution.py:1003
  226.1 7.3 %collective-permute-done.27.refs_4_.refs_6_.refs_7_ = bf16[1536,256]{1,0:T(8,128)(2,1)S(1)} collective-permute-done((bf16[1536,256]{1,0:T(8,128)(2,1)}, bf16[1536,256]{1,0:T(8,128)(2,1)S(1)}, u32[]{:S(2)}, u32[]{:S(2)}) %collective-permute-start.27) | collective-permute-done | bytes 786464 | tf_op jit(solution)/shard_map/ppermute | solution.py:44
  233.3 1.6 collective-permute-done.28.refs_3_.refs_5_.refs_6_
  235.7 11.8 %shard_map.289 = (f32[1536,960]{1,0:T(8,128)}, bf16[960,2048]{1,0:T(8,128)(2,1)}) custom-call(bf16[480,2048]{1,0:T(8,128)(2,1)} %shard_map.288.own.cot, bf16[480,2048]{1,0:T(8,128)(2,1)} %collective-permute-done.29.other, bf16[4608,512]{1,0:T(8,128)(2,1)} %shard_map.285.refs_0_.refs_2_.refs_7_.refs_3_.refs_8_.refs_1_, ...), custom_call_target="tpu_custom_call" | custom-call | flops 11800000512 | tf_op jit(solution)/shard_map/pallas_call | solution.py:621
  250.5 12.0 %shard_map.287 = (f32[1536,960]{1,0:T(8,128)}, bf16[960,2048]{1,0:T(8,128)(2,1)}) custom-call(bf16[480,2048]{1,0:T(8,128)(2,1)} %get-tuple-element.283.own, bf16[480,2048]{1,0:T(8,128)(2,1)} %collective-permute-done.26.other, bf16[4608,512]{1,0:T(8,128)(2,1)} %shard_map.285.refs_0_.refs_2_.refs_7_.refs_3_.refs_8_.refs_1_, ...), custom_call_target="tpu_custom_call" | custom-call | flops 11800000512 | tf_op jit(solution)/shard_map/pallas_call | solution.py:621
  262.5 20.0 %shard_map.290 = (bf16[3,1536,960]{2,1,0:T(8,128)(2,1)}, bf16[3,960,1536]{2,1,0:T(8,128)(2,1)}, f32[8,1,960]{2,1,0:T(1,128)}) custom-call(bf16[960,2048]{1,0:T(8,128)(2,1)} %get-tuple-element.211.both.second, f32[1536,960]{1,0:T(8,128)} %get-tuple-element.212.gate_ref, f32[1536,960]{1,0:T(8,128)} %get-tuple-element.213.grad_act, ...), custom_call_target="tpu_custom_call" | custom-call | flops 20000000000 | tf_op jit(solution)/shard_map/pallas_call | solution.py:662
  282.5 14.1 %shard_map.291 = bf16[480,2048]{1,0:T(8,128)(2,1)} custom-call(bf16[3,960,1536]{2,1,0:T(8,128)(2,1)} %get-tuple-element.234.refs_0_.refs_1_, bf16[3,960,1536]{2,1,0:T(8,128)(2,1)} %get-tuple-element.234.refs_0_.refs_1_, bf16[4608,512]{1,0:T(8,128)(2,1)} %shard_map.285.refs_0_.refs_2_.refs_7_.refs_3_.refs_8_.refs_1_, ...), custom_call_target="tpu_custom_call" | custom-call | flops 10000000000 | tf_op jit(solution)/shard_map/pallas_call | solution.py:741
  296.6 4.2 collective-permute-done.33.refs_2_
  302.1 14.6 %shard_map.292 = bf16[480,2048]{1,0:T(8,128)(2,1)} custom-call(bf16[3,960,1536]{2,1,0:T(8,128)(2,1)} %get-tuple-element.234.refs_0_.refs_1_, bf16[3,960,1536]{2,1,0:T(8,128)(2,1)} %get-tuple-element.234.refs_0_.refs_1_, bf16[480,2048]{1,0:T(8,128)(2,1)} %copy-done.9, bf16[4608,512]{1,0:T(8,128)(2,1)} %shard_map.285.refs_0_.refs_2_.refs_7_.refs_3_.refs_8_.refs_1_, ...), custom_call_target="tpu_custom_call" | custom-call | flops 10000000000 | tf_op jit(solution)/shard_map/pallas_call | solution.py:741
  316.7 27.0 %shard_map.293 = (bf16[4608,512]{1,0:T(8,128)(2,1)}, bf16[4608,256]{1,0:T(8,128)(2,1)}, bf16[4608,256]{1,0:T(8,128)(2,1)}, bf16[4608,256]{1,0:T(8,128)(2,1)}, bf...) custom-call(bf16[3,1536,960]{2,1,0:T(8,128)(2,1)} %get-tuple-element.222.left, ...), custom_call_target="tpu_custom_call" | custom-call | flops 49999998976 | tf_op jit(solution)/shard_map/pallas_call | solution.py:783
  345.1 9.4 %shard_map.295 = bf16[480,2048]{1,0:T(8,128)(2,1)} custom-call(bf16[3,960,1536]{2,1,0:T(8,128)(2,1)} %get-tuple-element.234.refs_0_.refs_1_, bf16[4608,512]{1,0:T(8,128)(2,1)} %shard_map.285.refs_0_.refs_2_.refs_7_.refs_3_.refs_8_.refs_1_, bf16[4608,512]{1,0:T(8,128)(2,1)} %collective-permute-done.22.refs_1_.refs_3_.refs_8_.refs_4_.refs_9_.refs_2_, ...), custom_call_target="tpu_custom_call" | custom-call | flops 10000000000 | tf_op jit(solution)/shard_map/pallas_call | solution.py:741
  354.6 1.6 collective-permute-start.37
  356.2 2.6 collective-permute-start.38
  358.7 3.3 collective-permute-start.39
  362.1 2.4 collective-permute-done.39.fourth
  366.6 9.5 %shard_map.294.own = bf16[480,2048]{1,0:T(8,128)(2,1)} custom-call(bf16[3,960,1536]{2,1,0:T(8,128)(2,1)} %get-tuple-element.234.refs_0_.refs_1_, bf16[4608,512]{1,0:T(8,128)(2,1)} %shard_map.285.refs_0_.refs_2_.refs_7_.refs_3_.refs_8_.refs_1_, bf16[4608,512]{1,0:T(8,128)(2,1)} %collective-permute-done.22.refs_1_.refs_3_.refs_8_.refs_4_.refs_9_.refs_2_, ...), custom_call_target="tpu_custom_call" | custom-call | flops 10000000000 | tf_op jit(solution)/shard_map/pallas_call | solution.py:741
  377.2 1.5 collective-permute-start.42
  378.7 1.6 shard_map.298.gate_grads
  380.3 18.0 %all-reduce.7.cloned.1.call-done.grad_moe = bf16[480,2048]{1,0:T(8,128)(2,1)} async-done(((bf16[480,2048]{1,0:T(8,128)(2,1)}), bf16[480,2048]{1,0:T(8,128)(2,1)}) %all-reduce.7.cloned.1.call-update) | async-done | bytes 1966096 | tf_op jit(solution)/shard_map/psum | solution.py:1265
  398.3 4.3 shard_map.296
  402.7 9.3 %shard_map.299 = (f32[480,2048]{1,0:T(8,128)}, bf16[480,2048]{1,0:T(8,128)(2,1)}, bf16[480,16]{1,0:T(8,128)(2,1)}, f32[1,2048]{1,0:T(1,128)}) custom-call(bf16[480,2048]{1,0:T(8,128)(2,1)} %all-reduce.7.cloned.1.call-done.grad_moe, f32[480,16]{1,0:T(8,128)} %shard_map.298.gate_grads, f32[480,16]{1,0:T(8,128)} %get-tuple-element.214.gates, ...), custom_call_target="tpu_custom_call" | custom-call | flops 8600000512 | tf_op jit(solution)/shard_map/pallas_call | solution.py:1048
  412.0 6.5 %shard_map.300.grad = bf16[480,1024]{1,0:T(8,128)(2,1)} custom-call(s32[3]{0:T(128)} %pad_add_fusion.2.scal, bf16[480,2048]{1,0:T(8,128)(2,1)} %get-tuple-element.310.grad.right_own.right_sent, bf16[1024,256]{1,0:T(8,128)(2,1)} %refs_0_.7, bf16[1024,256]{1,0:T(8,128)(2,1)} %copy-done.20, bf16[1024,256]{1,0:T(8,128)(2,1)} %copy-done.21, ...), custom_call_target="tpu_custom_call" | custom-call | flops 6499999744 | tf_op jit(solution)/shard_map/pallas_call | solution.py:509
  418.5 28.1 %shard_map.301 = (bf16[480,1024]{1,0:T(8,128)(2,1)}, f32[480,256]{1,0:T(8,128)}, bf16[960,256]{1,0:T(8,128)(2,1)}, f32[480,256]{1,0:T(8,128)}, f32[1,128]{1,0:T(1,128)}) custom-call(bf16[480,1280]{1,0:T(8,128)(2,1)} %get-tuple-element.183.query, bf16[1920,256]{1,0:T(8,128)(2,1)} %pad_maximum_fusion.keys.values, ...), custom_call_target="tpu_custom_call" | custom-call | flops 30000001024 | tf_op jit(solution)/shard_map/pallas_call | solution.py:438
  448.3 2.9 shard_map.302
  452.0 2.2 shard_map.303
  455.6 7.1 %shard_map.304 = (bf16[4608,256]{1,0:T(8,128)(2,1)}, bf16[4608,256]{1,0:T(8,128)(2,1)}) custom-call(bf16[4608,256]{1,0:T(8,128)(2,1)} %get-tuple-element.263.a, bf16[4608,256]{1,0:T(8,128)(2,1)} %collective-permute-done.35.b, bf16[4608,256]{1,0:T(8,128)(2,1)} %get-tuple-element.264.c, bf16[4608,256]{1,0:T(8,128)(2,1)} %collective-permute-done.34.d), custom_call_target="tpu_custom_call" | custom-call | flops 500000000 | tf_op jit(solution)/shard_map/pallas_call | solution.py:802
  463.4 10.0 %shard_map.305 = (bf16[480,2048]{1,0:T(8,128)(2,1)}, f32[1,2048]{1,0:T(1,128)}, bf16[480,256]{1,0:T(8,128)(2,1)}, f32[1,128]{1,0:T(1,128)}) custom-call(s32[3]{0:T(128)} %pad_add_fusion.2.scal, bf16[480,1024]{1,0:T(8,128)(2,1)} %get-tuple-element.246.query_back.first, f32[480,256]{1,0:T(8,128)} %get-tuple-element.266.kv_part, bf16[480,256]{1,0:T(8,128)(2,1)} %copy-done.46, ...), custom_call_target="tpu_custom_call" | custom-call | flops 9799999488 | tf_op jit(solution)/shard_map/pallas_call | solution.py:571
  476.4 8.0 %shard_map.312 = (f32[1024,1024]{1,0:T(8,128)}, bf16[1024,1024]{1,0:T(8,128)(2,1)}) custom-call(s32[3]{0:T(128)} %pad_add_fusion.2.scal, bf16[480,1024]{1,0:T(8,128)(2,1)} %get-tuple-element.309.mixed.left, bf16[480,2048]{1,0:T(8,128)(2,1)} %get-tuple-element.310.grad.right_own.right_sent, bf16[480,2048]{1,0:T(8,128)(2,1)} %get-tuple-element.310.grad.right_own.right_sent), custom_call_target="tpu_custom_call" | custom-call | flops 500000000 | tf_op jit(solution)/shard_map/pallas_call | solution.py:905
  485.4 2.0 convolution_multiply_fusion
  487.4 38.2 %collective-permute-done.45.x_second = bf16[4608,256]{1,0:T(8,128)(2,1)S(1)} collective-permute-done((bf16[4608,256]{1,0:T(8,128)(2,1)}, bf16[4608,256]{1,0:T(8,128)(2,1)S(1)}, u32[]{:S(2)}, u32[]{:S(2)}) %collective-permute-start.45) | collective-permute-done | bytes 2359328 | tf_op jit(solution)/shard_map/ppermute | solution.py:44
  527.0 12.0 %shard_map.306 = (f32[4608,256]{1,0:T(8,128)}, bf16[4608,256]{1,0:T(8,128)(2,1)}) custom-call(s32[3]{0:T(128)} %pad_add_fusion.2.scal, bf16[4608,512]{1,0:T(8,128)(2,1)} %get-tuple-element.224.own, bf16[4608,256]{1,0:T(8,128)(2,1)} %copy-done.5, bf16[4608,256]{1,0:T(8,128)(2,1)} %collective-permute-done.46.y_first, bf16[4608,256]{1,0:T(8,128)(2,1)} %copy-done.6, ...), custom_call_target="tpu_custom_call" | custom-call | flops 500000000 | tf_op jit(solution)/shard_map/pallas_call | solution.py:826
  539.0 7.6 %shard_map.307 = (f32[1024,1280]{1,0:T(8,128)}, bf16[1024,1280]{1,0:T(8,128)(2,1)}) custom-call(s32[3]{0:T(128)} %pad_add_fusion.2.scal, bf16[480,2048]{1,0:T(8,128)(2,1)} %get-tuple-element.275.left_own.left_sent, bf16[480,2048]{1,0:T(8,128)(2,1)} %get-tuple-element.275.left_own.left_sent, bf16[480,1024]{1,0:T(8,128)(2,1)} %get-tuple-element.246.query_back.first, ...), custom_call_target="tpu_custom_call" | custom-call | flops 500000000 | tf_op jit(solution)/shard_map/pallas_call | solution.py:182
  547.5 4.2 shard_map.308
  554.3 3.4 collective-permute-done.48
  559.3 2.3 collective-permute-done.49
  563.1 2.5 collective-permute-start.51
  566.0 5.1 shard_map.309
  573.4 4.3 shard_map.313
  579.5 4.8 collective-permute-done.63.d
  584.3 1.6 collective-permute-start.61
  586.7 2.0 shard_map.314
  591.1 2.2 shard_map.310
  593.3 1.8 collective-permute-start.54
  595.6 3.3 collective-permute-done.65.x_second
  598.9 1.8 collective-permute-start.58
  602.2 2.5 shard_map.315
  606.1 7.7 %shard_map.316 = (f32[3072,256]{1,0:T(8,128)}, f32[3072,256]{1,0:T(8,128)}, f32[3072,256]{1,0:T(8,128)}) custom-call(s32[3]{0:T(128)} %pad_add_fusion.2.scal, f32[4608,256]{1,0:T(8,128)} %get-tuple-element.274.refs_0_.refs_1_.refs_2_, f32[4608,256]{1,0:T(8,128)} %get-tuple-element.274.refs_0_.refs_1_.refs_2_, ...), custom_call_target="tpu_custom_call" | custom-call | flops 500000000 | tf_op jit(solution)/shard_map/pallas_call | solution.py:182
  614.7 2.7 shard_map.311
  (313 shorter events, 78.5 us)
Async XLA Ops:
  7.2 210.9 %all-reduce.5.cloned.1.call-start = ((), (), s32[]{:S(2)}) async-start(), calls=%async_computation.2 | async-start | bytes 3932160 | tf_op jit(solution)/shard_map/psum | solution.py:1246
  11.7 19.1 %collective-permute-start = (bf16[256,1408]{1,0:T(8,128)(2,1)S(1)}, bf16[256,1408]{1,0:T(8,128)(2,1)S(1)}, u32[]{:S(2)}, u32[]{:S(2)}) collective-permute-start(bf16[256,1408]{1,0:T(8,128)(2,1)S(1)} %concatenate.36.refs_0_.refs_10_), channel_id=1, source_target_pairs={{0,8},{4,12},{8,0},{12,4},{1,9},{5,13},{9,1},{13,5},{2,10},{6,14},... | collective-permute-start | bytes 2162696 | tf_op jit(solution)/shard_map/ppermute | solution.py:44
  14.7 17.6 %collective-permute-start.1 = (bf16[256,1408]{1,0:T(8,128)(2,1)S(1)}, bf16[256,1408]{1,0:T(8,128)(2,1)S(1)}, u32[]{:S(2)}, u32[]{:S(2)}) collective-permute-start(bf16[256,1408]{1,0:T(8,128)(2,1)S(1)} %concatenate.36.refs_0_.refs_10_), channel_id=1, source_target_pairs={{0,16},{16,0},{1,17},{17,1},{2,18},{18,2},{3,19},{19,3},{4,20},{20... | collective-permute-start | bytes 2162696 | tf_op jit(solution)/shard_map/ppermute | solution.py:48
  16.2 34.6 %collective-permute-start.4 = (bf16[256,1408]{1,0:T(8,128)(2,1)S(1)}, bf16[256,1408]{1,0:T(8,128)(2,1)}, u32[]{:S(2)}, u32[]{:S(2)}) collective-permute-start(bf16[256,1408]{1,0:T(8,128)(2,1)S(1)} %concatenate.36.refs_0_.refs_10_), channel_id=1, source_target_pairs={{0,4},{4,0},{8,12},{12,8},{1,5},{5,1},{9,13},{13,9},{2,6},{6,2},{1... | collective-permute-start | bytes 2162696 | tf_op jit(solution)/shard_map/ppermute | solution.py:40
  36.6 45.8 %collective-permute-start.21 = (bf16[3,8,192,256]{3,2,1,0:T(8,128)(2,1)}, bf16[3,8,192,256]{3,2,1,0:T(8,128)(2,1)}, u32[]{:S(2)}, u32[]{:S(2)}) collective-permute-start(bf16[3,8,192,256]{3,2,1,0:T(8,128)(2,1)} %shard_map.284), channel_id=1, source_target_pairs={{0,4},{4,0},{8,12},{12,8},{1,5},{5,1},{9,13},{13,9},{2,6},{6,2},{1... | collective-permute-start | bytes 7077896 | tf_op jit(solution)/shard_map/ppermute | solution.py:40
  36.7 10.9 %collective-permute-start.2 = (bf16[128,1408]{1,0:T(8,128)(2,1)S(1)}, bf16[128,1408]{1,0:T(8,128)(2,1)S(1)}, u32[]{:S(2)}, u32[]{:S(2)}) collective-permute-start(bf16[128,1408]{1,0:T(8,128)(2,1)S(1)} %split.12), channel_id=1, source_target_pairs={{0,8},{4,12},{8,0},{12,4},{1,9},{5,13},{9,1},{13,5},{2,10},{6,14},... | collective-permute-start | bytes 1081352 | tf_op jit(solution)/shard_map/ppermute | solution.py:44
  37.1 10.5 %collective-permute-start.3 = (bf16[128,1408]{1,0:T(8,128)(2,1)S(1)}, bf16[128,1408]{1,0:T(8,128)(2,1)S(1)}, u32[]{:S(2)}, u32[]{:S(2)}) collective-permute-start(bf16[128,1408]{1,0:T(8,128)(2,1)S(1)} %split.13), channel_id=1, source_target_pairs={{0,16},{16,0},{1,17},{17,1},{2,18},{18,2},{3,19},{19,3},{4,20},{20... | collective-permute-start | bytes 1081352 | tf_op jit(solution)/shard_map/ppermute | solution.py:48
  47.7 13.8 %collective-permute-start.12 = (bf16[1024,256]{1,0:T(8,128)(2,1)}, bf16[1024,256]{1,0:T(8,128)(2,1)S(1)}, u32[]{:S(2)}, u32[]{:S(2)}) collective-permute-start(bf16[1024,256]{1,0:T(8,128)(2,1)} %refs_0_.7), channel_id=1, source_target_pairs={{0,8},{4,12},{8,0},{12,4},{1,9},{5,13},{9,1},{13,5},{2,10},{6,14},... | collective-permute-start | bytes 1572872 | tf_op jit(solution)/shard_map/ppermute | solution.py:44
  49.3 13.2 %collective-permute-start.13 = (bf16[1024,256]{1,0:T(8,128)(2,1)}, bf16[1024,256]{1,0:T(8,128)(2,1)S(1)}, u32[]{:S(2)}, u32[]{:S(2)}) collective-permute-start(bf16[1024,256]{1,0:T(8,128)(2,1)} %refs_0_.7), channel_id=1, source_target_pairs={{0,16},{16,0},{1,17},{17,1},{2,18},{18,2},{3,19},{19,3},{4,20},{20... | collective-permute-start | bytes 1572872 | tf_op jit(solution)/shard_map/ppermute | solution.py:48
  50.9 16.0 %collective-permute-start.5 = (bf16[256,1408]{1,0:T(8,128)(2,1)S(1)}, bf16[256,1408]{1,0:T(8,128)(2,1)S(1)}, u32[]{:S(2)}, u32[]{:S(2)}) collective-permute-start(bf16[256,1408]{1,0:T(8,128)(2,1)S(1)} %collective-permute-done.refs_1_.refs_11_), channel_id=1, source_target_pairs={{0,4},{4,0},{8,12},{12,8},{1,5},{5,1},{9,13},{13,9},{2,6},{6,2},{1... | collective-permute-start | bytes 2162696 | tf_op jit(solution)/shard_map/ppermute | solution.py:40
  50.9 16.0 %collective-permute-start.6 = (bf16[256,1408]{1,0:T(8,128)(2,1)S(1)}, bf16[256,1408]{1,0:T(8,128)(2,1)S(1)}, u32[]{:S(2)}, u32[]{:S(2)}) collective-permute-start(bf16[256,1408]{1,0:T(8,128)(2,1)S(1)} %collective-permute-done.1.refs_2_.refs_12_), channel_id=1, source_target_pairs={{0,4},{4,0},{8,12},{12,8},{1,5},{5,1},{9,13},{13,9},{2,6},{6,2},{1... | collective-permute-start | bytes 2162696 | tf_op jit(solution)/shard_map/ppermute | solution.py:40
  64.5 17.9 %collective-permute-start.14 = (bf16[1024,128]{1,0:T(8,128)(2,1)S(1)}, bf16[1024,128]{1,0:T(8,128)(2,1)S(1)}, u32[]{:S(2)}, u32[]{:S(2)}) collective-permute-start(bf16[1024,128]{1,0:T(8,128)(2,1)S(1)} %split.14), channel_id=1, source_target_pairs={{0,8},{4,12},{8,0},{12,4},{1,9},{5,13},{9,1},{13,5},{2,10},{6,14},... | collective-permute-start | bytes 786440 | tf_op jit(solution)/shard_map/ppermute | solution.py:44
  65.4 17.0 %collective-permute-start.15 = (bf16[1024,128]{1,0:T(8,128)(2,1)S(1)}, bf16[1024,128]{1,0:T(8,128)(2,1)}, u32[]{:S(2)}, u32[]{:S(2)}) collective-permute-start(bf16[1024,128]{1,0:T(8,128)(2,1)S(1)} %split.15), channel_id=1, source_target_pairs={{0,16},{16,0},{1,17},{17,1},{2,18},{18,2},{3,19},{19,3},{4,20},{20... | collective-permute-start | bytes 786440 | tf_op jit(solution)/shard_map/ppermute | solution.py:48
  81.1 7.7 %collective-permute-start.10 = (bf16[480,256]{1,0:T(8,128)(2,1)S(1)}, bf16[480,256]{1,0:T(8,128)(2,1)S(1)}, u32[]{:S(2)}, u32[]{:S(2)}) collective-permute-start(bf16[480,256]{1,0:T(8,128)(2,1)S(1)} %slice.64), channel_id=1, source_target_pairs={{0,8},{4,12},{8,0},{12,4},{1,9},{5,13},{9,1},{13,5},{2,10},{6,14},... | collective-permute-start | bytes 737288 | tf_op jit(solution)/shard_map/ppermute | solution.py:44
  88.8 103.0 %collective-permute-start.22 = (bf16[4608,512]{1,0:T(8,128)(2,1)}, bf16[4608,512]{1,0:T(8,128)(2,1)}, u32[]{:S(2)}, u32[]{:S(2)}) collective-permute-start(bf16[4608,512]{1,0:T(8,128)(2,1)} %shard_map.285.refs_0_.refs_2_.refs_7_.refs_3_.refs_8_.refs_1_), channel_id=1, source_target_pairs={{0,8},{4,12},{8,0},{12,4},{1,9},{5,13},{9,1},{13,5},{2,10},{6,14},... | collective-permute-start | bytes 14155784 | tf_op jit(solution)/shard_map/ppermute | solution.py:44
  90.2 102.8 %collective-permute-start.23 = (bf16[4608,512]{1,0:T(8,128)(2,1)}, bf16[4608,512]{1,0:T(8,128)(2,1)}, u32[]{:S(2)}, u32[]{:S(2)}) collective-permute-start(bf16[4608,512]{1,0:T(8,128)(2,1)} %shard_map.285.refs_0_.refs_2_.refs_7_.refs_3_.refs_8_.refs_1_), channel_id=1, source_target_pairs={{0,16},{16,0},{1,17},{17,1},{2,18},{18,2},{3,19},{19,3},{4,20},{20... | collective-permute-start | bytes 14155784 | tf_op jit(solution)/shard_map/ppermute | solution.py:48
  90.7 5.8 collective-permute-start.16
  95.4 15.9 %collective-permute-start.17 = (bf16[1024,256]{1,0:T(8,128)(2,1)S(1)}, bf16[1024,256]{1,0:T(8,128)(2,1)S(1)}, u32[]{:S(2)}, u32[]{:S(2)}) collective-permute-start(bf16[1024,256]{1,0:T(8,128)(2,1)S(1)} %collective-permute-done.12.refs_1_), channel_id=1, source_target_pairs={{0,4},{4,0},{8,12},{12,8},{1,5},{5,1},{9,13},{13,9},{2,6},{6,2},{1... | collective-permute-start | bytes 1572872 | tf_op jit(solution)/shard_map/ppermute | solution.py:40
  96.5 14.8 %collective-permute-start.18 = (bf16[1024,256]{1,0:T(8,128)(2,1)S(1)}, bf16[1024,256]{1,0:T(8,128)(2,1)S(1)}, u32[]{:S(2)}, u32[]{:S(2)}) collective-permute-start(bf16[1024,256]{1,0:T(8,128)(2,1)S(1)} %collective-permute-done.13.refs_2_), channel_id=1, source_target_pairs={{0,4},{4,0},{8,12},{12,8},{1,5},{5,1},{9,13},{13,9},{2,6},{6,2},{1... | collective-permute-start | bytes 1572872 | tf_op jit(solution)/shard_map/ppermute | solution.py:40
  97.0 14.3 %collective-permute-start.20 = (bf16[1024,128]{1,0:T(8,128)(2,1)S(1)}, bf16[1024,128]{1,0:T(8,128)(2,1)S(1)}, u32[]{:S(2)}, u32[]{:S(2)}) collective-permute-start(bf16[1024,128]{1,0:T(8,128)(2,1)S(1)} %collective-permute-done.14.refs_4_), channel_id=1, source_target_pairs={{0,4},{4,0},{8,12},{12,8},{1,5},{5,1},{9,13},{13,9},{2,6},{6,2},{1... | collective-permute-start | bytes 786440 | tf_op jit(solution)/shard_map/ppermute | solution.py:40
  119.0 279.3 %all-reduce.7.cloned.1.call-start = ((), (), s32[]{:S(2)}) async-start(), calls=%async_computation.3 | async-start | bytes 3932160 | tf_op jit(solution)/shard_map/psum | solution.py:1265
  198.3 17.5 %collective-permute-start.24 = (bf16[1536,256]{1,0:T(8,128)(2,1)S(1)}, bf16[1536,256]{1,0:T(8,128)(2,1)}, u32[]{:S(2)}, u32[]{:S(2)}) collective-permute-start(bf16[1536,256]{1,0:T(8,128)(2,1)S(1)} %get-tuple-element.199), channel_id=1, source_target_pairs={{0,8},{4,12},{8,0},{12,4},{1,9},{5,13},{9,1},{13,5},{2,10},{6,14},... | collective-permute-start | bytes 2359304 | tf_op jit(solution)/shard_map/ppermute | solution.py:44
  198.9 17.2 %collective-permute-start.25 = (bf16[1536,256]{1,0:T(8,128)(2,1)S(1)}, bf16[1536,256]{1,0:T(8,128)(2,1)}, u32[]{:S(2)}, u32[]{:S(2)}) collective-permute-start(bf16[1536,256]{1,0:T(8,128)(2,1)S(1)} %get-tuple-element.200), channel_id=1, source_target_pairs={{0,16},{16,0},{1,17},{17,1},{2,18},{18,2},{3,19},{19,3},{4,20},{20... | collective-permute-start | bytes 2359304 | tf_op jit(solution)/shard_map/ppermute | solution.py:48
  204.0 31.7 %collective-permute-start.29 = (bf16[480,2048]{1,0:T(8,128)(2,1)}, bf16[480,2048]{1,0:T(8,128)(2,1)}, u32[]{:S(2)}, u32[]{:S(2)}) collective-permute-start(bf16[480,2048]{1,0:T(8,128)(2,1)} %shard_map.288.own.cot), channel_id=1, source_target_pairs={{0,4},{4,0},{8,12},{12,8},{1,5},{5,1},{9,13},{13,9},{2,6},{6,2},{1... | collective-permute-start | bytes 5898248 | tf_op jit(solution)/shard_map/ppermute | solution.py:40
  216.0 17.3 %collective-permute-start.27 = (bf16[1536,256]{1,0:T(8,128)(2,1)}, bf16[1536,256]{1,0:T(8,128)(2,1)S(1)}, u32[]{:S(2)}, u32[]{:S(2)}) collective-permute-start(bf16[1536,256]{1,0:T(8,128)(2,1)} %get-tuple-element.207), channel_id=1, source_target_pairs={{0,8},{4,12},{8,0},{12,4},{1,9},{5,13},{9,1},{13,5},{2,10},{6,14},... | collective-permute-start | bytes 2359304 | tf_op jit(solution)/shard_map/ppermute | solution.py:44
  217.6 17.4 %collective-permute-start.28 = (bf16[1536,256]{1,0:T(8,128)(2,1)}, bf16[1536,256]{1,0:T(8,128)(2,1)S(1)}, u32[]{:S(2)}, u32[]{:S(2)}) collective-permute-start(bf16[1536,256]{1,0:T(8,128)(2,1)} %get-tuple-element.208), channel_id=1, source_target_pairs={{0,16},{16,0},{1,17},{17,1},{2,18},{18,2},{3,19},{19,3},{4,20},{20... | collective-permute-start | bytes 2359304 | tf_op jit(solution)/shard_map/ppermute | solution.py:48
  224.4 26.0 %collective-permute-start.26 = (bf16[480,2048]{1,0:T(8,128)(2,1)}, bf16[480,2048]{1,0:T(8,128)(2,1)}, u32[]{:S(2)}, u32[]{:S(2)}) collective-permute-start(bf16[480,2048]{1,0:T(8,128)(2,1)} %get-tuple-element.283.own), channel_id=1, source_target_pairs={{0,4},{4,0},{8,12},{12,8},{1,5},{5,1},{9,13},{13,9},{2,6},{6,2},{1... | collective-permute-start | bytes 5898248 | tf_op jit(solution)/shard_map/ppermute | solution.py:40
  225.5 22.1 %collective-permute-start.30 = (f32[8,480]{1,0:T(8,128)S(1)}, f32[8,480]{1,0:T(8,128)S(1)}, u32[]{:S(2)}, u32[]{:S(2)}) collective-permute-start(f32[8,480]{1,0:T(8,128)S(1)} %get-tuple-element.345), channel_id=1, source_target_pairs={{0,4},{4,0},{8,12},{12,8},{1,5},{5,1},{9,13},{13,9},{2,6},{6,2},{1... | collective-permute-start | bytes 46088 | tf_op jit(solution)/shard_map/ppermute | solution.py:40
  234.9 14.4 %collective-permute-start.31 = (bf16[1536,256]{1,0:T(8,128)(2,1)S(1)}, bf16[1536,256]{1,0:T(8,128)(2,1)S(1)}, u32[]{:S(2)}, u32[]{:S(2)}) collective-permute-start(bf16[1536,256]{1,0:T(8,128)(2,1)S(1)} %get-tuple-element.215), channel_id=1, source_target_pairs={{0,8},{4,12},{8,0},{12,4},{1,9},{5,13},{9,1},{13,5},{2,10},{6,14},... | collective-permute-start | bytes 2359304 | tf_op jit(solution)/shard_map/ppermute | solution.py:44
  235.3 15.2 %collective-permute-start.32 = (bf16[1536,256]{1,0:T(8,128)(2,1)S(1)}, bf16[1536,256]{1,0:T(8,128)(2,1)S(1)}, u32[]{:S(2)}, u32[]{:S(2)}) collective-permute-start(bf16[1536,256]{1,0:T(8,128)(2,1)S(1)} %get-tuple-element.216), channel_id=1, source_target_pairs={{0,16},{16,0},{1,17},{17,1},{2,18},{18,2},{3,19},{19,3},{4,20},{20... | collective-permute-start | bytes 2359304 | tf_op jit(solution)/shard_map/ppermute | solution.py:48
  316.7 131.6 %reduce-scatter.3.cloned.1.call-start = ((), (), s32[]{:S(2)}) async-start(), calls=%async_computation.4 | async-start | bytes 2457600 | tf_op jit(solution)/shard_map/reduce_scatter | solution.py:1282
  343.7 58.9 %collective-permute-start.34 = (bf16[4608,256]{1,0:T(8,128)(2,1)}, bf16[4608,256]{1,0:T(8,128)(2,1)}, u32[]{:S(2)}, u32[]{:S(2)}) collective-permute-start(bf16[4608,256]{1,0:T(8,128)(2,1)} %get-tuple-element.228), channel_id=1, source_target_pairs={{0,8},{4,12},{8,0},{12,4},{1,9},{5,13},{9,1},{13,5},{2,10},{6,14},... | collective-permute-start | bytes 7077896 | tf_op jit(solution)/shard_map/ppermute | solution.py:44
  344.4 58.2 %collective-permute-start.35 = (bf16[4608,256]{1,0:T(8,128)(2,1)}, bf16[4608,256]{1,0:T(8,128)(2,1)}, u32[]{:S(2)}, u32[]{:S(2)}) collective-permute-start(bf16[4608,256]{1,0:T(8,128)(2,1)} %get-tuple-element.229), channel_id=1, source_target_pairs={{0,16},{16,0},{1,17},{17,1},{2,18},{18,2},{3,19},{19,3},{4,20},{20... | collective-permute-start | bytes 7077896 | tf_op jit(solution)/shard_map/ppermute | solution.py:48
  354.6 43.7 %collective-permute-start.36 = (bf16[480,2048]{1,0:T(8,128)(2,1)}, bf16[480,2048]{1,0:T(8,128)(2,1)}, u32[]{:S(2)}, u32[]{:S(2)}) collective-permute-start(bf16[480,2048]{1,0:T(8,128)(2,1)} %shard_map.295), channel_id=1, source_target_pairs={{0,4},{4,0},{8,12},{12,8},{1,5},{5,1},{9,13},{13,9},{2,6},{6,2},{1... | collective-permute-start | bytes 5898248 | tf_op jit(solution)/shard_map/ppermute | solution.py:40
  356.2 5.9 collective-permute-start.38
  358.7 5.7 collective-permute-start.39
  366.6 10.6 %collective-permute-start.40 = (f32[8,480]{1,0:T(8,128)}, f32[8,480]{1,0:T(8,128)S(1)}, u32[]{:S(2)}, u32[]{:S(2)}) collective-permute-start(f32[8,480]{1,0:T(8,128)} %get-tuple-element.238), channel_id=1, source_target_pairs={{0,4},{4,0},{8,12},{12,8},{1,5},{5,1},{9,13},{13,9},{2,6},{6,2},{1... | collective-permute-start | bytes 46088 | tf_op jit(solution)/shard_map/ppermute | solution.py:40
  376.0 71.8 %collective-permute-start.41 = (bf16[4608,256]{1,0:T(8,128)(2,1)}, bf16[4608,256]{1,0:T(8,128)(2,1)S(1)}, u32[]{:S(2)}, u32[]{:S(2)}) collective-permute-start(bf16[4608,256]{1,0:T(8,128)(2,1)} %get-tuple-element.253), channel_id=1, source_target_pairs={{0,8},{4,12},{8,0},{12,4},{1,9},{5,13},{9,1},{13,5},{2,10},{6,14},... | collective-permute-start | bytes 7077896 | tf_op jit(solution)/shard_map/ppermute | solution.py:44
  377.2 71.1 %collective-permute-start.42 = (bf16[4608,256]{1,0:T(8,128)(2,1)}, bf16[4608,256]{1,0:T(8,128)(2,1)}, u32[]{:S(2)}, u32[]{:S(2)}) collective-permute-start(bf16[4608,256]{1,0:T(8,128)(2,1)} %get-tuple-element.254), channel_id=1, source_target_pairs={{0,16},{16,0},{1,17},{17,1},{2,18},{18,2},{3,19},{19,3},{4,20},{20... | collective-permute-start | bytes 7077896 | tf_op jit(solution)/shard_map/ppermute | solution.py:48
  402.6 144.8 %reduce-scatter.5.cloned.1.call-start = ((), (), s32[]{:S(2)}) async-start(), calls=%async_computation.6 | async-start | bytes 2457600 | tf_op jit(solution)/shard_map/reduce_scatter | solution.py:1306
  446.6 4.6 collective-permute-start.43
  454.2 8.5 %collective-permute-start.44 = (bf16[480,256]{1,0:T(8,128)(2,1)}, bf16[480,256]{1,0:T(8,128)(2,1)S(1)}, u32[]{:S(2)}, u32[]{:S(2)}) collective-permute-start(bf16[480,256]{1,0:T(8,128)(2,1)} %get-tuple-element.262), channel_id=1, source_target_pairs={{0,8},{4,12},{8,0},{12,4},{1,9},{5,13},{9,1},{13,5},{2,10},{6,14},... | collective-permute-start | bytes 737288 | tf_op jit(solution)/shard_map/ppermute | solution.py:44
  473.4 131.3 %all-gather.3.cloned.1.call-start = ((), (), s32[]{:S(2)}) async-start(), calls=%async_computation.5 | async-start | bytes 2457600 | tf_op jit(solution)/shard_map/all_gather | solution.py:1293
  473.4 52.2 %collective-permute-start.45 = (bf16[4608,256]{1,0:T(8,128)(2,1)}, bf16[4608,256]{1,0:T(8,128)(2,1)S(1)}, u32[]{:S(2)}, u32[]{:S(2)}) collective-permute-start(bf16[4608,256]{1,0:T(8,128)(2,1)} %get-tuple-element.265), channel_id=1, source_target_pairs={{0,8},{4,12},{8,0},{12,4},{1,9},{5,13},{9,1},{13,5},{2,10},{6,14},... | collective-permute-start | bytes 7077896 | tf_op jit(solution)/shard_map/ppermute | solution.py:44
  474.2 52.0 %collective-permute-start.46 = (bf16[4608,256]{1,0:T(8,128)(2,1)}, bf16[4608,256]{1,0:T(8,128)(2,1)}, u32[]{:S(2)}, u32[]{:S(2)}) collective-permute-start(bf16[4608,256]{1,0:T(8,128)(2,1)} %get-tuple-element.271), channel_id=1, source_target_pairs={{0,16},{16,0},{1,17},{17,1},{2,18},{18,2},{3,19},{19,3},{4,20},{20... | collective-permute-start | bytes 7077896 | tf_op jit(solution)/shard_map/ppermute | solution.py:48
  475.0 142.4 %all-gather.5.cloned.1.call-start = ((), (), s32[]{:S(2)}) async-start(), calls=%async_computation.7 | async-start | bytes 2457600 | tf_op jit(solution)/shard_map/all_gather | solution.py:1354
  484.4 87.6 %collective-permute-start.60 = (bf16[1024,1024]{1,0:T(8,128)(2,1)}, bf16[1024,1024]{1,0:T(8,128)(2,1)}, u32[]{:S(2)}, u32[]{:S(2)}) collective-permute-start(bf16[1024,1024]{1,0:T(8,128)(2,1)} %get-tuple-element.312), channel_id=1, source_target_pairs={{0,4},{4,0},{8,12},{12,8},{1,5},{5,1},{9,13},{13,9},{2,6},{6,2},{1... | collective-permute-start | bytes 6291464 | tf_op jit(solution)/shard_map/ppermute | solution.py:40
  546.6 19.1 %collective-permute-start.53 = (bf16[1024,1280]{1,0:T(8,128)(2,1)}, bf16[1024,1280]{1,0:T(8,128)(2,1)}, u32[]{:S(2)}, u32[]{:S(2)}) collective-permute-start(bf16[1024,1280]{1,0:T(8,128)(2,1)} %get-tuple-element.277), channel_id=1, source_target_pairs={{0,4},{4,0},{8,12},{12,8},{1,5},{5,1},{9,13},{13,9},{2,6},{6,2},{1... | collective-permute-start | bytes 7864328 | tf_op jit(solution)/shard_map/ppermute | solution.py:40
  552.6 52.1 %collective-permute-start.67 = (bf16[4608,256]{1,0:T(8,128)(2,1)}, bf16[4608,256]{1,0:T(8,128)(2,1)S(1)}, u32[]{:S(2)}, u32[]{:S(2)}) collective-permute-start(bf16[4608,256]{1,0:T(8,128)(2,1)} %get-tuple-element.332), channel_id=1, source_target_pairs={{0,4},{4,0},{8,12},{12,8},{1,5},{5,1},{9,13},{13,9},{2,6},{6,2},{1... | collective-permute-start | bytes 7077896 | tf_op jit(solution)/shard_map/ppermute | solution.py:40
  561.6 9.5 %collective-permute-start.50 = (f32[24,256]{1,0:T(8,128)S(1)}, f32[24,256]{1,0:T(8,128)S(1)}, u32[]{:S(2)}, u32[]{:S(2)}) collective-permute-start(f32[24,256]{1,0:T(8,128)S(1)} %fusion.2), channel_id=1, source_target_pairs={{0,1},{1,0},{2,3},{3,2},{4,5},{5,4},{6,7},{7,6},{8,9},{9,8},{10,11... | collective-permute-start | bytes 73736 | tf_op jit(solution)/shard_map/ppermute | solution.py:58
  563.1 14.6 %collective-permute-start.51 = (f32[24,256]{1,0:T(8,128)S(1)}, f32[24,256]{1,0:T(8,128)S(1)}, u32[]{:S(2)}, u32[]{:S(2)}) collective-permute-start(f32[24,256]{1,0:T(8,128)S(1)} %fusion.2), channel_id=1, source_target_pairs={{0,2},{1,3},{2,0},{3,1},{4,6},{5,7},{6,4},{7,5},{8,10},{9,11},{10,... | collective-permute-start | bytes 73736 | tf_op jit(solution)/shard_map/ppermute | solution.py:58
  565.7 13.3 %collective-permute-start.52 = (f32[24,256]{1,0:T(8,128)S(1)}, f32[24,256]{1,0:T(8,128)S(1)}, u32[]{:S(2)}, u32[]{:S(2)}) collective-permute-start(f32[24,256]{1,0:T(8,128)S(1)} %fusion.2), channel_id=1, source_target_pairs={{0,3},{1,2},{2,1},{3,0},{4,7},{5,6},{6,5},{7,4},{8,11},{9,10},{10,... | collective-permute-start | bytes 73736 | tf_op jit(solution)/shard_map/ppermute | solution.py:58
  571.1 17.6 %collective-permute-start.56 = (bf16[128,1280]{1,0:T(8,128)(2,1)}, bf16[128,1280]{1,0:T(8,128)(2,1)S(1)}, u32[]{:S(2)}, u32[]{:S(2)}) collective-permute-start(bf16[128,1280]{1,0:T(8,128)(2,1)} %get-tuple-element.296), channel_id=1, source_target_pairs={{0,8},{4,12},{8,0},{12,4},{1,9},{5,13},{9,1},{13,5},{2,10},{6,14},... | collective-permute-start | bytes 983048 | tf_op jit(solution)/shard_map/ppermute | solution.py:44
  572.0 17.7 %collective-permute-start.57 = (bf16[128,1280]{1,0:T(8,128)(2,1)}, bf16[128,1280]{1,0:T(8,128)(2,1)S(1)}, u32[]{:S(2)}, u32[]{:S(2)}) collective-permute-start(bf16[128,1280]{1,0:T(8,128)(2,1)} %get-tuple-element.297), channel_id=1, source_target_pairs={{0,16},{16,0},{1,17},{17,1},{2,18},{18,2},{3,19},{19,3},{4,20},{20... | collective-permute-start | bytes 983048 | tf_op jit(solution)/shard_map/ppermute | solution.py:48
  577.7 6.6 %collective-permute-start.63 = (bf16[1024,128]{1,0:T(8,128)(2,1)}, bf16[1024,128]{1,0:T(8,128)(2,1)S(1)}, u32[]{:S(2)}, u32[]{:S(2)}) collective-permute-start(bf16[1024,128]{1,0:T(8,128)(2,1)} %get-tuple-element.322), channel_id=1, source_target_pairs={{0,8},{4,12},{8,0},{12,4},{1,9},{5,13},{9,1},{13,5},{2,10},{6,14},... | collective-permute-start | bytes 786440 | tf_op jit(solution)/shard_map/ppermute | solution.py:44
  579.0 6.9 %collective-permute-start.64 = (bf16[1024,128]{1,0:T(8,128)(2,1)}, bf16[1024,128]{1,0:T(8,128)(2,1)S(1)}, u32[]{:S(2)}, u32[]{:S(2)}) collective-permute-start(bf16[1024,128]{1,0:T(8,128)(2,1)} %get-tuple-element.323), channel_id=1, source_target_pairs={{0,16},{16,0},{1,17},{17,1},{2,18},{18,2},{3,19},{19,3},{4,20},{20... | collective-permute-start | bytes 786440 | tf_op jit(solution)/shard_map/ppermute | solution.py:48
  584.3 9.0 %collective-permute-start.61 = (bf16[1024,128]{1,0:T(8,128)(2,1)}, bf16[1024,128]{1,0:T(8,128)(2,1)S(1)}, u32[]{:S(2)}, u32[]{:S(2)}) collective-permute-start(bf16[1024,128]{1,0:T(8,128)(2,1)} %get-tuple-element.316), channel_id=1, source_target_pairs={{0,8},{4,12},{8,0},{12,4},{1,9},{5,13},{9,1},{13,5},{2,10},{6,14},... | collective-permute-start | bytes 786440 | tf_op jit(solution)/shard_map/ppermute | solution.py:44
  586.0 9.4 %collective-permute-start.62 = (bf16[1024,128]{1,0:T(8,128)(2,1)}, bf16[1024,128]{1,0:T(8,128)(2,1)S(1)}, u32[]{:S(2)}, u32[]{:S(2)}) collective-permute-start(bf16[1024,128]{1,0:T(8,128)(2,1)} %get-tuple-element.317), channel_id=1, source_target_pairs={{0,16},{16,0},{1,17},{17,1},{2,18},{18,2},{3,19},{19,3},{4,20},{20... | collective-permute-start | bytes 786440 | tf_op jit(solution)/shard_map/ppermute | solution.py:48
  588.7 10.2 %collective-permute-start.65 = (bf16[1024,128]{1,0:T(8,128)(2,1)}, bf16[1024,128]{1,0:T(8,128)(2,1)S(1)}, u32[]{:S(2)}, u32[]{:S(2)}) collective-permute-start(bf16[1024,128]{1,0:T(8,128)(2,1)} %get-tuple-element.327), channel_id=1, source_target_pairs={{0,8},{4,12},{8,0},{12,4},{1,9},{5,13},{9,1},{13,5},{2,10},{6,14},... | collective-permute-start | bytes 786440 | tf_op jit(solution)/shard_map/ppermute | solution.py:44
  589.7 11.2 %collective-permute-start.66 = (bf16[1024,128]{1,0:T(8,128)(2,1)}, bf16[1024,128]{1,0:T(8,128)(2,1)S(1)}, u32[]{:S(2)}, u32[]{:S(2)}) collective-permute-start(bf16[1024,128]{1,0:T(8,128)(2,1)} %get-tuple-element.328), channel_id=1, source_target_pairs={{0,16},{16,0},{1,17},{17,1},{2,18},{18,2},{3,19},{19,3},{4,20},{20... | collective-permute-start | bytes 786440 | tf_op jit(solution)/shard_map/ppermute | solution.py:48
  593.3 20.4 %collective-permute-start.54 = (bf16[128,1280]{1,0:T(8,128)(2,1)}, bf16[128,1280]{1,0:T(8,128)(2,1)S(1)}, u32[]{:S(2)}, u32[]{:S(2)}) collective-permute-start(bf16[128,1280]{1,0:T(8,128)(2,1)} %get-tuple-element.290), channel_id=1, source_target_pairs={{0,8},{4,12},{8,0},{12,4},{1,9},{5,13},{9,1},{13,5},{2,10},{6,14},... | collective-permute-start | bytes 983048 | tf_op jit(solution)/shard_map/ppermute | solution.py:44
  595.3 18.4 %collective-permute-start.55 = (bf16[128,1280]{1,0:T(8,128)(2,1)}, bf16[128,1280]{1,0:T(8,128)(2,1)S(1)}, u32[]{:S(2)}, u32[]{:S(2)}) collective-permute-start(bf16[128,1280]{1,0:T(8,128)(2,1)} %get-tuple-element.291), channel_id=1, source_target_pairs={{0,16},{16,0},{1,17},{17,1},{2,18},{18,2},{3,19},{19,3},{4,20},{20... | collective-permute-start | bytes 983048 | tf_op jit(solution)/shard_map/ppermute | solution.py:48
  598.9 14.9 %collective-permute-start.58 = (bf16[128,1280]{1,0:T(8,128)(2,1)}, bf16[128,1280]{1,0:T(8,128)(2,1)S(1)}, u32[]{:S(2)}, u32[]{:S(2)}) collective-permute-start(bf16[128,1280]{1,0:T(8,128)(2,1)} %get-tuple-element.301), channel_id=1, source_target_pairs={{0,8},{4,12},{8,0},{12,4},{1,9},{5,13},{9,1},{13,5},{2,10},{6,14},... | collective-permute-start | bytes 983048 | tf_op jit(solution)/shard_map/ppermute | solution.py:44
  601.0 12.9 %collective-permute-start.59 = (bf16[128,1280]{1,0:T(8,128)(2,1)}, bf16[128,1280]{1,0:T(8,128)(2,1)}, u32[]{:S(2)}, u32[]{:S(2)}) collective-permute-start(bf16[128,1280]{1,0:T(8,128)(2,1)} %get-tuple-element.302), channel_id=1, source_target_pairs={{0,16},{16,0},{1,17},{17,1},{2,18},{18,2},{3,19},{19,3},{4,20},{20... | collective-permute-start | bytes 983048 | tf_op jit(solution)/shard_map/ppermute | solution.py:48
  (64 other events, 446.3 us)
Sparse Core Ops, SparseCore 0:
  119.1 82.3 all-reduce.4
  316.8 81.4 all-reduce.6
  402.7 40.4 reduce-scatter.2
  473.5 40.9 reduce-scatter.4
  516.0 42.8 all-gather.2
  560.3 42.6 all-gather.4
